TPU v7x, 512 devices: a whole 4x4x16 slice. The times are simulated.
512 devices in a mesh: seq: 32 (over z_lo, y), tp: 16 (over z_hi, x, core).
Axes of the slice: x: 4, y: 4, z: 16 (z_hi: 2, z_lo: 8; z = z_hi * 8 + z_lo), core: 2. Of those that a mesh axis runs over, the one named last changes fastest.
Arguments:
- page_counts: int32 [32], replicated, may hold values from 1 to 4, 64 in all
- page_order: int32 [64], replicated, may hold values from 0 to 63, each once
- queries: bfloat16 [8192, 8192], P('seq', 'tp'), may hold values from -8 to 8
- keys: bfloat16 [8192, 1024], P('seq'), may hold values from -8 to 8
- values: bfloat16 [8192, 1024], P('seq'), may hold values from -6 to 6
- out_weight: bfloat16 [8192, 8192], P('tp', 'seq'), may hold values from -1 to 1
Outputs:
- mixed: bfloat16 [8192, 8192], P(('seq', 'tp'))
All inputs are finite; a program needn't handle non-finite values.
Results may differ from a plain program's by a relative error of at most 0.018.
Values may be sent and summed in bfloat16 or wider, within the bound.
No kernel may reach another device: no remote copies, remote signals or barrier semaphores. Data moves between devices by JAX's collectives and lax.ppermute only.
A program may use at most 64 MiB of HBM per device.

v0:
```python
import jax
import jax.numpy as jnp
from jax import lax
from jax.sharding import PartitionSpec as P

HQ = 64
KVH = 8
HD = 128
PAGE = 64


def slot_positions(page_counts, page_order, seq_count, slots):
    slot_ids = jnp.arange(seq_count * slots, dtype=jnp.int32)
    owner = slot_ids // slots
    local = slot_ids % slots
    before = jnp.cumsum(page_counts) - page_counts
    match_owner = owner[:, None] == jnp.arange(seq_count, dtype=jnp.int32)[None, :]
    held = jnp.sum(jnp.where(match_owner, page_counts[None, :], 0), axis=1)
    earlier = jnp.sum(jnp.where(match_owner, before[None, :], 0), axis=1)
    rank = earlier + local
    live = local < held
    match_rank = rank[:, None] == jnp.arange(page_order.shape[0], dtype=jnp.int32)[None, :]
    page = jnp.sum(jnp.where(match_rank, page_order[None, :], 0), axis=1)
    offsets = jnp.arange(PAGE, dtype=jnp.int32)
    pos = (page[:, None] * PAGE + offsets[None, :]).reshape(-1)
    return (pos, jnp.repeat(live, PAGE))


def body(page_counts, page_order, queries, keys, values, out_weight):
    seq_count = lax.axis_size("seq")
    seq_me = lax.axis_index("seq")
    tp_me = lax.axis_index("tp")
    row_count = queries.shape[0]
    slots = row_count // PAGE
    heads_here = queries.shape[1] // HD
    group = HQ // KVH
    kv_here = max(1, heads_here // group)
    per_kv = heads_here // kv_here
    kv_first = tp_me * heads_here // group
    scale = HD ** (-0.5)
    pos_all, live_all = slot_positions(page_counts, page_order, seq_count, slots)
    my_pos = lax.dynamic_slice_in_dim(pos_all, seq_me * row_count, row_count).reshape(slots, PAGE)
    my_live = lax.dynamic_slice_in_dim(live_all, seq_me * row_count, row_count).reshape(slots, PAGE)
    query_tiles = queries.reshape(slots, PAGE, kv_here, per_kv, HD)
    work_tiles, work_pos, work_live = (query_tiles, my_pos, my_live)
    key_local = lax.dynamic_slice_in_dim(keys, kv_first * HD, kv_here * HD, 1)
    value_local = lax.dynamic_slice_in_dim(values, kv_first * HD, kv_here * HD, 1)
    key_piece = lax.all_gather(key_local, "seq", axis=0, tiled=True)
    value_piece = lax.all_gather(value_local, "seq", axis=0, tiled=True)
    count = key_piece.shape[0]
    key_heads = key_piece.reshape(count, kv_here, HD)
    value_heads = value_piece.reshape(count, kv_here, HD)

    def one_tile(dummy, inputs):
        query_tile, tile_pos, tile_live, best, total, accum = inputs
        visible = live_all[None, :] & (pos_all[None, :] <= tile_pos[:, None]) & tile_live[:, None]

        def update(state):
            old_best, old_total, old_accum = state
            scores = (
                jnp.einsum(
                    "rkgd,nkd->rkgn", query_tile, key_heads, preferred_element_type=jnp.float32
                )
                * scale
            )
            seen = visible[:, None, None, :]
            scores = jnp.where(seen, scores, jnp.float32(-1e30))
            new_best = jnp.maximum(old_best, jnp.max(scores, axis=3))
            weights = jnp.where(seen, jnp.exp(scores - new_best[..., None]), jnp.float32(0.0))
            fade = jnp.exp(old_best - new_best)
            new_total = old_total * fade + jnp.sum(weights, axis=3)
            update_term = jnp.einsum(
                "rkgn,nkd->rkgd",
                weights.astype(jnp.bfloat16),
                value_heads,
                preferred_element_type=jnp.float32,
            )
            new_accum = old_accum * fade[..., None] + update_term
            return (new_best, new_total, new_accum)

        result = lax.cond(jnp.any(visible), update, lambda state: state, (best, total, accum))
        return (dummy, result)

    best_all = jnp.full((slots, PAGE, kv_here, per_kv), -1e30, jnp.float32)
    total_all = jnp.zeros((slots, PAGE, kv_here, per_kv), jnp.float32)
    accum_all = jnp.zeros((slots, PAGE, kv_here, per_kv, HD), jnp.float32)
    _, new_state = lax.scan(
        one_tile, jnp.int32(0), (work_tiles, work_pos, work_live, best_all, total_all, accum_all)
    )
    best, total, accum = new_state
    safe_total = jnp.where(work_live[..., None, None], total, jnp.float32(1.0))
    attention = accum / safe_total[..., None]
    attention = jnp.where(work_live[..., None, None, None], attention, jnp.float32(0.0))
    attention = attention.reshape(slots, PAGE, heads_here * HD).astype(jnp.bfloat16)
    attention = attention.reshape(row_count, heads_here * HD)
    terms = jnp.dot(
        attention,
        lax.all_gather(out_weight, "seq", axis=1, tiled=True),
        preferred_element_type=jnp.float32,
    )
    mixed = lax.psum_scatter(terms.astype(jnp.bfloat16), "tp", scatter_dimension=0, tiled=True)
    return mixed


def solution(mesh):
    return jax.shard_map(
        body,
        mesh=mesh,
        in_specs=(P(), P(), P("seq", "tp"), P("seq", None), P("seq", None), P("tp", "seq")),
        out_specs=P(("seq", "tp"), None),
        check_vma=False,
    )
```

profile of v0, /device:TPU:1, one launch (start us, length us, event | category | flops | bytes accessed | tf_op | source)
XLA Modules:
  0.0 839.6 jit_solution(4283316418315881933)
XLA Ops:
  6.5 1.0 copy-done
  7.6 0.6 constant_dynamic-slice_fusion.2
  8.3 1.5 constant_dynamic-slice_fusion.1
  9.8 0.7 all-gather.8.cloned.1.call-update
  10.6 0.7 copy.11
  11.4 0.1 reduce.6
  11.5 0.7 sub.42
  12.2 0.7 select_reduce_fusion.2
  13.0 0.1 reshape.162
  13.2 0.1 broadcast_in_dim.124
  13.3 0.7 select_reduce_fusion
  14.4 1.0 reshape.166
  15.5 202.3 %all-gather.4.cloned.1.call-done = bf16[8192,128]{1,0:T(8,128)(2,1)} async-done(((bf16[256,128]{1,0:T(8,128)(2,1)}), bf16[8192,128]{1,0:T(8,128)(2,1)}) %all-gather.4.cloned.1.call-update) | async-done | bytes 2097168 | tf_op jit(solution)/shard_map/all_gather | solution.py:48
  217.7 224.1 %all-gather.6.cloned.1.call-done = bf16[8192,128]{1,0:T(8,128)(2,1)} async-done(((bf16[256,128]{1,0:T(8,128)(2,1)}), bf16[8192,128]{1,0:T(8,128)(2,1)}) %all-gather.6.cloned.1.call-update) | async-done | bytes 2097168 | tf_op jit(solution)/shard_map/all_gather | solution.py:49
  441.8 17.4 %while.14 = (s32[]{:T(128)}, f32[4,64,1,4]{1,3,2,0:T(4,128)S(1)}, f32[4,64,1,4,128]{4,1,3,2,0:T(8,128)S(1)}, s32[4,64]{1,0:T(4,128)S(1)}, pred[4,64]{1,0:T(4,128...) while((s32[]{:T(128)}, f32[4,64,1,4]{1,3,2,0:T(4,128)S(1)}, ...), condition=%wide.region_10.11_spmd.clone.clone, body=%wide.region_4.10_spmd.clone.sunk.clone | while | flops 1094788096 | bytes 40881984 | solution.py:87
  442.1 0.1 and.82
  442.2 1.4 fusion.49
  444.3 7.3 conditional.4
  444.3 3.5 fusion.42
  447.8 1.8 fusion.26
  449.5 2.0 fusion.7
  451.9 0.1 and.82
  452.0 1.4 fusion.49
  454.5 0.1 and.82
  454.6 1.4 fusion.49
  457.0 0.1 and.82
  457.1 1.4 fusion.49
  459.3 0.2 select_convert_fusion
  459.5 0.2 copy.13
  459.7 202.5 %all-gather.8.cloned.1.call-done = bf16[512,8192]{1,0:T(8,128)(2,1)} async-done(((bf16[512,256]{1,0:T(8,128)(2,1)}), bf16[512,8192]{1,0:T(8,128)(2,1)}) %all-gather.8.cloned.1.call-update) | async-done | bytes 8388624 | tf_op jit(solution)/shard_map/all_gather | solution.py:98
  662.2 7.7 convolution_convert_fusion
  670.0 163.1 %reduce-scatter.2.cloned.1.call-done = bf16[16,8192]{1,0:T(8,128)(2,1)} async-done(((bf16[256,8192]{1,0:T(8,128)(2,1)}), bf16[16,8192]{1,0:T(8,128)(2,1)}) %reduce-scatter.2.cloned.1.call-update) | async-done | bytes 262160 | tf_op jit(solution)/shard_map/reduce_scatter | solution.py:101
  (74 shorter events, 2.1 us)
Async XLA Ops:
  6.5 1.0 copy-start
  6.5 211.2 %all-gather.4.cloned.1.call-start = ((), (), s32[]{:S(2)}) async-start(), calls=%async_computation.1 | async-start | bytes 2162688 | tf_op jit(solution)/shard_map/all_gather | solution.py:48
  8.2 433.6 %all-gather.6.cloned.1.call-start = ((), (), s32[]{:S(2)}) async-start(), calls=%async_computation.2 | async-start | bytes 2162688 | tf_op jit(solution)/shard_map/all_gather | solution.py:49
  9.8 652.4 %all-gather.8.cloned.1.call-start = ((), (), s32[]{:S(2)}) async-start(), calls=%async_computation.3 | async-start | bytes 8650752 | tf_op jit(solution)/shard_map/all_gather | solution.py:98
  10.5 822.6 %reduce-scatter.2.cloned.1.call-start = ((), (), s32[]{:S(2)}) async-start(), calls=%async_computation.4 | async-start | bytes 4456448 | tf_op jit(solution)/shard_map/reduce_scatter | solution.py:101
  444.3 3.5 copy-start.1
Sparse Core Ops, SparseCore 0:
  9.4 208.2 all-gather.3
  219.8 221.9 all-gather.5
  443.8 218.3 all-gather.7
  670.1 162.9 reduce-scatter.1
where the time goes:
time: 840 us
  waiting for transfers between devices  793 us (94%)
  between operations  13.2 us (2%)
  matrix products  12.9 us (2%)
  other arithmetic  10.6 us (1%)
    all_gather x1, waiting for transfers between devices, body(): value_piece = lax.all_gather(value_local, 'seq', axis=0, tiled=True)  224 us
    all_gather x1, waiting for transfers between devices, body(): lax.all_gather(out_weight, 'seq', axis=1, tiled=True)  202 us
    all_gather x1, waiting for transfers between devices, body(): key_piece = lax.all_gather(key_local, 'seq', axis=0, tiled=True)  202 us
    reduce_scatter x1, waiting for transfers between devices, body(): lax.psum_scatter(terms.astype(jnp.bfloat16), 'tp', scatter_dimension=0, t...  163 us
  transfers between devices with their start and end apart: 4, of which 4 were waited for; matrix products, arithmetic and copies ran while one was open for 3% of the time, Pallas kernels for 0%

commit v1 on v0

v1 whole, which is shorter than its diff:
```python
import jax
import jax.numpy as jnp
from jax import lax
from jax.experimental import pallas as pl
from jax.experimental.pallas import tpu as pltpu
from jax.sharding import Mesh, PartitionSpec as P

HD = 128
PAGE = 64
SLOTS = 4
PAGES = 64
HEADS = 4
ZL, Y, ZH, X, C = 8, 4, 2, 4, 2
N_SEQ = ZL * Y
ROWS = SLOTS * PAGE
CHUNK = 512
SCALE = HD**-0.5


def attention_kernel(counts, order, place, q_ref, own_ref, other_ref, o_ref, k_sc, v_sc):
    me = place[0]
    core = place[1]

    def sort_pages(k_ref, v_ref):
        def one(d, rank):
            held = counts[d]
            base = ((d % Y) * ZL + d // Y) * ROWS
            for j in range(SLOTS):

                @pl.when(j < held)
                def _():
                    to = pl.multiple_of(order[rank + j] * PAGE, PAGE)
                    at = pl.multiple_of(base + j * PAGE, PAGE)
                    k_sc[pl.ds(to, PAGE), :] = k_ref[pl.ds(at, PAGE), :]
                    v_sc[pl.ds(to, PAGE), :] = v_ref[pl.ds(at, PAGE), :]

            return rank + held

        lax.fori_loop(0, N_SEQ, one, jnp.int32(0))

    @pl.when(core == 0)
    def _():
        sort_pages(own_ref, other_ref)

    @pl.when(core == 1)
    def _():
        sort_pages(other_ref, own_ref)

    before = lax.fori_loop(0, me, lambda d, s: s + counts[d], jnp.int32(0))
    live = counts[me]

    def store(j, rows):
        for b in range(2):
            to = (2 * (j % 2) + b) * 64 + (j // 2) * 32
            for h in range(HEADS):
                o_ref[to : to + 32, h * HD : (h + 1) * HD] = rows(h, b)

    for j in range(SLOTS):

        @pl.when(j < live)
        def _():
            page = order[before + j]
            q = jnp.concatenate(
                [q_ref[j * PAGE : (j + 1) * PAGE, h * HD : (h + 1) * HD] for h in range(HEADS)], axis=0
            )

            def step(i, state, last):
                best, total, accum = state
                at = pl.multiple_of(i * CHUNK, CHUNK)
                k = k_sc[pl.ds(at, CHUNK), :]
                v = v_sc[pl.ds(at, CHUNK), :]
                s = lax.dot_general(q, k, (((1,), (1,)), ((), ())), preferred_element_type=jnp.float32)
                if last:
                    row = lax.broadcasted_iota(jnp.int32, s.shape, 0) % PAGE + page * PAGE
                    col = lax.broadcasted_iota(jnp.int32, s.shape, 1) + at
                    s = jnp.where(col <= row, s, jnp.float32(-1e30))
                new = jnp.maximum(best, jnp.max(s, axis=1, keepdims=True))
                p = jnp.exp((s - new) * SCALE)
                fade = jnp.exp((best - new) * SCALE)
                total = total * fade + jnp.sum(p, axis=1, keepdims=True)
                accum = accum * fade + jnp.dot(p.astype(jnp.bfloat16), v, preferred_element_type=jnp.float32)
                return new, total, accum

            state = (
                jnp.full((HEADS * PAGE, 1), -1e30, jnp.float32),
                jnp.zeros((HEADS * PAGE, 1), jnp.float32),
                jnp.zeros((HEADS * PAGE, HD), jnp.float32),
            )
            full = page // (CHUNK // PAGE)
            state = lax.fori_loop(0, full, lambda i, s: step(i, s, False), state)
            _, total, accum = step(full, state, True)
            out = (accum / total).astype(jnp.bfloat16)
            store(j, lambda h, b: out[h * PAGE + b * 32 : h * PAGE + b * 32 + 32, :])

        @pl.when(j >= live)
        def _():
            store(j, lambda h, b: jnp.zeros((32, HD), jnp.bfloat16))


def attend(counts, order, place, q, own, other):
    smem = pl.BlockSpec(memory_space=pltpu.SMEM)
    vmem = pl.BlockSpec(memory_space=pltpu.VMEM)
    return pl.pallas_call(
        attention_kernel,
        out_shape=jax.ShapeDtypeStruct(q.shape, jnp.bfloat16),
        in_specs=[smem, smem, smem, vmem, vmem, vmem],
        out_specs=vmem,
        scratch_shapes=[pltpu.VMEM((PAGES * PAGE, HD), jnp.bfloat16) for _ in range(2)],
        compiler_params=pltpu.CompilerParams(vmem_limit_bytes=40 << 20),
    )(counts, order, place, q, own, other)


def project_kernel(a_ref, b_ref, w_ref, o_ref):
    half = a_ref.shape[2]
    part = jnp.dot(a_ref[0], w_ref[:half, :], preferred_element_type=jnp.float32)
    part += jnp.dot(b_ref[0], w_ref[half:, :], preferred_element_type=jnp.float32)
    o_ref[...] = part.astype(jnp.bfloat16).reshape(o_ref.shape)


def project(a, b, w):
    n = w.shape[1]
    return pl.pallas_call(
        project_kernel,
        grid=(Y,),
        out_shape=jax.ShapeDtypeStruct((X, Y, ROWS // X, n), jnp.bfloat16),
        in_specs=[
            pl.BlockSpec((1, ROWS, a.shape[2]), lambda i: (i, 0, 0)),
            pl.BlockSpec((1, ROWS, a.shape[2]), lambda i: (i, 0, 0)),
            pl.BlockSpec(w.shape, lambda i: (0, 0)),
        ],
        out_specs=pl.BlockSpec((X, 1, ROWS // X, n), lambda i: (0, i, 0, 0)),
        compiler_params=pltpu.CompilerParams(vmem_limit_bytes=40 << 20),
    )(a, b, w)


def spread(piece, axis, count):
    return lax.all_to_all(jnp.broadcast_to(piece[None], (count, *piece.shape)), axis, 0, 0)


def swap(piece, axis):
    return lax.ppermute(piece, axis, [(0, 1), (1, 0)])


def body(counts, order, queries, keys, values, weight):
    zl, y, zh, x, c = (lax.axis_index(name) for name in ("zl", "y", "zh", "x", "c"))
    with jax.named_scope("weight_gather"):
        given = swap(lax.dynamic_slice_in_dim(weight, (1 - c) * 128, 128, 1), "c")
        kept = lax.dynamic_slice_in_dim(weight, c * 128, 128, 1)
        wide = lax.all_gather(jnp.concatenate([kept, given], axis=0), "zl", axis=1, tiled=True)
    with jax.named_scope("cache_gather"):
        head = (zh * X + x) * HD
        piece = jnp.where(
            c == 0,
            lax.dynamic_slice_in_dim(keys, head, HD, 1),
            lax.dynamic_slice_in_dim(values, head, HD, 1),
        )
        own = spread(piece, "zl", ZL).reshape(ZL * ROWS, HD)
        own = spread(own, "y", Y).reshape(N_SEQ * ROWS, HD)
        other = swap(own, "c")
    with jax.named_scope("attention"):
        place = jnp.stack([zl * Y + y, c]).astype(jnp.int32)
        heads = attend(counts, order, place, queries, own, other)
    with jax.named_scope("rows_gather"):
        mine = spread(heads, "y", Y)
        theirs = swap(mine, "c")
    with jax.named_scope("projection"):
        parts = project(mine, theirs, wide)
    with jax.named_scope("sum_x"):
        parts = lax.all_to_all(parts, "x", 0, 0)
        total = jnp.sum(parts.astype(jnp.float32), axis=0).reshape(Y, ZH, 32, ZL * 128)
    with jax.named_scope("sum_zh"):
        away = lax.dynamic_slice_in_dim(total, 1 - zh, 1, 1).astype(jnp.bfloat16)
        stay = lax.dynamic_slice_in_dim(total, zh, 1, 1)
        mixed = (stay + swap(away, "zh").astype(jnp.float32)).astype(jnp.bfloat16)
    with jax.named_scope("columns"):
        mixed = lax.all_to_all(mixed.reshape(Y * C, 16, ZL * 128), ("y", "c"), 0, 0)
        mixed = mixed.reshape(Y, C, 16, ZL, 128).transpose(2, 3, 0, 1, 4)
    return mixed.reshape(16, N_SEQ * 256)


def solution(mesh):
    fine = Mesh(mesh.devices.reshape(ZL, Y, ZH, X, C), ("zl", "y", "zh", "x", "c"))
    seq, tp = ("zl", "y"), ("zh", "x", "c")
    return jax.shard_map(
        body,
        mesh=fine,
        in_specs=(P(), P(), P(seq, tp), P(seq, None), P(seq, None), P(tp, seq)),
        out_specs=P((*seq, *tp), None),
        check_vma=False,
    )
```

time: 840 us -> 231 us (0.28)
  waiting for transfers between devices: 793 us -> 81.1 us
  blocking collectives: 0 us -> 81 us
  starting transfers between devices: 0.12 us -> 34.9 us
  matrix products: 12.9 us -> 0 us
  Pallas kernels: 0 us -> 10.2 us
  other arithmetic: 10.6 us -> 2.13 us
    all_gather x3 -> x1, waiting for transfers between devices: 629 us -> 37.5 us  [body(): lax.all_gather(jnp.concatenate([kept, given], axis=0), 'zl', axis=1, tile...]
    reduce_scatter x1 -> x0, waiting for transfers between devices: 163 us -> none  [body(): lax.psum_scatter(terms.astype(jnp.bfloat16), 'tp', scatter_dimension=0, t...]
    all_to_all x0 -> x3, blocking collectives: none -> 81 us  [the longest x2 53.6 us: spread(): lax.all_to_all(jnp.broadcast_to(piece[None], (count, *piece.shape)), axis...]
    all_to_all x0 -> x2, waiting for transfers between devices: none -> 36.8 us  [the longest x1 18.8 us: spread(): lax.all_to_all(jnp.broadcast_to(piece[None], (count, *piece.shape)), axis...]
    ppermute x0 -> x4, starting transfers between devices: none -> 26.9 us  [swap(): return lax.ppermute(piece, axis, [(0, 1), (1, 0)])]
    dot_general x3 -> x0, matrix products: 12.9 us -> none  [the longest x1 7.71 us: body(): jnp.dot(attention, lax.all_gather(out_weight, 'seq', axis=1, tiled=True),...]
    pallas_call x0 -> x2, Pallas kernels: none -> 10.2 us  [the longest x1 6.42 us: attend(): pl.pallas_call(attention_kernel, out_shape=jax.ShapeDtypeStruct(q.shape,...]
  transfers between devices with their start and end apart: 4 -> 7, of which waited for: 4 -> 5; matrix products, arithmetic and copies ran while one was open for 3% -> 0% of each run, Pallas kernels for 0% -> 3%
where the time goes in v1:
time: 231 us; the launch traced here: 228 us
  waiting for transfers between devices  81.1 us (35%)
  blocking collectives  81 us (35%)
  starting transfers between devices  34.9 us (15%)
  between operations  13.5 us (6%)
  Pallas kernels  10.2 us (4%)
  local copies, waits for them, and re-layouts  4.63 us (2%)
    all_to_all x2, blocking collectives, spread(): lax.all_to_all(jnp.broadcast_to(piece[None], (count, *piece.shape)), axis...  53.6 us
    all_gather x1, waiting for transfers between devices, body(): lax.all_gather(jnp.concatenate([kept, given], axis=0), 'zl', axis=1, tile...  37.5 us
    all_to_all x1, blocking collectives, body(): mixed = lax.all_to_all(mixed.reshape(Y * C, 16, ZL * 128), ('y', 'c'), 0, 0)  27.4 us
    ppermute x4, starting transfers between devices, swap(): return lax.ppermute(piece, axis, [(0, 1), (1, 0)])  26.9 us
    all_to_all x1, waiting for transfers between devices, spread(): lax.all_to_all(jnp.broadcast_to(piece[None], (count, *piece.shape)), axis...  18.8 us
    all_to_all x1, waiting for transfers between devices, body(): parts = lax.all_to_all(parts, 'x', 0, 0)  18 us
    ppermute x4, waiting for transfers between devices, swap(): return lax.ppermute(piece, axis, [(0, 1), (1, 0)])  6.79 us
    pallas_call x1, Pallas kernels, attend(): pl.pallas_call(attention_kernel, out_shape=jax.ShapeDtypeStruct(q.shape,...  6.42 us
  transfers between devices with their start and end apart: 7, of which 5 were waited for; matrix products, arithmetic and copies ran while one was open for 0% of the time, Pallas kernels for 3%

profile of v1, /device:TPU:1, one launch (start us, length us, event | category | flops | bytes accessed | tf_op | source)
XLA Modules:
  0.0 227.5 jit_solution(18388814484977488976)
XLA Ops:
  6.5 0.9 dynamic-slice_select_fusion
  7.4 0.1 broadcast_in_dim.8
  7.5 35.6 %all_to_all.25 = bf16[8,256,128]{2,1,0:T(8,128)(2,1)S(1)} all-to-all(bf16[8,256,128]{2,1,0:T(8,128)(2,1)S(1)} %broadcast_in_dim.8), channel_id=1, replica_groups=mesh['zl'=8,'y'=4,'zh'=2,'x'=4,'c'=2] {'zl'}, dimensions={0} | all-to-all | bytes 1048576 | tf_op jit(solution)/shard_map/cache_gather/all_to_all | solution.py:137
  43.1 1.6 broadcast_in_dim.10
  44.7 4.3 %all-to-all-start.1 = ((bf16[4,2048,128]{2,1,0:T(8,128)(2,1)}), bf16[4,2048,128]{2,1,0:T(8,128)(2,1)S(1)}, u32[]{:S(2)}, u32[]{:S(2)}) async-start(bf16[4,2048,128]{2,1,0:T(8,128)(2,1)} %broadcast_in_dim.10), calls=%async_computation.1 | async-start | bytes 4194304 | tf_op jit(solution)/shard_map/cache_gather/all_to_all | solution.py:137
  49.0 0.0 all-gather.2.cloned.1.call-start
  49.0 18.8 %all-to-all-done.1 = bf16[4,2048,128]{2,1,0:T(8,128)(2,1)S(1)} async-done(((bf16[4,2048,128]{2,1,0:T(8,128)(2,1)}), bf16[4,2048,128]{2,1,0:T(8,128)(2,1)S(1)}, u32[]{:S(2)}, u32[]{:S(2)}) %all-to-all-start.1) | async-done | bytes 2097184 | tf_op jit(solution)/shard_map/cache_gather/all_to_all | solution.py:137
  67.8 10.4 %collective-permute-start = (bf16[8192,128]{1,0:T(8,128)(2,1)S(1)}, bf16[8192,128]{1,0:T(8,128)(2,1)}, u32[]{:S(2)}, u32[]{:S(2)}) collective-permute-start(bf16[8192,128]{1,0:T(8,128)(2,1)S(1)} %bitcast.12), channel_id=1, source_target_pairs={{0,1},{1,0},{2,3},{3,2},{4,5},{5,4},{6,7},{7,6},{8,9},{9,8},{10,11... | collective-permute-start | bytes 6291464 | tf_op jit(solution)/shard_map/cache_gather/ppermute | solution.py:141
  78.2 0.0 copy-done.4
  78.3 1.9 collective-permute-start.2
  80.2 2.0 collective-permute-done.2
  82.2 0.7 pad_maximum_fusion
  82.9 0.0 all-gather.2.cloned.1.call-update
  82.9 0.1 pad_add_fusion.place
  83.0 0.0 collective-permute-done.other_ref
  83.0 6.4 %attention.1 = bf16[256,512]{1,0:T(8,128)(2,1)S(1)} custom-call(s32[32]{0:T(128)S(1)} %copy-done.2, s32[64]{0:T(128)S(1)} %copy-done.3, s32[2]{0:T(128)S(1)} %pad_add_fusion.place, bf16[256,512]{1,0:T(8,128)(2,1)S(1)} %copy-done.1, bf16[8192,128]{1,0:T(8,128)(2,1)S(1)} %bitcast.13, bf16[8192,128]{1,0:T(8,128)(2,1)} %collective-permute-done.other_ref), custom_call_target="tpu_custom_call" | custom-call | tf_op jit(solution)/shard_map/attention/pallas_call | solution.py:103
  89.4 0.1 broadcast_in_dim.22
  89.5 18.0 %all_to_all.26.a_ref = bf16[4,256,512]{2,1,0:T(8,128)(2,1)S(1)} all-to-all(bf16[4,256,512]{2,1,0:T(8,128)(2,1)S(1)} %broadcast_in_dim.22), channel_id=1, replica_groups=mesh['zl'=8,'y'=4,'zh'=2,'x'=4,'c'=2] {'y'}, dimensions={0} | all-to-all | bytes 2097152 | tf_op jit(solution)/shard_map/rows_gather/all_to_all | solution.py:137
  107.6 3.3 %collective-permute-start.1 = (bf16[4,256,512]{2,1,0:T(8,128)(2,1)S(1)}, bf16[4,256,512]{2,1,0:T(8,128)(2,1)S(1)}, u32[]{:S(2)}, u32[]{:S(2)}) collective-permute-start(bf16[4,256,512]{2,1,0:T(8,128)(2,1)S(1)} %all_to_all.26.a_ref), channel_id=1, source_target_pairs={{0,1},{1,0},{2,3},{3,2},{4,5},{5,4},{6,7},{7,6},{8,9},{9,8},{10,11... | collective-permute-start | bytes 3145736 | tf_op jit(solution)/shard_map/rows_gather/ppermute | solution.py:141
  110.9 37.5 %all-gather.2.cloned.1.call-done.w_ref = bf16[1024,1024]{1,0:T(8,128)(2,1)} async-done(((bf16[1024,128]{1,0:T(8,128)(2,1)}), bf16[1024,1024]{1,0:T(8,128)(2,1)}) %all-gather.2.cloned.1.call-update) | async-done | bytes 2097168 | tf_op jit(solution)/shard_map/weight_gather/all_gather | solution.py:149
  148.4 0.0 collective-permute-done.1.b_ref
  148.4 1.6 copy-done
  150.0 3.8 %projection.1 = bf16[4,4,64,1024]{3,2,1,0:T(8,128)(2,1)} custom-call(bf16[4,256,512]{2,1,0:T(8,128)(2,1)S(1)} %all_to_all.26.a_ref, bf16[4,256,512]{2,1,0:T(8,128)(2,1)S(1)} %collective-permute-done.1.b_ref, bf16[1024,1024]{1,0:T(8,128)(2,1)S(1)} %copy-done), custom_call_target="tpu_custom_call" | custom-call | tf_op jit(solution)/shard_map/projection/pallas_call | solution.py:122
  153.8 3.6 %all-to-all-start.3 = ((bf16[4,4,64,1024]{3,2,1,0:T(8,128)(2,1)}), bf16[4,4,64,1024]{3,2,1,0:T(8,128)(2,1)S(1)}, u32[]{:S(2)}, u32[]{:S(2)}) async-start(bf16[4,4,64,1024]{3,2,1,0:T(8,128)(2,1)} %projection.1), calls=%async_computation.3 | async-start | bytes 4194304 | tf_op jit(solution)/shard_map/sum_x/all_to_all | solution.py:169
  157.4 18.0 %all-to-all-done.3 = bf16[4,4,64,1024]{3,2,1,0:T(8,128)(2,1)S(1)} async-done(((bf16[4,4,64,1024]{3,2,1,0:T(8,128)(2,1)}), bf16[4,4,64,1024]{3,2,1,0:T(8,128)(2,1)S(1)}, u32[]{:S(2)}, u32[]{:S(2)}) %all-to-all-start.3) | async-done | bytes 2097184 | tf_op jit(solution)/shard_map/sum_x/all_to_all | solution.py:169
  175.4 0.4 convert_reduce_fusion
  175.9 11.3 %collective-permute-start.3 = (bf16[4,1,32,1024]{3,2,1,0:T(8,128)(2,1)S(1)}, bf16[4,1,32,1024]{3,2,1,0:T(8,128)(2,1)S(1)}, u32[]{:S(2)}, u32[]{:S(2)}) collective-permute-start(bf16[4,1,32,1024]{3,2,1,0:T(8,128)(2,1)S(1)} %dynamic-slice_convert_fusion), channel_id=1, source_target_pairs={{0,8},{8,0},{1,9},{9,1},{2,10},{10,2},{3,11},{11,3},{4,12},{12,4},... | collective-permute-start | bytes 786440 | tf_op jit(solution)/shard_map/sum_zh/ppermute | solution.py:141
  187.2 4.8 %collective-permute-done.3 = bf16[4,1,32,1024]{3,2,1,0:T(8,128)(2,1)S(1)} collective-permute-done((bf16[4,1,32,1024]{3,2,1,0:T(8,128)(2,1)S(1)}, bf16[4,1,32,1024]{3,2,1,0:T(8,128)(2,1)S(1)}, u32[]{:S(2)}, u32[]{:S(2)}) %collective-permute-start.3) | collective-permute-done | bytes 262176 | tf_op jit(solution)/shard_map/sum_zh/ppermute | solution.py:141
  192.0 0.1 add_convert_fusion
  192.1 27.4 %all_to_all.27 = bf16[8,16,1024]{2,1,0:T(8,128)(2,1)S(1)} all-to-all(bf16[8,16,1024]{2,1,0:T(8,128)(2,1)S(1)} %bitcast.19), channel_id=1, replica_groups=mesh['zl'=8,'y'=4,'zh'=2,'x'=4,'c'=2] {'y','c'}, dimensions={0} | all-to-all | bytes 524288 | tf_op jit(solution)/shard_map/columns/all_to_all | solution.py:176
  219.5 0.3 copy.7
  219.8 0.9 reshape.23
  (11 shorter events, 0.1 us)
Async XLA Ops:
  44.7 33.5 %copy-start.4 = (bf16[512,256]{1,0:T(8,128)(2,1)S(1)}, bf16[512,256]{1,0:T(8,128)(2,1)}, u32[]{:S(2)}) copy-start(bf16[512,256]{1,0:T(8,128)(2,1)} %param.11) | copy-start | bytes 786436
  44.7 38.3 %copy-start.1 = (bf16[256,512]{1,0:T(8,128)(2,1)S(1)}, bf16[256,512]{1,0:T(8,128)(2,1)}, u32[]{:S(2)}) copy-start(bf16[256,512]{1,0:T(8,128)(2,1)} %q_ref.1) | copy-start | bytes 786436
  44.7 38.3 %copy-start.2 = (s32[32]{0:T(128)S(1)}, s32[32]{0:T(128)}, u32[]{:S(2)}) copy-start(s32[32]{0:T(128)} %counts.1) | copy-start | bytes 388
  44.7 38.3 %copy-start.3 = (s32[64]{0:T(128)S(1)}, s32[64]{0:T(128)}, u32[]{:S(2)}) copy-start(s32[64]{0:T(128)} %order.1) | copy-start | bytes 772
  44.7 23.1 %all-to-all-start.1 = ((bf16[4,2048,128]{2,1,0:T(8,128)(2,1)}), bf16[4,2048,128]{2,1,0:T(8,128)(2,1)S(1)}, u32[]{:S(2)}, u32[]{:S(2)}) async-start(bf16[4,2048,128]{2,1,0:T(8,128)(2,1)} %broadcast_in_dim.10), calls=%async_computation.1 | async-start | bytes 4194304 | tf_op jit(solution)/shard_map/cache_gather/all_to_all | solution.py:137
  49.0 99.4 %all-gather.2.cloned.1.call-start = ((), (), s32[]{:S(2)}) async-start(), calls=%async_computation.5 | async-start | bytes 2359296 | tf_op jit(solution)/shard_map/weight_gather/all_gather | solution.py:149
  67.8 15.2 %collective-permute-start = (bf16[8192,128]{1,0:T(8,128)(2,1)S(1)}, bf16[8192,128]{1,0:T(8,128)(2,1)}, u32[]{:S(2)}, u32[]{:S(2)}) collective-permute-start(bf16[8192,128]{1,0:T(8,128)(2,1)S(1)} %bitcast.12), channel_id=1, source_target_pairs={{0,1},{1,0},{2,3},{3,2},{4,5},{5,4},{6,7},{7,6},{8,9},{9,8},{10,11... | collective-permute-start | bytes 6291464 | tf_op jit(solution)/shard_map/cache_gather/ppermute | solution.py:141
  78.3 3.9 %collective-permute-start.2 = (bf16[512,128]{1,0:T(8,128)(2,1)S(1)}, bf16[512,128]{1,0:T(8,128)(2,1)S(1)}, u32[]{:S(2)}, u32[]{:S(2)}) collective-permute-start(bf16[512,128]{1,0:T(8,128)(2,1)S(1)} %get-tuple-element.6), channel_id=1, source_target_pairs={{0,1},{1,0},{2,3},{3,2},{4,5},{5,4},{6,7},{7,6},{8,9},{9,8},{10,11... | collective-permute-start | bytes 393224 | tf_op jit(solution)/shard_map/weight_gather/ppermute | solution.py:141
  107.6 40.9 %collective-permute-start.1 = (bf16[4,256,512]{2,1,0:T(8,128)(2,1)S(1)}, bf16[4,256,512]{2,1,0:T(8,128)(2,1)S(1)}, u32[]{:S(2)}, u32[]{:S(2)}) collective-permute-start(bf16[4,256,512]{2,1,0:T(8,128)(2,1)S(1)} %all_to_all.26.a_ref), channel_id=1, source_target_pairs={{0,1},{1,0},{2,3},{3,2},{4,5},{5,4},{6,7},{7,6},{8,9},{9,8},{10,11... | collective-permute-start | bytes 3145736 | tf_op jit(solution)/shard_map/rows_gather/ppermute | solution.py:141
  148.4 1.6 copy-start
  153.8 21.6 %all-to-all-start.3 = ((bf16[4,4,64,1024]{3,2,1,0:T(8,128)(2,1)}), bf16[4,4,64,1024]{3,2,1,0:T(8,128)(2,1)S(1)}, u32[]{:S(2)}, u32[]{:S(2)}) async-start(bf16[4,4,64,1024]{3,2,1,0:T(8,128)(2,1)} %projection.1), calls=%async_computation.3 | async-start | bytes 4194304 | tf_op jit(solution)/shard_map/sum_x/all_to_all | solution.py:169
  175.9 16.1 %collective-permute-start.3 = (bf16[4,1,32,1024]{3,2,1,0:T(8,128)(2,1)S(1)}, bf16[4,1,32,1024]{3,2,1,0:T(8,128)(2,1)S(1)}, u32[]{:S(2)}, u32[]{:S(2)}) collective-permute-start(bf16[4,1,32,1024]{3,2,1,0:T(8,128)(2,1)S(1)} %dynamic-slice_convert_fusion), channel_id=1, source_target_pairs={{0,8},{8,0},{1,9},{9,1},{2,10},{10,2},{3,11},{11,3},{4,12},{12,4},... | collective-permute-start | bytes 786440 | tf_op jit(solution)/shard_map/sum_zh/ppermute | solution.py:141
Sparse Core Ops, SparseCore 0:
  83.0 65.3 all-gather.1

commit v2 on v1

--- a/solution.py
+++ b/solution.py
@@ -10,41 +10,52 @@
 SLOTS = 4
 PAGES = 64
 HEADS = 4
-ZL, Y, ZH, X, C = 8, 4, 2, 4, 2
+ZP, ZQ, Y, ZH, X, C = 4, 2, 4, 2, 4, 2
+ZL = ZP * ZQ
 N_SEQ = ZL * Y
 ROWS = SLOTS * PAGE
 CHUNK = 512
 SCALE = HD**-0.5
 
 
-def attention_kernel(counts, order, place, q_ref, own_ref, other_ref, o_ref, k_sc, v_sc):
+def attention_kernel(counts, order, place, q_ref, *refs):
+    own_refs, other_refs = refs[:Y], refs[Y : 2 * Y]
+    o_ref, k_sc, v_sc = refs[2 * Y :]
     me = place[0]
     core = place[1]
-
-    def sort_pages(k_ref, v_ref):
-        def one(d, rank):
-            held = counts[d]
-            base = ((d % Y) * ZL + d // Y) * ROWS
-            for j in range(SLOTS):
-
-                @pl.when(j < held)
-                def _():
-                    to = pl.multiple_of(order[rank + j] * PAGE, PAGE)
-                    at = pl.multiple_of(base + j * PAGE, PAGE)
-                    k_sc[pl.ds(to, PAGE), :] = k_ref[pl.ds(at, PAGE), :]
-                    v_sc[pl.ds(to, PAGE), :] = v_ref[pl.ds(at, PAGE), :]
-
-            return rank + held
-
-        lax.fori_loop(0, N_SEQ, one, jnp.int32(0))
+    my_y = me % Y
+    my_q = (me // Y) % ZQ
+
+    def sort_pages(k_refs, v_refs):
+        def one(z, rank):
+            base = (((z + my_q) % ZQ) * ZP + z // ZQ) * ROWS
+            for col in range(Y):
+                held = counts[z * Y + col]
+                for shift in range(Y):
+
+                    @pl.when((my_y + shift) % Y == col)
+                    def _():
+                        for j in range(SLOTS):
+
+                            @pl.when(j < held)
+                            def _():
+                                to = pl.multiple_of(order[rank + j] * PAGE, PAGE)
+                                at = pl.multiple_of(base + j * PAGE, PAGE)
+                                k_sc[pl.ds(to, PAGE), :] = k_refs[shift][pl.ds(at, PAGE), :]
+                                v_sc[pl.ds(to, PAGE), :] = v_refs[shift][pl.ds(at, PAGE), :]
+
+                rank = rank + held
+            return rank
+
+        lax.fori_loop(0, ZL, one, jnp.int32(0))
 
     @pl.when(core == 0)
     def _():
-        sort_pages(own_ref, other_ref)
+        sort_pages(own_refs, other_refs)
 
     @pl.when(core == 1)
     def _():
-        sort_pages(other_ref, own_ref)
+        sort_pages(other_refs, own_refs)
 
     before = lax.fori_loop(0, me, lambda d, s: s + counts[d], jnp.int32(0))
     live = counts[me]
@@ -103,11 +114,11 @@
     return pl.pallas_call(
         attention_kernel,
         out_shape=jax.ShapeDtypeStruct(q.shape, jnp.bfloat16),
-        in_specs=[smem, smem, smem, vmem, vmem, vmem],
+        in_specs=[smem, smem, smem, vmem] + [vmem] * (2 * Y),
         out_specs=vmem,
         scratch_shapes=[pltpu.VMEM((PAGES * PAGE, HD), jnp.bfloat16) for _ in range(2)],
         compiler_params=pltpu.CompilerParams(vmem_limit_bytes=40 << 20),
-    )(counts, order, place, q, own, other)
+    )(counts, order, place, q, *own, *other)
 
 
 def project_kernel(a_ref, b_ref, w_ref, o_ref):
@@ -141,12 +152,16 @@
     return lax.ppermute(piece, axis, [(0, 1), (1, 0)])
 
 
+def from_next(piece, axis, count, shift):
+    return lax.ppermute(piece, axis, [((i + shift) % count, i) for i in range(count)])
+
+
 def body(counts, order, queries, keys, values, weight):
-    zl, y, zh, x, c = (lax.axis_index(name) for name in ("zl", "y", "zh", "x", "c"))
+    zp, zq, y, zh, x, c = (lax.axis_index(name) for name in ("zp", "zq", "y", "zh", "x", "c"))
     with jax.named_scope("weight_gather"):
         given = swap(lax.dynamic_slice_in_dim(weight, (1 - c) * 128, 128, 1), "c")
         kept = lax.dynamic_slice_in_dim(weight, c * 128, 128, 1)
-        wide = lax.all_gather(jnp.concatenate([kept, given], axis=0), "zl", axis=1, tiled=True)
+        narrow = jnp.concatenate([kept, given], axis=0)
     with jax.named_scope("cache_gather"):
         head = (zh * X + x) * HD
         piece = jnp.where(
@@ -154,12 +169,16 @@
             lax.dynamic_slice_in_dim(keys, head, HD, 1),
             lax.dynamic_slice_in_dim(values, head, HD, 1),
         )
-        own = spread(piece, "zl", ZL).reshape(ZL * ROWS, HD)
-        own = spread(own, "y", Y).reshape(N_SEQ * ROWS, HD)
-        other = swap(own, "c")
+        narrow, piece = lax.optimization_barrier((narrow, piece))
+        wide = lax.all_gather(narrow, ("zp", "zq"), axis=1, tiled=True)
+        near = spread(piece, "zp", ZP)
+        near = jnp.concatenate([near, swap(near, "zq")], axis=0).reshape(ZL * ROWS, HD)
+        own = [near] + [from_next(near, "y", Y, shift) for shift in range(1, Y)]
+        other = [swap(one, "c") for one in own]
     with jax.named_scope("attention"):
-        place = jnp.stack([zl * Y + y, c]).astype(jnp.int32)
+        place = jnp.stack([(zp * ZQ + zq) * Y + y, c]).astype(jnp.int32)
         heads = attend(counts, order, place, queries, own, other)
+        heads, wide = lax.optimization_barrier((heads, wide))
     with jax.named_scope("rows_gather"):
         mine = spread(heads, "y", Y)
         theirs = swap(mine, "c")
@@ -179,8 +198,8 @@
 
 
 def solution(mesh):
-    fine = Mesh(mesh.devices.reshape(ZL, Y, ZH, X, C), ("zl", "y", "zh", "x", "c"))
-    seq, tp = ("zl", "y"), ("zh", "x", "c")
+    fine = Mesh(mesh.devices.reshape(ZP, ZQ, Y, ZH, X, C), ("zp", "zq", "y", "zh", "x", "c"))
+    seq, tp = ("zp", "zq", "y"), ("zh", "x", "c")
     return jax.shard_map(
         body,
         mesh=fine,

time: 231 us -> 211 us (0.913)
  blocking collectives: 81 us -> 51.1 us
  starting transfers between devices: 34.9 us -> 60 us
  waiting for transfers between devices: 81.1 us -> 63.4 us
  Pallas kernels: 10.2 us -> 14.4 us
    all_gather x1, waiting for transfers between devices: 37.5 us -> 0.02 us  [body(): wide = lax.all_gather(narrow, ('zp', 'zq'), axis=1, tiled=True)]
    ppermute x4 -> x8, waiting for transfers between devices: 6.79 us -> 34.4 us  [swap(): return lax.ppermute(piece, axis, [(0, 1), (1, 0)])]
    ppermute x4 -> x8, starting transfers between devices: 26.9 us -> 47.4 us  [swap(): return lax.ppermute(piece, axis, [(0, 1), (1, 0)])]
    all_to_all x1 -> x0, waiting for transfers between devices: 18.8 us -> none  [spread(): lax.all_to_all(jnp.broadcast_to(piece[None], (count, *piece.shape)), axis...]
    all_to_all x1, blocking collectives: 27.4 us -> 10.4 us  [body(): mixed = lax.all_to_all(mixed.reshape(Y * C, 16, ZL * 128), ('y', 'c'), 0, 0)]
    all_to_all x2, blocking collectives: 53.6 us -> 40.7 us  [spread(): lax.all_to_all(jnp.broadcast_to(piece[None], (count, *piece.shape)), axis...]
    ppermute x0 -> x3, starting transfers between devices: none -> 8.61 us  [from_next(): lax.ppermute(piece, axis, [((i + shift) % count, i) for i in range(count)])]
    all_to_all x1, waiting for transfers between devices: 18 us -> 25.8 us  [body(): parts = lax.all_to_all(parts, 'x', 0, 0)]
  transfers between devices with their start and end apart: 7 -> 13, of which waited for: 5 -> 7; matrix products, arithmetic and copies ran while one was open for 0% -> 1% of each run, Pallas kernels for 3% -> 5%
where the time goes in v2:
time: 211 us; the launch traced here: 208 us
  waiting for transfers between devices  63.4 us (30%)
  starting transfers between devices  60 us (28%)
  blocking collectives  51.1 us (24%)
  Pallas kernels  14.4 us (7%)
  between operations  13.6 us (6%)
  local copies, waits for them, and re-layouts  3.33 us (2%)
  other arithmetic  2.18 us (1%)
    ppermute x8, starting transfers between devices, swap(): return lax.ppermute(piece, axis, [(0, 1), (1, 0)])  47.4 us
    all_to_all x2, blocking collectives, spread(): lax.all_to_all(jnp.broadcast_to(piece[None], (count, *piece.shape)), axis...  40.7 us
    ppermute x8, waiting for transfers between devices, swap(): return lax.ppermute(piece, axis, [(0, 1), (1, 0)])  34.4 us
    all_to_all x1, waiting for transfers between devices, body(): parts = lax.all_to_all(parts, 'x', 0, 0)  25.8 us
    pallas_call x1, Pallas kernels, attend(): pl.pallas_call(attention_kernel, out_shape=jax.ShapeDtypeStruct(q.shape,...  10.6 us
    all_to_all x1, blocking collectives, body(): mixed = lax.all_to_all(mixed.reshape(Y * C, 16, ZL * 128), ('y', 'c'), 0, 0)  10.4 us
    ppermute x3, starting transfers between devices, from_next(): lax.ppermute(piece, axis, [((i + shift) % count, i) for i in range(count)])  8.61 us
  transfers between devices with their start and end apart: 13, of which 7 were waited for; matrix products, arithmetic and copies ran while one was open for 1% of the time, Pallas kernels for 5%

profile of v2, /device:TPU:1, one launch (start us, length us, event | category | flops | bytes accessed | tf_op | source)
XLA Modules:
  0.0 208.0 jit_solution(14965022695740336771)
XLA Ops:
  6.5 1.0 constant_dynamic-slice_fusion.1
  7.6 8.8 %collective-permute-start = (bf16[512,128]{1,0:T(8,128)(2,1)S(1)}, bf16[512,128]{1,0:T(8,128)(2,1)S(1)}, u32[]{:S(2)}, u32[]{:S(2)}) collective-permute-start(bf16[512,128]{1,0:T(8,128)(2,1)S(1)} %get-tuple-element.14), channel_id=1, source_target_pairs={{0,1},{1,0},{2,3},{3,2},{4,5},{5,4},{6,7},{7,6},{8,9},{9,8},{10,11... | collective-permute-start | bytes 393224 | tf_op jit(solution)/shard_map/weight_gather/ppermute | solution.py:152
  16.4 0.9 dynamic-slice_select_fusion
  17.3 0.7 pad_maximum_fusion.1
  18.1 20.0 %all_to_all.20 = bf16[4,256,128]{2,1,0:T(8,128)(2,1)S(1)} all-to-all(bf16[4,256,128]{2,1,0:T(8,128)(2,1)S(1)} %broadcast_in_dim.4), channel_id=1, replica_groups=mesh['zp'=4,'zq'=2,'y'=4,'zh'=2,'x'=4,'c'=2] {'zp'}, dimensions={0} | all-to-all | bytes 524288 | tf_op jit(solution)/shard_map/cache_gather/all_to_all | solution.py:148
  38.1 4.7 %collective-permute-start.1 = (bf16[4,256,128]{2,1,0:T(8,128)(2,1)S(1)}, bf16[4,256,128]{2,1,0:T(8,128)(2,1)S(1)}, u32[]{:S(2)}, u32[]{:S(2)}) collective-permute-start(bf16[4,256,128]{2,1,0:T(8,128)(2,1)S(1)} %all_to_all.20), channel_id=1, source_target_pairs={{0,64},{64,0},{1,65},{65,1},{2,66},{66,2},{3,67},{67,3},{4,68},{68... | collective-permute-start | bytes 786440 | tf_op jit(solution)/shard_map/cache_gather/ppermute | solution.py:152
  42.8 14.8 %collective-permute-done.1 = bf16[4,256,128]{2,1,0:T(8,128)(2,1)S(1)} collective-permute-done((bf16[4,256,128]{2,1,0:T(8,128)(2,1)S(1)}, bf16[4,256,128]{2,1,0:T(8,128)(2,1)S(1)}, u32[]{:S(2)}, u32[]{:S(2)}) %collective-permute-start.1) | collective-permute-done | bytes 262176 | tf_op jit(solution)/shard_map/cache_gather/ppermute | solution.py:152
  57.6 1.9 collective-permute-start.2
  59.6 4.8 %collective-permute-start.3 = (bf16[2048,128]{1,0:T(8,128)(2,1)S(1)}, bf16[2048,128]{1,0:T(8,128)(2,1)S(1)}, u32[]{:S(2)}, u32[]{:S(2)}) collective-permute-start(bf16[2048,128]{1,0:T(8,128)(2,1)S(1)} %bitcast.12), channel_id=1, source_target_pairs={{32,0},{48,16},{0,32},{16,48},{33,1},{49,17},{1,33},{17,49},{34,2}... | collective-permute-start | bytes 1572872 | tf_op jit(solution)/shard_map/cache_gather/ppermute | solution.py:156
  64.4 1.9 collective-permute-start.4
  66.3 5.8 %collective-permute-start.5 = (bf16[2048,128]{1,0:T(8,128)(2,1)S(1)}, bf16[2048,128]{1,0:T(8,128)(2,1)S(1)}, u32[]{:S(2)}, u32[]{:S(2)}) collective-permute-start(bf16[2048,128]{1,0:T(8,128)(2,1)S(1)} %bitcast.14), channel_id=1, source_target_pairs={{0,1},{1,0},{2,3},{3,2},{4,5},{5,4},{6,7},{7,6},{8,9},{9,8},{10,11... | collective-permute-start | bytes 1572872 | tf_op jit(solution)/shard_map/cache_gather/ppermute | solution.py:152
  72.2 6.2 %collective-permute-start.6 = (bf16[2048,128]{1,0:T(8,128)(2,1)S(1)}, bf16[2048,128]{1,0:T(8,128)(2,1)S(1)}, u32[]{:S(2)}, u32[]{:S(2)}) collective-permute-start(bf16[2048,128]{1,0:T(8,128)(2,1)S(1)} %collective-permute-done.2.refs_1_), channel_id=1, source_target_pairs={{0,1},{1,0},{2,3},{3,2},{4,5},{5,4},{6,7},{7,6},{8,9},{9,8},{10,11... | collective-permute-start | bytes 1572872 | tf_op jit(solution)/shard_map/cache_gather/ppermute | solution.py:152
  78.4 5.9 %collective-permute-start.7 = (bf16[2048,128]{1,0:T(8,128)(2,1)S(1)}, bf16[2048,128]{1,0:T(8,128)(2,1)}, u32[]{:S(2)}, u32[]{:S(2)}) collective-permute-start(bf16[2048,128]{1,0:T(8,128)(2,1)S(1)} %collective-permute-done.3.refs_2_), channel_id=1, source_target_pairs={{0,1},{1,0},{2,3},{3,2},{4,5},{5,4},{6,7},{7,6},{8,9},{9,8},{10,11... | collective-permute-start | bytes 1572872 | tf_op jit(solution)/shard_map/cache_gather/ppermute | solution.py:152
  84.2 3.2 %collective-permute-done.4.refs_3_ = bf16[2048,128]{1,0:T(8,128)(2,1)S(1)} collective-permute-done((bf16[2048,128]{1,0:T(8,128)(2,1)S(1)}, bf16[2048,128]{1,0:T(8,128)(2,1)S(1)}, u32[]{:S(2)}, u32[]{:S(2)}) %collective-permute-start.4) | collective-permute-done | bytes 524320 | tf_op jit(solution)/shard_map/cache_gather/ppermute | solution.py:156
  87.4 3.1 %collective-permute-start.8 = (bf16[2048,128]{1,0:T(8,128)(2,1)S(1)}, bf16[2048,128]{1,0:T(8,128)(2,1)}, u32[]{:S(2)}, u32[]{:S(2)}) collective-permute-start(bf16[2048,128]{1,0:T(8,128)(2,1)S(1)} %collective-permute-done.4.refs_3_), channel_id=1, source_target_pairs={{0,1},{1,0},{2,3},{3,2},{4,5},{5,4},{6,7},{7,6},{8,9},{9,8},{10,11... | collective-permute-start | bytes 1572872 | tf_op jit(solution)/shard_map/cache_gather/ppermute | solution.py:152
  90.5 0.1 pad_add_fusion.place
  90.6 1.5 collective-permute-done.8.refs_7_
  92.1 0.9 copy-done.1
  93.1 10.6 %attention.1 = bf16[256,512]{1,0:T(8,128)(2,1)S(1)} custom-call(s32[32]{0:T(128)S(1)} %copy-done.2, s32[64]{0:T(128)S(1)} %copy-done.3, s32[2]{0:T(128)S(1)} %pad_add_fusion.place, bf16[256,512]{1,0:T(8,128)(2,1)S(1)} %copy-done.1, bf16[2048,128]{1,0:T(8,128)(2,1)S(1)} %bitcast.15, bf16[2048,128]{1,0:T(8,128)(2,1)S(1)} %collective-permute-done.2.refs_1_, ...), custom_call_target="tpu_custom_call" | custom-call | tf_op jit(solution)/shard_map/attention/pallas_call | solution.py:114
  103.7 0.1 broadcast_in_dim.5
  103.8 20.7 %all_to_all.21.a_ref = bf16[4,256,512]{2,1,0:T(8,128)(2,1)S(1)} all-to-all(bf16[4,256,512]{2,1,0:T(8,128)(2,1)S(1)} %broadcast_in_dim.5), channel_id=1, replica_groups=mesh['zp'=4,'zq'=2,'y'=4,'zh'=2,'x'=4,'c'=2] {'y'}, dimensions={0} | all-to-all | bytes 2097152 | tf_op jit(solution)/shard_map/rows_gather/all_to_all | solution.py:148
  124.5 3.2 %collective-permute-start.9 = (bf16[4,256,512]{2,1,0:T(8,128)(2,1)S(1)}, bf16[4,256,512]{2,1,0:T(8,128)(2,1)S(1)}, u32[]{:S(2)}, u32[]{:S(2)}) collective-permute-start(bf16[4,256,512]{2,1,0:T(8,128)(2,1)S(1)} %all_to_all.21.a_ref), channel_id=1, source_target_pairs={{0,1},{1,0},{2,3},{3,2},{4,5},{5,4},{6,7},{7,6},{8,9},{9,8},{10,11... | collective-permute-start | bytes 3145736 | tf_op jit(solution)/shard_map/rows_gather/ppermute | solution.py:152
  127.7 2.3 %collective-permute-done.9.b_ref = bf16[4,256,512]{2,1,0:T(8,128)(2,1)S(1)} collective-permute-done((bf16[4,256,512]{2,1,0:T(8,128)(2,1)S(1)}, bf16[4,256,512]{2,1,0:T(8,128)(2,1)S(1)}, u32[]{:S(2)}, u32[]{:S(2)}) %collective-permute-start.9) | collective-permute-done | bytes 1048608 | tf_op jit(solution)/shard_map/rows_gather/ppermute | solution.py:152
  130.0 3.8 %projection.1 = bf16[4,4,64,1024]{3,2,1,0:T(8,128)(2,1)} custom-call(bf16[4,256,512]{2,1,0:T(8,128)(2,1)S(1)} %all_to_all.21.a_ref, bf16[4,256,512]{2,1,0:T(8,128)(2,1)S(1)} %collective-permute-done.9.b_ref, bf16[1024,1024]{1,0:T(8,128)(2,1)S(1)} %copy-done), custom_call_target="tpu_custom_call" | custom-call | tf_op jit(solution)/shard_map/projection/pallas_call | solution.py:133
  133.7 3.9 %all-to-all-start.2 = ((bf16[4,4,64,1024]{3,2,1,0:T(8,128)(2,1)}), bf16[4,4,64,1024]{3,2,1,0:T(8,128)(2,1)S(1)}, u32[]{:S(2)}, u32[]{:S(2)}) async-start(bf16[4,4,64,1024]{3,2,1,0:T(8,128)(2,1)} %projection.1), calls=%async_computation.2 | async-start | bytes 4194304 | tf_op jit(solution)/shard_map/sum_x/all_to_all | solution.py:188
  137.7 25.8 %all-to-all-done.2 = bf16[4,4,64,1024]{3,2,1,0:T(8,128)(2,1)S(1)} async-done(((bf16[4,4,64,1024]{3,2,1,0:T(8,128)(2,1)}), bf16[4,4,64,1024]{3,2,1,0:T(8,128)(2,1)S(1)}, u32[]{:S(2)}, u32[]{:S(2)}) %all-to-all-start.2) | async-done | bytes 2097184 | tf_op jit(solution)/shard_map/sum_x/all_to_all | solution.py:188
  163.4 0.4 convert_reduce_fusion
  163.9 9.8 %collective-permute-start.10 = (bf16[4,1,32,1024]{3,2,1,0:T(8,128)(2,1)S(1)}, bf16[4,1,32,1024]{3,2,1,0:T(8,128)(2,1)S(1)}, u32[]{:S(2)}, u32[]{:S(2)}) collective-permute-start(bf16[4,1,32,1024]{3,2,1,0:T(8,128)(2,1)S(1)} %dynamic-slice_convert_fusion), channel_id=1, source_target_pairs={{0,8},{8,0},{1,9},{9,1},{2,10},{10,2},{3,11},{11,3},{4,12},{12,4},... | collective-permute-start | bytes 786440 | tf_op jit(solution)/shard_map/sum_zh/ppermute | solution.py:152
  173.7 15.7 %collective-permute-done.10 = bf16[4,1,32,1024]{3,2,1,0:T(8,128)(2,1)S(1)} collective-permute-done((bf16[4,1,32,1024]{3,2,1,0:T(8,128)(2,1)S(1)}, bf16[4,1,32,1024]{3,2,1,0:T(8,128)(2,1)S(1)}, u32[]{:S(2)}, u32[]{:S(2)}) %collective-permute-start.10) | collective-permute-done | bytes 262176 | tf_op jit(solution)/shard_map/sum_zh/ppermute | solution.py:152
  189.5 10.4 %all_to_all.22 = bf16[8,16,1024]{2,1,0:T(8,128)(2,1)S(1)} all-to-all(bf16[8,16,1024]{2,1,0:T(8,128)(2,1)S(1)} %bitcast.20), channel_id=1, replica_groups=mesh['zp'=4,'zq'=2,'y'=4,'zh'=2,'x'=4,'c'=2] {'y','c'}, dimensions={0} | all-to-all | bytes 524288 | tf_op jit(solution)/shard_map/columns/all_to_all | solution.py:195
  200.0 0.3 copy.7
  200.2 0.9 reshape.21
  (21 shorter events, 0.3 us)
Async XLA Ops:
  6.5 85.6 %copy-start.2 = (s32[32]{0:T(128)S(1)}, s32[32]{0:T(128)}, u32[]{:S(2)}) copy-start(s32[32]{0:T(128)} %counts.1) | copy-start | bytes 388
  6.5 85.6 %copy-start.3 = (s32[64]{0:T(128)S(1)}, s32[64]{0:T(128)}, u32[]{:S(2)}) copy-start(s32[64]{0:T(128)} %order.1) | copy-start | bytes 772
  6.5 97.1 %all-gather.2.cloned.1.call-start = ((), (), s32[]{:S(2)}) async-start(), calls=%async_computation.4 | async-start | bytes 2359296 | tf_op jit(solution)/shard_map/cache_gather/all_gather | solution.py:173
  7.6 9.8 %collective-permute-start = (bf16[512,128]{1,0:T(8,128)(2,1)S(1)}, bf16[512,128]{1,0:T(8,128)(2,1)S(1)}, u32[]{:S(2)}, u32[]{:S(2)}) collective-permute-start(bf16[512,128]{1,0:T(8,128)(2,1)S(1)} %get-tuple-element.14), channel_id=1, source_target_pairs={{0,1},{1,0},{2,3},{3,2},{4,5},{5,4},{6,7},{7,6},{8,9},{9,8},{10,11... | collective-permute-start | bytes 393224 | tf_op jit(solution)/shard_map/weight_gather/ppermute | solution.py:152
  38.1 19.5 %collective-permute-start.1 = (bf16[4,256,128]{2,1,0:T(8,128)(2,1)S(1)}, bf16[4,256,128]{2,1,0:T(8,128)(2,1)S(1)}, u32[]{:S(2)}, u32[]{:S(2)}) collective-permute-start(bf16[4,256,128]{2,1,0:T(8,128)(2,1)S(1)} %all_to_all.20), channel_id=1, source_target_pairs={{0,64},{64,0},{1,65},{65,1},{2,66},{66,2},{3,67},{67,3},{4,68},{68... | collective-permute-start | bytes 786440 | tf_op jit(solution)/shard_map/cache_gather/ppermute | solution.py:152
  57.6 14.5 %collective-permute-start.2 = (bf16[2048,128]{1,0:T(8,128)(2,1)S(1)}, bf16[2048,128]{1,0:T(8,128)(2,1)S(1)}, u32[]{:S(2)}, u32[]{:S(2)}) collective-permute-start(bf16[2048,128]{1,0:T(8,128)(2,1)S(1)} %bitcast.11), channel_id=1, source_target_pairs={{16,0},{32,16},{48,32},{0,48},{17,1},{33,17},{49,33},{1,49},{18,2}... | collective-permute-start | bytes 1572872 | tf_op jit(solution)/shard_map/cache_gather/ppermute | solution.py:156
  59.6 18.8 %collective-permute-start.3 = (bf16[2048,128]{1,0:T(8,128)(2,1)S(1)}, bf16[2048,128]{1,0:T(8,128)(2,1)S(1)}, u32[]{:S(2)}, u32[]{:S(2)}) collective-permute-start(bf16[2048,128]{1,0:T(8,128)(2,1)S(1)} %bitcast.12), channel_id=1, source_target_pairs={{32,0},{48,16},{0,32},{16,48},{33,1},{49,17},{1,33},{17,49},{34,2}... | collective-permute-start | bytes 1572872 | tf_op jit(solution)/shard_map/cache_gather/ppermute | solution.py:156
  64.4 23.0 %collective-permute-start.4 = (bf16[2048,128]{1,0:T(8,128)(2,1)S(1)}, bf16[2048,128]{1,0:T(8,128)(2,1)S(1)}, u32[]{:S(2)}, u32[]{:S(2)}) collective-permute-start(bf16[2048,128]{1,0:T(8,128)(2,1)S(1)} %bitcast.13), channel_id=1, source_target_pairs={{48,0},{0,16},{16,32},{32,48},{49,1},{1,17},{17,33},{33,49},{50,2}... | collective-permute-start | bytes 1572872 | tf_op jit(solution)/shard_map/cache_gather/ppermute | solution.py:156
  66.3 24.3 %collective-permute-start.5 = (bf16[2048,128]{1,0:T(8,128)(2,1)S(1)}, bf16[2048,128]{1,0:T(8,128)(2,1)S(1)}, u32[]{:S(2)}, u32[]{:S(2)}) collective-permute-start(bf16[2048,128]{1,0:T(8,128)(2,1)S(1)} %bitcast.14), channel_id=1, source_target_pairs={{0,1},{1,0},{2,3},{3,2},{4,5},{5,4},{6,7},{7,6},{8,9},{9,8},{10,11... | collective-permute-start | bytes 1572872 | tf_op jit(solution)/shard_map/cache_gather/ppermute | solution.py:152
  72.2 18.4 %collective-permute-start.6 = (bf16[2048,128]{1,0:T(8,128)(2,1)S(1)}, bf16[2048,128]{1,0:T(8,128)(2,1)S(1)}, u32[]{:S(2)}, u32[]{:S(2)}) collective-permute-start(bf16[2048,128]{1,0:T(8,128)(2,1)S(1)} %collective-permute-done.2.refs_1_), channel_id=1, source_target_pairs={{0,1},{1,0},{2,3},{3,2},{4,5},{5,4},{6,7},{7,6},{8,9},{9,8},{10,11... | collective-permute-start | bytes 1572872 | tf_op jit(solution)/shard_map/cache_gather/ppermute | solution.py:152
  78.4 12.2 %collective-permute-start.7 = (bf16[2048,128]{1,0:T(8,128)(2,1)S(1)}, bf16[2048,128]{1,0:T(8,128)(2,1)}, u32[]{:S(2)}, u32[]{:S(2)}) collective-permute-start(bf16[2048,128]{1,0:T(8,128)(2,1)S(1)} %collective-permute-done.3.refs_2_), channel_id=1, source_target_pairs={{0,1},{1,0},{2,3},{3,2},{4,5},{5,4},{6,7},{7,6},{8,9},{9,8},{10,11... | collective-permute-start | bytes 1572872 | tf_op jit(solution)/shard_map/cache_gather/ppermute | solution.py:152
  87.4 4.7 %collective-permute-start.8 = (bf16[2048,128]{1,0:T(8,128)(2,1)S(1)}, bf16[2048,128]{1,0:T(8,128)(2,1)}, u32[]{:S(2)}, u32[]{:S(2)}) collective-permute-start(bf16[2048,128]{1,0:T(8,128)(2,1)S(1)} %collective-permute-done.4.refs_3_), channel_id=1, source_target_pairs={{0,1},{1,0},{2,3},{3,2},{4,5},{5,4},{6,7},{7,6},{8,9},{9,8},{10,11... | collective-permute-start | bytes 1572872 | tf_op jit(solution)/shard_map/cache_gather/ppermute | solution.py:152
  92.1 1.0 copy-start.1
  103.7 26.3 %copy-start = (bf16[1024,1024]{1,0:T(8,128)(2,1)S(1)}, bf16[1024,1024]{1,0:T(8,128)(2,1)}, u32[]{:S(2)}) copy-start(bf16[1024,1024]{1,0:T(8,128)(2,1)} %all-gather.2.cloned.1.call-done.w_ref) | copy-start | bytes 6291460
  124.5 5.4 %collective-permute-start.9 = (bf16[4,256,512]{2,1,0:T(8,128)(2,1)S(1)}, bf16[4,256,512]{2,1,0:T(8,128)(2,1)S(1)}, u32[]{:S(2)}, u32[]{:S(2)}) collective-permute-start(bf16[4,256,512]{2,1,0:T(8,128)(2,1)S(1)} %all_to_all.21.a_ref), channel_id=1, source_target_pairs={{0,1},{1,0},{2,3},{3,2},{4,5},{5,4},{6,7},{7,6},{8,9},{9,8},{10,11... | collective-permute-start | bytes 3145736 | tf_op jit(solution)/shard_map/rows_gather/ppermute | solution.py:152
  133.7 29.7 %all-to-all-start.2 = ((bf16[4,4,64,1024]{3,2,1,0:T(8,128)(2,1)}), bf16[4,4,64,1024]{3,2,1,0:T(8,128)(2,1)S(1)}, u32[]{:S(2)}, u32[]{:S(2)}) async-start(bf16[4,4,64,1024]{3,2,1,0:T(8,128)(2,1)} %projection.1), calls=%async_computation.2 | async-start | bytes 4194304 | tf_op jit(solution)/shard_map/sum_x/all_to_all | solution.py:188
  163.9 25.5 %collective-permute-start.10 = (bf16[4,1,32,1024]{3,2,1,0:T(8,128)(2,1)S(1)}, bf16[4,1,32,1024]{3,2,1,0:T(8,128)(2,1)S(1)}, u32[]{:S(2)}, u32[]{:S(2)}) collective-permute-start(bf16[4,1,32,1024]{3,2,1,0:T(8,128)(2,1)S(1)} %dynamic-slice_convert_fusion), channel_id=1, source_target_pairs={{0,8},{8,0},{1,9},{9,1},{2,10},{10,2},{3,11},{11,3},{4,12},{12,4},... | collective-permute-start | bytes 786440 | tf_op jit(solution)/shard_map/sum_zh/ppermute | solution.py:152
Sparse Core Ops, SparseCore 0:
  18.2 71.2 all-gather.1

commit v3 on v1

--- a/solution.py
+++ b/solution.py
@@ -10,7 +10,10 @@
 SLOTS = 4
 PAGES = 64
 HEADS = 4
-ZL, Y, ZH, X, C = 8, 4, 2, 4, 2
+ZA, ZB, ZQ, Y, ZH, X, C = 2, 2, 2, 4, 2, 4, 2
+ZL, QUAD = ZA * ZB * ZQ, ZB * ZQ
+Z = ZH * ZL
+LINE = ("za", "zb", "zq", "zh", "c")
 N_SEQ = ZL * Y
 ROWS = SLOTS * PAGE
 CHUNK = 512
@@ -20,11 +23,16 @@
 def attention_kernel(counts, order, place, q_ref, own_ref, other_ref, o_ref, k_sc, v_sc):
     me = place[0]
     core = place[1]
+    my_zh = place[2]
+    my_z = me // Y
 
     def sort_pages(k_ref, v_ref):
         def one(d, rank):
             held = counts[d]
-            base = ((d % Y) * ZL + d // Y) * ROWS
+            z = d // Y
+            far = (z + my_z) % 2
+            near = my_z + far * (1 - 2 * (my_z % 2))
+            base = ((d % Y) * ZL + far * (ZL // 2) + (z - near + ZL) % ZL // 2) * ROWS
             for j in range(SLOTS):
 
                 @pl.when(j < held)
@@ -50,10 +58,10 @@
     live = counts[me]
 
     def store(j, rows):
+        kept = (my_zh == j // 2).astype(jnp.int32)
         for b in range(2):
-            to = (2 * (j % 2) + b) * 64 + (j // 2) * 32
             for h in range(HEADS):
-                o_ref[to : to + 32, h * HD : (h + 1) * HD] = rows(h, b)
+                o_ref[kept, 2 * (j % 2) + b, :, h * HD : (h + 1) * HD] = rows(h, b)
 
     for j in range(SLOTS):
 
@@ -102,7 +110,7 @@
     vmem = pl.BlockSpec(memory_space=pltpu.VMEM)
     return pl.pallas_call(
         attention_kernel,
-        out_shape=jax.ShapeDtypeStruct(q.shape, jnp.bfloat16),
+        out_shape=jax.ShapeDtypeStruct((ZH, X, 32, HEADS * HD), jnp.bfloat16),
         in_specs=[smem, smem, smem, vmem, vmem, vmem],
         out_specs=vmem,
         scratch_shapes=[pltpu.VMEM((PAGES * PAGE, HD), jnp.bfloat16) for _ in range(2)],
@@ -110,27 +118,26 @@
     )(counts, order, place, q, own, other)
 
 
-def project_kernel(a_ref, b_ref, w_ref, o_ref):
-    half = a_ref.shape[2]
-    part = jnp.dot(a_ref[0], w_ref[:half, :], preferred_element_type=jnp.float32)
-    part += jnp.dot(b_ref[0], w_ref[half:, :], preferred_element_type=jnp.float32)
-    o_ref[...] = part.astype(jnp.bfloat16).reshape(o_ref.shape)
-
-
-def project(a, b, w):
-    n = w.shape[1]
+def project_kernel(me, a_ref, b_ref, w_ref, o_ref):
+    half = a_ref.shape[-1]
+    w = jnp.concatenate([w_ref[0, 0], w_ref[0, 1]], axis=1)
+    part = jnp.dot(a_ref[...].reshape(-1, half), w[:half], preferred_element_type=jnp.float32)
+    part += jnp.dot(b_ref[...].reshape(-1, half), w[half:], preferred_element_type=jnp.float32)
+    part = part.astype(jnp.bfloat16).reshape(QUAD, X, 32, 2 * HD)
+    for i in range(QUAD):
+        o_ref[:, me[0] ^ i] = part[i]
+
+
+def project(me, a, b, w):
+    rows = pl.BlockSpec(a.shape, lambda i: (0, 0, 0, 0))
     return pl.pallas_call(
         project_kernel,
         grid=(Y,),
-        out_shape=jax.ShapeDtypeStruct((X, Y, ROWS // X, n), jnp.bfloat16),
-        in_specs=[
-            pl.BlockSpec((1, ROWS, a.shape[2]), lambda i: (i, 0, 0)),
-            pl.BlockSpec((1, ROWS, a.shape[2]), lambda i: (i, 0, 0)),
-            pl.BlockSpec(w.shape, lambda i: (0, 0)),
-        ],
-        out_specs=pl.BlockSpec((X, 1, ROWS // X, n), lambda i: (0, i, 0, 0)),
-        compiler_params=pltpu.CompilerParams(vmem_limit_bytes=40 << 20),
-    )(a, b, w)
+        out_shape=jax.ShapeDtypeStruct((X, QUAD, 32, ZL * HD), jnp.bfloat16),
+        in_specs=[pl.BlockSpec(memory_space=pltpu.SMEM), rows, rows, pl.BlockSpec((1, *w.shape[1:]), lambda i: (i, 0, 0, 0))],
+        out_specs=pl.BlockSpec((X, QUAD, 32, 2 * HD), lambda i: (0, 0, 0, i)),
+        compiler_params=pltpu.CompilerParams(vmem_limit_bytes=24 << 20),
+    )(me, a, b, w)
 
 
 def spread(piece, axis, count):
@@ -141,46 +148,86 @@
     return lax.ppermute(piece, axis, [(0, 1), (1, 0)])
 
 
+def quad(piece, step):
+    return lax.ppermute(piece, ("zb", "zq"), [(i, i ^ step) for i in range(QUAD)])
+
+
+def along(piece, step):
+    def place(z, c):
+        return ((z % ZL) * ZH + z // ZL) * C + c
+
+    perm = [(place(z, c), place((z + step(z, c)) % Z, c)) for z in range(Z) for c in range(C)]
+    return lax.ppermute(piece, LINE, perm)
+
+
 def body(counts, order, queries, keys, values, weight):
-    zl, y, zh, x, c = (lax.axis_index(name) for name in ("zl", "y", "zh", "x", "c"))
-    with jax.named_scope("weight_gather"):
-        given = swap(lax.dynamic_slice_in_dim(weight, (1 - c) * 128, 128, 1), "c")
-        kept = lax.dynamic_slice_in_dim(weight, c * 128, 128, 1)
-        wide = lax.all_gather(jnp.concatenate([kept, given], axis=0), "zl", axis=1, tiled=True)
-    with jax.named_scope("cache_gather"):
-        head = (zh * X + x) * HD
-        piece = jnp.where(
+    za, zb, zq, y, zh, x, c = (lax.axis_index(name) for name in ("za", "zb", "zq", "y", "zh", "x", "c"))
+    zl = (za * ZB + zb) * ZQ + zq
+
+    def piece(step):
+        owner = (zh * ZL + zl + step + Z) % Z // ZL
+        head = (owner * X + x) * HD
+        return jnp.where(
             c == 0,
             lax.dynamic_slice_in_dim(keys, head, HD, 1),
             lax.dynamic_slice_in_dim(values, head, HD, 1),
         )
-        own = spread(piece, "zl", ZL).reshape(ZL * ROWS, HD)
-        own = spread(own, "y", Y).reshape(N_SEQ * ROWS, HD)
+
+    with jax.named_scope("cache_gather"):
+        near = [
+            piece(0),
+            along(piece(-2), lambda z, c: -2),
+            along(piece(8 * c - 4), lambda z, c: 8 * c - 4),
+            along(piece(2), lambda z, c: 2),
+        ]
+        near, weight = lax.optimization_barrier((near, weight))
+        near = jnp.concatenate(near, axis=0)
+        near = jnp.concatenate([near, swap(near, "zq")], axis=0)
+    with jax.named_scope("weight_gather"):
+        given = swap(lax.dynamic_slice_in_dim(weight, (1 - c) * HD, HD, 1), "c")
+        kept = lax.dynamic_slice_in_dim(weight, c * HD, HD, 1)
+        narrow = jnp.concatenate([kept, given], axis=0)
+        near, narrow = lax.optimization_barrier((near, narrow))
+        facing = swap(narrow, "za")
+    with jax.named_scope("cache_gather"):
+        own = spread(near, "y", Y).reshape(N_SEQ * ROWS, HD)
+        own, narrow, facing = lax.optimization_barrier((own, narrow, facing))
         other = swap(own, "c")
+    with jax.named_scope("weight_gather"):
+        wide = jnp.stack([jnp.where(za == 0, narrow, facing), jnp.where(za == 0, facing, narrow)])
+        wide = spread(wide, "y", Y)
     with jax.named_scope("attention"):
-        place = jnp.stack([zl * Y + y, c]).astype(jnp.int32)
+        place = jnp.stack([zl * Y + y, c, zh]).astype(jnp.int32)
         heads = attend(counts, order, place, queries, own, other)
+
+    def sum_x(mine, wide):
+        with jax.named_scope("rows_gather"):
+            theirs = swap(mine, "c")
+        with jax.named_scope("projection"):
+            here = jnp.reshape(zb * ZQ + zq, (1,)).astype(jnp.int32)
+            parts = project(here, mine, theirs, wide)
+        with jax.named_scope("sum_x"):
+            parts = lax.all_to_all(parts, "x", 0, 0)
+            return jnp.sum(parts.astype(jnp.float32), axis=0)
+
     with jax.named_scope("rows_gather"):
-        mine = spread(heads, "y", Y)
-        theirs = swap(mine, "c")
-    with jax.named_scope("projection"):
-        parts = project(mine, theirs, wide)
-    with jax.named_scope("sum_x"):
-        parts = lax.all_to_all(parts, "x", 0, 0)
-        total = jnp.sum(parts.astype(jnp.float32), axis=0).reshape(Y, ZH, 32, ZL * 128)
+        first, second = (jnp.stack([rows] + [quad(rows, step) for step in range(1, QUAD)]) for rows in heads)
+        first, wide = lax.optimization_barrier((first, wide))
+    away = sum_x(first, wide)
     with jax.named_scope("sum_zh"):
-        away = lax.dynamic_slice_in_dim(total, 1 - zh, 1, 1).astype(jnp.bfloat16)
-        stay = lax.dynamic_slice_in_dim(total, zh, 1, 1)
-        mixed = (stay + swap(away, "zh").astype(jnp.float32)).astype(jnp.bfloat16)
+        away, second = lax.optimization_barrier((away.astype(jnp.bfloat16), second))
+        back = swap(away, "zh")
+    stay = sum_x(second, wide)
     with jax.named_scope("columns"):
-        mixed = lax.all_to_all(mixed.reshape(Y * C, 16, ZL * 128), ("y", "c"), 0, 0)
-        mixed = mixed.reshape(Y, C, 16, ZL, 128).transpose(2, 3, 0, 1, 4)
+        mixed = (stay + back.astype(jnp.float32)).astype(jnp.bfloat16)
+        mixed = lax.all_to_all(mixed.reshape(QUAD * C, 16, ZL * HD), ("zb", "zq", "c"), 0, 0)
+        mixed = mixed.reshape(ZB, ZQ, C, 16, Y, ZA, HD).transpose(3, 5, 0, 1, 4, 2, 6)
     return mixed.reshape(16, N_SEQ * 256)
 
 
 def solution(mesh):
-    fine = Mesh(mesh.devices.reshape(ZL, Y, ZH, X, C), ("zl", "y", "zh", "x", "c"))
-    seq, tp = ("zl", "y"), ("zh", "x", "c")
+    fine = Mesh(mesh.devices.reshape(ZA, ZB, ZQ, Y, ZH, X, C), ("za", "zb", "zq", "y", "zh", "x", "c"))
+    seq, tp = ("za", "zb", "zq", "y"), ("zh", "x", "c")
     return jax.shard_map(
         body,
         mesh=fine,

time: 231 us -> 195 us (0.84)
  the two profiles are of different devices: /device:TPU:1 before, /device:TPU:10 now
where the time goes in v3:
time: 195 us; the launch traced here: 194 us
  starting transfers between devices  83 us (43%)
  waiting for transfers between devices  67.6 us (35%)
  Pallas kernels  17.2 us (9%)
  blocking collectives  17.2 us (9%)
  local copies, waits for them, and re-layouts  5.65 us (3%)
  other arithmetic  3.16 us (2%)
    ppermute x7, waiting for transfers between devices, swap(): return lax.ppermute(piece, axis, [(0, 1), (1, 0)])  44.4 us
    ppermute x7, starting transfers between devices, swap(): return lax.ppermute(piece, axis, [(0, 1), (1, 0)])  23.5 us
    ppermute x6, starting transfers between devices, quad(): lax.ppermute(piece, ('zb', 'zq'), [(i, i ^ step) for i in range(QUAD)])  20.2 us
    ppermute x3, starting transfers between devices, along(): return lax.ppermute(piece, LINE, perm)  19.7 us
    all_to_all x1, blocking collectives, body(): lax.all_to_all(mixed.reshape(QUAD * C, 16, ZL * HD), ('zb', 'zq', 'c'), 0...  17.2 us
    pallas_call x1, Pallas kernels, attend(): pl.pallas_call(attention_kernel, out_shape=jax.ShapeDtypeStruct((ZH, X, 3...  11.6 us
    ppermute x6, waiting for transfers between devices, quad(): lax.ppermute(piece, ('zb', 'zq'), [(i, i ^ step) for i in range(QUAD)])  11.3 us
    all_to_all x2, starting transfers between devices, spread(): lax.all_to_all(jnp.broadcast_to(piece[None], (count, *piece.shape)), axis...  9.84 us
  transfers between devices with their start and end apart: 20, of which 13 were waited for; matrix products, arithmetic and copies ran while one was open for 2% of the time, Pallas kernels for 6%

profile of v3, /device:TPU:10, one launch (start us, length us, event | category | flops | bytes accessed | tf_op | source)
XLA Modules:
  0.0 194.1 jit_solution(7033328428701982300)
XLA Ops:
  1.1 11.9 %collective-permute-start = (bf16[256,128]{1,0:T(8,128)(2,1)S(1)}, bf16[256,128]{1,0:T(8,128)(2,1)S(1)}, u32[]{:S(2)}, u32[]{:S(2)}) collective-permute-start(bf16[256,128]{1,0:T(8,128)(2,1)S(1)} %get-tuple-element.34), channel_id=1, source_target_pairs={{0,392},{1,393},{64,456},{65,457},{128,0},{129,1},{192,64},{193,65... | collective-permute-start | bytes 196616 | tf_op jit(solution)/shard_map/cache_gather/ppermute | solution.py:160
  13.1 5.5 %collective-permute-start.1 = (bf16[256,128]{1,0:T(8,128)(2,1)S(1)}, bf16[256,128]{1,0:T(8,128)(2,1)S(1)}, u32[]{:S(2)}, u32[]{:S(2)}) collective-permute-start(bf16[256,128]{1,0:T(8,128)(2,1)S(1)} %get-tuple-element.36), channel_id=1, source_target_pairs={{0,264},{1,257},{64,328},{65,321},{128,392},{129,385},{192,456},{1... | collective-permute-start | bytes 196616 | tf_op jit(solution)/shard_map/cache_gather/ppermute | solution.py:160
  18.5 2.3 %collective-permute-start.2 = (bf16[256,128]{1,0:T(8,128)(2,1)S(1)}, bf16[256,128]{1,0:T(8,128)(2,1)S(1)}, u32[]{:S(2)}, u32[]{:S(2)}) collective-permute-start(bf16[256,128]{1,0:T(8,128)(2,1)S(1)} %get-tuple-element.33), channel_id=1, source_target_pairs={{0,128},{1,129},{64,192},{65,193},{128,256},{129,257},{192,320},{1... | collective-permute-start | bytes 196616 | tf_op jit(solution)/shard_map/cache_gather/ppermute | solution.py:160
  20.9 2.9 %collective-permute-done.1 = bf16[256,128]{1,0:T(8,128)(2,1)S(1)} collective-permute-done((bf16[256,128]{1,0:T(8,128)(2,1)S(1)}, bf16[256,128]{1,0:T(8,128)(2,1)S(1)}, u32[]{:S(2)}, u32[]{:S(2)}) %collective-permute-start.1) | collective-permute-done | bytes 65568 | tf_op jit(solution)/shard_map/cache_gather/ppermute | solution.py:160
  23.9 3.1 %collective-permute-done.2 = bf16[256,128]{1,0:T(8,128)(2,1)S(1)} collective-permute-done((bf16[256,128]{1,0:T(8,128)(2,1)S(1)}, bf16[256,128]{1,0:T(8,128)(2,1)S(1)}, u32[]{:S(2)}, u32[]{:S(2)}) %collective-permute-start.2) | collective-permute-done | bytes 65568 | tf_op jit(solution)/shard_map/cache_gather/ppermute | solution.py:160
  27.0 3.5 %collective-permute-start.3 = (bf16[1024,128]{1,0:T(8,128)(2,1)S(1)}, bf16[1024,128]{1,0:T(8,128)(2,1)S(1)}, u32[]{:S(2)}, u32[]{:S(2)}) collective-permute-start(bf16[1024,128]{1,0:T(8,128)(2,1)S(1)} %pad_maximum_fusion.3), channel_id=1, source_target_pairs={{0,64},{64,0},{1,65},{65,1},{2,66},{66,2},{3,67},{67,3},{4,68},{68... | collective-permute-start | bytes 786440 | tf_op jit(solution)/shard_map/cache_gather/ppermute | solution.py:148
  31.5 1.9 collective-permute-start.4
  36.9 4.9 %all-to-all-start = ((bf16[4,2048,128]{2,1,0:T(8,128)(2,1)}), bf16[4,2048,128]{2,1,0:T(8,128)(2,1)}, u32[]{:S(2)}, u32[]{:S(2)}) async-start(bf16[4,2048,128]{2,1,0:T(8,128)(2,1)} %broadcast_in_dim.4), calls=%async_computation | async-start | bytes 4194304 | tf_op jit(solution)/shard_map/cache_gather/all_to_all | solution.py:144
  41.8 4.3 %collective-permute-start.5 = (bf16[1024,128]{1,0:T(8,128)(2,1)S(1)}, bf16[1024,128]{1,0:T(8,128)(2,1)S(1)}, u32[]{:S(2)}, u32[]{:S(2)}) collective-permute-start(bf16[1024,128]{1,0:T(8,128)(2,1)S(1)} %pad_maximum_fusion.4), channel_id=1, source_target_pairs={{0,256},{256,0},{1,257},{257,1},{2,258},{258,2},{3,259},{259,3},{4... | collective-permute-start | bytes 786440 | tf_op jit(solution)/shard_map/weight_gather/ppermute | solution.py:148
  46.1 24.5 %collective-permute-done.5 = bf16[1024,128]{1,0:T(8,128)(2,1)S(1)} collective-permute-done((bf16[1024,128]{1,0:T(8,128)(2,1)S(1)}, bf16[1024,128]{1,0:T(8,128)(2,1)S(1)}, u32[]{:S(2)}, u32[]{:S(2)}) %collective-permute-start.5) | collective-permute-done | bytes 262176 | tf_op jit(solution)/shard_map/weight_gather/ppermute | solution.py:148
  70.6 1.9 collective-permute-start.6
  74.2 4.9 %all-to-all-start.1 = ((bf16[4,2,1024,128]{3,2,1,0:T(8,128)(2,1)}), bf16[4,2,1024,128]{3,2,1,0:T(8,128)(2,1)S(1)}, u32[]{:S(2)}, u32[]{:S(2)}) async-start(bf16[4,2,1024,128]{3,2,1,0:T(8,128)(2,1)} %broadcast_in_dim.5), calls=%async_computation.1 | async-start | bytes 4194304 | tf_op jit(solution)/shard_map/weight_gather/all_to_all | solution.py:144
  79.3 11.6 %attention.1 = bf16[2,4,32,512]{3,2,1,0:T(8,128)(2,1)S(1)} custom-call(s32[32]{0:T(128)S(1)} %copy-done.1, s32[64]{0:T(128)S(1)} %copy-done.2, s32[3]{0:T(128)S(1)} %pad_add_fusion.place, bf16[256,512]{1,0:T(8,128)(2,1)S(1)} %copy-done, bf16[8192,128]{1,0:T(8,128)(2,1)} %bitcast.4.own_ref, bf16[8192,128]{1,0:T(8,128)(2,1)} %collective-permute-done.6.other_ref), custom_call_target="tpu_custom_call" | custom-call | tf_op jit(solution)/shard_map/attention/pallas_call | solution.py:111
  90.9 1.9 collective-permute-start.9
  92.9 1.9 collective-permute-start.8
  94.8 6.3 %collective-permute-start.7 = (bf16[4,32,512]{2,1,0:T(8,128)(2,1)S(1)}, bf16[4,32,512]{2,1,0:T(8,128)(2,1)S(1)}, u32[]{:S(2)}, u32[]{:S(2)}) collective-permute-start(bf16[4,32,512]{2,1,0:T(8,128)(2,1)S(1)} %get-tuple-element.40), channel_id=1, source_target_pairs={{0,64},{64,0},{128,192},{192,128},{1,65},{65,1},{129,193},{193,129... | collective-permute-start | bytes 393224 | tf_op jit(solution)/shard_map/rows_gather/ppermute | solution.py:152
  101.1 4.6 %collective-permute-done.8 = bf16[4,32,512]{2,1,0:T(8,128)(2,1)S(1)} collective-permute-done((bf16[4,32,512]{2,1,0:T(8,128)(2,1)S(1)}, bf16[4,32,512]{2,1,0:T(8,128)(2,1)S(1)}, u32[]{:S(2)}, u32[]{:S(2)}) %collective-permute-start.8) | collective-permute-done | bytes 131104 | tf_op jit(solution)/shard_map/rows_gather/ppermute | solution.py:152
  106.9 1.9 collective-permute-start.10
  110.7 2.8 %projection.2 = bf16[4,4,32,1024]{3,2,1,0:T(8,128)(2,1)} custom-call(s32[1]{0:T(128)} %bitcast.me, bf16[4,4,32,512]{3,2,1,0:T(8,128)(2,1)S(1)} %pad_maximum_fusion.a_ref, bf16[4,4,32,512]{3,2,1,0:T(8,128)(2,1)S(1)} %collective-permute-done.10.b_ref, bf16[4,2,1024,128]{3,2,1,0:T(8,128)(2,1)S(1)} %all-to-all-done.1.w_ref), custom_call_target="tpu_custom_call" | custom-call | tf_op jit(solution)/shard_map/projection/pallas_call | solution.py:133
  113.5 4.9 %all-to-all-start.2 = ((bf16[4,4,32,1024]{3,2,1,0:T(8,128)(2,1)}), bf16[4,4,32,1024]{3,2,1,0:T(8,128)(2,1)}, u32[]{:S(2)}, u32[]{:S(2)}) async-start(bf16[4,4,32,1024]{3,2,1,0:T(8,128)(2,1)} %projection.2), calls=%async_computation.2 | async-start | bytes 2097152 | tf_op jit(solution)/shard_map/sum_x/all_to_all | solution.py:210
  118.4 3.4 %collective-permute-start.13 = (bf16[4,32,512]{2,1,0:T(8,128)(2,1)S(1)}, bf16[4,32,512]{2,1,0:T(8,128)(2,1)S(1)}, u32[]{:S(2)}, u32[]{:S(2)}) collective-permute-start(bf16[4,32,512]{2,1,0:T(8,128)(2,1)S(1)} %get-tuple-element.41), channel_id=1, source_target_pairs={{0,192},{64,128},{128,64},{192,0},{1,193},{65,129},{129,65},{193,1... | collective-permute-start | bytes 393224 | tf_op jit(solution)/shard_map/rows_gather/ppermute | solution.py:152
  121.7 1.9 collective-permute-start.12
  123.7 4.8 %collective-permute-start.11 = (bf16[4,32,512]{2,1,0:T(8,128)(2,1)S(1)}, bf16[4,32,512]{2,1,0:T(8,128)(2,1)S(1)}, u32[]{:S(2)}, u32[]{:S(2)}) collective-permute-start(bf16[4,32,512]{2,1,0:T(8,128)(2,1)S(1)} %get-tuple-element.41), channel_id=1, source_target_pairs={{0,64},{64,0},{128,192},{192,128},{1,65},{65,1},{129,193},{193,129... | collective-permute-start | bytes 393224 | tf_op jit(solution)/shard_map/rows_gather/ppermute | solution.py:152
  128.5 4.4 %collective-permute-done.12 = bf16[4,32,512]{2,1,0:T(8,128)(2,1)S(1)} collective-permute-done((bf16[4,32,512]{2,1,0:T(8,128)(2,1)S(1)}, bf16[4,32,512]{2,1,0:T(8,128)(2,1)S(1)}, u32[]{:S(2)}, u32[]{:S(2)}) %collective-permute-start.12) | collective-permute-done | bytes 131104 | tf_op jit(solution)/shard_map/rows_gather/ppermute | solution.py:152
  135.6 1.9 collective-permute-start.14
  137.5 1.9 collective-permute-done.14.b_ref
  139.4 2.8 %projection.3 = bf16[4,4,32,1024]{3,2,1,0:T(8,128)(2,1)} custom-call(s32[1]{0:T(128)} %bitcast.me, bf16[4,4,32,512]{3,2,1,0:T(8,128)(2,1)S(1)} %pad_maximum_fusion.2.a_ref, bf16[4,4,32,512]{3,2,1,0:T(8,128)(2,1)S(1)} %collective-permute-done.14.b_ref, bf16[4,2,1024,128]{3,2,1,0:T(8,128)(2,1)S(1)} %all-to-all-done.1.w_ref), custom_call_target="tpu_custom_call" | custom-call | tf_op jit(solution)/shard_map/projection/pallas_call | solution.py:133
  142.2 4.8 %all-to-all-start.3 = ((bf16[4,4,32,1024]{3,2,1,0:T(8,128)(2,1)}), bf16[4,4,32,1024]{3,2,1,0:T(8,128)(2,1)S(1)}, u32[]{:S(2)}, u32[]{:S(2)}) async-start(bf16[4,4,32,1024]{3,2,1,0:T(8,128)(2,1)} %projection.3), calls=%async_computation.3 | async-start | bytes 2097152 | tf_op jit(solution)/shard_map/sum_x/all_to_all | solution.py:210
  147.0 8.0 %collective-permute-start.15 = (bf16[4,32,1024]{2,1,0:T(8,128)(2,1)S(1)}, bf16[4,32,1024]{2,1,0:T(8,128)(2,1)S(1)}, u32[]{:S(2)}, u32[]{:S(2)}) collective-permute-start(bf16[4,32,1024]{2,1,0:T(8,128)(2,1)S(1)} %reduce_sum.21), channel_id=1, source_target_pairs={{0,8},{8,0},{1,9},{9,1},{2,10},{10,2},{3,11},{11,3},{4,12},{12,4},... | collective-permute-start | bytes 786440 | tf_op jit(solution)/shard_map/sum_zh/ppermute | solution.py:148
  155.0 5.9 %all-to-all-done.3 = bf16[4,4,32,1024]{3,2,1,0:T(8,128)(2,1)S(1)} async-done(((bf16[4,4,32,1024]{3,2,1,0:T(8,128)(2,1)}), bf16[4,4,32,1024]{3,2,1,0:T(8,128)(2,1)S(1)}, u32[]{:S(2)}, u32[]{:S(2)}) %all-to-all-start.3) | async-done | bytes 1048608 | tf_op jit(solution)/shard_map/sum_x/all_to_all | solution.py:210
  161.1 14.4 %collective-permute-done.15 = bf16[4,32,1024]{2,1,0:T(8,128)(2,1)S(1)} collective-permute-done((bf16[4,32,1024]{2,1,0:T(8,128)(2,1)S(1)}, bf16[4,32,1024]{2,1,0:T(8,128)(2,1)S(1)}, u32[]{:S(2)}, u32[]{:S(2)}) %collective-permute-start.15) | collective-permute-done | bytes 262176 | tf_op jit(solution)/shard_map/sum_zh/ppermute | solution.py:148
  175.5 17.2 %all_to_all.25 = bf16[8,16,1024]{2,1,0:T(8,128)(2,1)S(1)} all-to-all(bf16[8,16,1024]{2,1,0:T(8,128)(2,1)S(1)} %bitcast.22), channel_id=1, replica_groups=mesh['za'=2,'zb'=2,'zq'=2,'y'=4,'zh'=2,'x'=4,'c'=2] {'zb','zq','c'}, dimensions={0} | all-to-all | bytes 524288 | tf_op jit(solution)/shard_map/columns/all_to_all | solution.py:223
  (41 shorter events, 14.7 us)
Async XLA Ops:
  1.1 19.8 %collective-permute-start = (bf16[256,128]{1,0:T(8,128)(2,1)S(1)}, bf16[256,128]{1,0:T(8,128)(2,1)S(1)}, u32[]{:S(2)}, u32[]{:S(2)}) collective-permute-start(bf16[256,128]{1,0:T(8,128)(2,1)S(1)} %get-tuple-element.34), channel_id=1, source_target_pairs={{0,392},{1,393},{64,456},{65,457},{128,0},{129,1},{192,64},{193,65... | collective-permute-start | bytes 196616 | tf_op jit(solution)/shard_map/cache_gather/ppermute | solution.py:160
  13.1 10.8 %collective-permute-start.1 = (bf16[256,128]{1,0:T(8,128)(2,1)S(1)}, bf16[256,128]{1,0:T(8,128)(2,1)S(1)}, u32[]{:S(2)}, u32[]{:S(2)}) collective-permute-start(bf16[256,128]{1,0:T(8,128)(2,1)S(1)} %get-tuple-element.36), channel_id=1, source_target_pairs={{0,264},{1,257},{64,328},{65,321},{128,392},{129,385},{192,456},{1... | collective-permute-start | bytes 196616 | tf_op jit(solution)/shard_map/cache_gather/ppermute | solution.py:160
  18.5 8.4 %collective-permute-start.2 = (bf16[256,128]{1,0:T(8,128)(2,1)S(1)}, bf16[256,128]{1,0:T(8,128)(2,1)S(1)}, u32[]{:S(2)}, u32[]{:S(2)}) collective-permute-start(bf16[256,128]{1,0:T(8,128)(2,1)S(1)} %get-tuple-element.33), channel_id=1, source_target_pairs={{0,128},{1,129},{64,192},{65,193},{128,256},{129,257},{192,320},{1... | collective-permute-start | bytes 196616 | tf_op jit(solution)/shard_map/cache_gather/ppermute | solution.py:160
  27.0 8.3 %collective-permute-start.3 = (bf16[1024,128]{1,0:T(8,128)(2,1)S(1)}, bf16[1024,128]{1,0:T(8,128)(2,1)S(1)}, u32[]{:S(2)}, u32[]{:S(2)}) collective-permute-start(bf16[1024,128]{1,0:T(8,128)(2,1)S(1)} %pad_maximum_fusion.3), channel_id=1, source_target_pairs={{0,64},{64,0},{1,65},{65,1},{2,66},{66,2},{3,67},{67,3},{4,68},{68... | collective-permute-start | bytes 786440 | tf_op jit(solution)/shard_map/cache_gather/ppermute | solution.py:148
  31.5 3.2 %collective-permute-start.4 = (bf16[512,128]{1,0:T(8,128)(2,1)S(1)}, bf16[512,128]{1,0:T(8,128)(2,1)S(1)}, u32[]{:S(2)}, u32[]{:S(2)}) collective-permute-start(bf16[512,128]{1,0:T(8,128)(2,1)S(1)} %get-tuple-element.44), channel_id=1, source_target_pairs={{0,1},{1,0},{2,3},{3,2},{4,5},{5,4},{6,7},{7,6},{8,9},{9,8},{10,11... | collective-permute-start | bytes 393224 | tf_op jit(solution)/shard_map/weight_gather/ppermute | solution.py:148
  36.9 33.7 %all-to-all-start = ((bf16[4,2048,128]{2,1,0:T(8,128)(2,1)}), bf16[4,2048,128]{2,1,0:T(8,128)(2,1)}, u32[]{:S(2)}, u32[]{:S(2)}) async-start(bf16[4,2048,128]{2,1,0:T(8,128)(2,1)} %broadcast_in_dim.4), calls=%async_computation | async-start | bytes 4194304 | tf_op jit(solution)/shard_map/cache_gather/all_to_all | solution.py:144
  41.8 28.8 %collective-permute-start.5 = (bf16[1024,128]{1,0:T(8,128)(2,1)S(1)}, bf16[1024,128]{1,0:T(8,128)(2,1)S(1)}, u32[]{:S(2)}, u32[]{:S(2)}) collective-permute-start(bf16[1024,128]{1,0:T(8,128)(2,1)S(1)} %pad_maximum_fusion.4), channel_id=1, source_target_pairs={{0,256},{256,0},{1,257},{257,1},{2,258},{258,2},{3,259},{259,3},{4... | collective-permute-start | bytes 786440 | tf_op jit(solution)/shard_map/weight_gather/ppermute | solution.py:148
  70.6 8.7 %collective-permute-start.6 = (bf16[8192,128]{1,0:T(8,128)(2,1)}, bf16[8192,128]{1,0:T(8,128)(2,1)}, u32[]{:S(2)}, u32[]{:S(2)}) collective-permute-start(bf16[8192,128]{1,0:T(8,128)(2,1)} %bitcast.4.own_ref), channel_id=1, source_target_pairs={{0,1},{1,0},{2,3},{3,2},{4,5},{5,4},{6,7},{7,6},{8,9},{9,8},{10,11... | collective-permute-start | bytes 6291464 | tf_op jit(solution)/shard_map/cache_gather/ppermute | solution.py:148
  74.2 5.0 %copy-start = (bf16[256,512]{1,0:T(8,128)(2,1)S(1)}, bf16[256,512]{1,0:T(8,128)(2,1)}, u32[]{:S(2)}) copy-start(bf16[256,512]{1,0:T(8,128)(2,1)} %q_ref.1) | copy-start | bytes 786436
  74.2 5.0 %copy-start.1 = (s32[32]{0:T(128)S(1)}, s32[32]{0:T(128)}, u32[]{:S(2)}) copy-start(s32[32]{0:T(128)} %counts.1) | copy-start | bytes 388
  74.2 5.0 %copy-start.2 = (s32[64]{0:T(128)S(1)}, s32[64]{0:T(128)}, u32[]{:S(2)}) copy-start(s32[64]{0:T(128)} %order.1) | copy-start | bytes 772
  74.2 32.6 %all-to-all-start.1 = ((bf16[4,2,1024,128]{3,2,1,0:T(8,128)(2,1)}), bf16[4,2,1024,128]{3,2,1,0:T(8,128)(2,1)S(1)}, u32[]{:S(2)}, u32[]{:S(2)}) async-start(bf16[4,2,1024,128]{3,2,1,0:T(8,128)(2,1)} %broadcast_in_dim.5), calls=%async_computation.1 | async-start | bytes 4194304 | tf_op jit(solution)/shard_map/weight_gather/all_to_all | solution.py:144
  90.9 10.1 %collective-permute-start.9 = (bf16[4,32,512]{2,1,0:T(8,128)(2,1)S(1)}, bf16[4,32,512]{2,1,0:T(8,128)(2,1)S(1)}, u32[]{:S(2)}, u32[]{:S(2)}) collective-permute-start(bf16[4,32,512]{2,1,0:T(8,128)(2,1)S(1)} %get-tuple-element.40), channel_id=1, source_target_pairs={{0,192},{64,128},{128,64},{192,0},{1,193},{65,129},{129,65},{193,1... | collective-permute-start | bytes 393224 | tf_op jit(solution)/shard_map/rows_gather/ppermute | solution.py:152
  92.9 12.8 %collective-permute-start.8 = (bf16[4,32,512]{2,1,0:T(8,128)(2,1)S(1)}, bf16[4,32,512]{2,1,0:T(8,128)(2,1)S(1)}, u32[]{:S(2)}, u32[]{:S(2)}) collective-permute-start(bf16[4,32,512]{2,1,0:T(8,128)(2,1)S(1)} %get-tuple-element.40), channel_id=1, source_target_pairs={{0,128},{64,192},{128,0},{192,64},{1,129},{65,193},{129,1},{193,65... | collective-permute-start | bytes 393224 | tf_op jit(solution)/shard_map/rows_gather/ppermute | solution.py:152
  94.8 12.0 %collective-permute-start.7 = (bf16[4,32,512]{2,1,0:T(8,128)(2,1)S(1)}, bf16[4,32,512]{2,1,0:T(8,128)(2,1)S(1)}, u32[]{:S(2)}, u32[]{:S(2)}) collective-permute-start(bf16[4,32,512]{2,1,0:T(8,128)(2,1)S(1)} %get-tuple-element.40), channel_id=1, source_target_pairs={{0,64},{64,0},{128,192},{192,128},{1,65},{65,1},{129,193},{193,129... | collective-permute-start | bytes 393224 | tf_op jit(solution)/shard_map/rows_gather/ppermute | solution.py:152
  106.9 3.8 %collective-permute-start.10 = (bf16[4,4,32,512]{3,2,1,0:T(8,128)(2,1)S(1)}, bf16[4,4,32,512]{3,2,1,0:T(8,128)(2,1)S(1)}, u32[]{:S(2)}, u32[]{:S(2)}) collective-permute-start(bf16[4,4,32,512]{3,2,1,0:T(8,128)(2,1)S(1)} %pad_maximum_fusion.a_ref), channel_id=1, source_target_pairs={{0,1},{1,0},{2,3},{3,2},{4,5},{5,4},{6,7},{7,6},{8,9},{9,8},{10,11... | collective-permute-start | bytes 1572872 | tf_op jit(solution)/shard_map/rows_gather/ppermute | solution.py:148
  113.5 20.7 %all-to-all-start.2 = ((bf16[4,4,32,1024]{3,2,1,0:T(8,128)(2,1)}), bf16[4,4,32,1024]{3,2,1,0:T(8,128)(2,1)}, u32[]{:S(2)}, u32[]{:S(2)}) async-start(bf16[4,4,32,1024]{3,2,1,0:T(8,128)(2,1)} %projection.2), calls=%async_computation.2 | async-start | bytes 2097152 | tf_op jit(solution)/shard_map/sum_x/all_to_all | solution.py:210
  118.4 10.1 %collective-permute-start.13 = (bf16[4,32,512]{2,1,0:T(8,128)(2,1)S(1)}, bf16[4,32,512]{2,1,0:T(8,128)(2,1)S(1)}, u32[]{:S(2)}, u32[]{:S(2)}) collective-permute-start(bf16[4,32,512]{2,1,0:T(8,128)(2,1)S(1)} %get-tuple-element.41), channel_id=1, source_target_pairs={{0,192},{64,128},{128,64},{192,0},{1,193},{65,129},{129,65},{193,1... | collective-permute-start | bytes 393224 | tf_op jit(solution)/shard_map/rows_gather/ppermute | solution.py:152
  121.7 11.2 %collective-permute-start.12 = (bf16[4,32,512]{2,1,0:T(8,128)(2,1)S(1)}, bf16[4,32,512]{2,1,0:T(8,128)(2,1)S(1)}, u32[]{:S(2)}, u32[]{:S(2)}) collective-permute-start(bf16[4,32,512]{2,1,0:T(8,128)(2,1)S(1)} %get-tuple-element.41), channel_id=1, source_target_pairs={{0,128},{64,192},{128,0},{192,64},{1,129},{65,193},{129,1},{193,65... | collective-permute-start | bytes 393224 | tf_op jit(solution)/shard_map/rows_gather/ppermute | solution.py:152
  123.7 10.4 %collective-permute-start.11 = (bf16[4,32,512]{2,1,0:T(8,128)(2,1)S(1)}, bf16[4,32,512]{2,1,0:T(8,128)(2,1)S(1)}, u32[]{:S(2)}, u32[]{:S(2)}) collective-permute-start(bf16[4,32,512]{2,1,0:T(8,128)(2,1)S(1)} %get-tuple-element.41), channel_id=1, source_target_pairs={{0,64},{64,0},{128,192},{192,128},{1,65},{65,1},{129,193},{193,129... | collective-permute-start | bytes 393224 | tf_op jit(solution)/shard_map/rows_gather/ppermute | solution.py:152
  135.6 3.8 %collective-permute-start.14 = (bf16[4,4,32,512]{3,2,1,0:T(8,128)(2,1)S(1)}, bf16[4,4,32,512]{3,2,1,0:T(8,128)(2,1)S(1)}, u32[]{:S(2)}, u32[]{:S(2)}) collective-permute-start(bf16[4,4,32,512]{3,2,1,0:T(8,128)(2,1)S(1)} %pad_maximum_fusion.2.a_ref), channel_id=1, source_target_pairs={{0,1},{1,0},{2,3},{3,2},{4,5},{5,4},{6,7},{7,6},{8,9},{9,8},{10,11... | collective-permute-start | bytes 1572872 | tf_op jit(solution)/shard_map/rows_gather/ppermute | solution.py:148
  142.2 18.7 %all-to-all-start.3 = ((bf16[4,4,32,1024]{3,2,1,0:T(8,128)(2,1)}), bf16[4,4,32,1024]{3,2,1,0:T(8,128)(2,1)S(1)}, u32[]{:S(2)}, u32[]{:S(2)}) async-start(bf16[4,4,32,1024]{3,2,1,0:T(8,128)(2,1)} %projection.3), calls=%async_computation.3 | async-start | bytes 2097152 | tf_op jit(solution)/shard_map/sum_x/all_to_all | solution.py:210
  147.0 28.5 %collective-permute-start.15 = (bf16[4,32,1024]{2,1,0:T(8,128)(2,1)S(1)}, bf16[4,32,1024]{2,1,0:T(8,128)(2,1)S(1)}, u32[]{:S(2)}, u32[]{:S(2)}) collective-permute-start(bf16[4,32,1024]{2,1,0:T(8,128)(2,1)S(1)} %reduce_sum.21), channel_id=1, source_target_pairs={{0,8},{8,0},{1,9},{9,1},{2,10},{10,2},{3,11},{11,3},{4,12},{12,4},... | collective-permute-start | bytes 786440 | tf_op jit(solution)/shard_map/sum_zh/ppermute | solution.py:148

commit v4 on v3

--- a/solution.py
+++ b/solution.py
@@ -1,3 +1,5 @@
+import math
+
 import jax
 import jax.numpy as jnp
 from jax import lax
@@ -16,8 +18,8 @@
 LINE = ("za", "zb", "zq", "zh", "c")
 N_SEQ = ZL * Y
 ROWS = SLOTS * PAGE
-CHUNK = 512
-SCALE = HD**-0.5
+CHUNK = 2048
+SCALE = HD**-0.5 * math.log2(math.e)
 
 
 def attention_kernel(counts, order, place, q_ref, own_ref, other_ref, o_ref, k_sc, v_sc):
@@ -27,24 +29,20 @@
     my_z = me // Y
 
     def sort_pages(k_ref, v_ref):
-        def one(d, rank):
-            held = counts[d]
+        def one(rank, at):
+            d, j = at
             z = d // Y
             far = (z + my_z) % 2
             near = my_z + far * (1 - 2 * (my_z % 2))
-            base = ((d % Y) * ZL + far * (ZL // 2) + (z - near + ZL) % ZL // 2) * ROWS
-            for j in range(SLOTS):
-
-                @pl.when(j < held)
-                def _():
-                    to = pl.multiple_of(order[rank + j] * PAGE, PAGE)
-                    at = pl.multiple_of(base + j * PAGE, PAGE)
-                    k_sc[pl.ds(to, PAGE), :] = k_ref[pl.ds(at, PAGE), :]
-                    v_sc[pl.ds(to, PAGE), :] = v_ref[pl.ds(at, PAGE), :]
-
-            return rank + held
-
-        lax.fori_loop(0, N_SEQ, one, jnp.int32(0))
+            base = (d % Y) * ZL + far * (ZL // 2) + (z - near + ZL) % ZL // 2
+            src = pl.multiple_of(base * ROWS + j * PAGE, PAGE)
+            to = pl.multiple_of(order[rank] * PAGE, PAGE)
+            k_sc[pl.ds(to, PAGE), :] = k_ref[pl.ds(src, PAGE), :]
+            v_sc[pl.ds(to, PAGE), :] = v_ref[pl.ds(src, PAGE), :]
+            last = j + 1 >= counts[d]
+            return jnp.where(last, jnp.minimum(d + 1, N_SEQ - 1), d), jnp.where(last, 0, j + 1)
+
+        lax.fori_loop(0, PAGES, one, (jnp.int32(0), jnp.int32(0)), unroll=4)
 
     @pl.when(core == 0)
     def _():
@@ -68,36 +66,57 @@
         @pl.when(j < live)
         def _():
             page = order[before + j]
-            q = jnp.concatenate(
-                [q_ref[j * PAGE : (j + 1) * PAGE, h * HD : (h + 1) * HD] for h in range(HEADS)], axis=0
-            )
-
-            def step(i, state, last):
-                best, total, accum = state
-                at = pl.multiple_of(i * CHUNK, CHUNK)
+            groups = 1
+            count = HEADS // groups
+            q = [
+                jnp.concatenate(
+                    [q_ref[j * PAGE : (j + 1) * PAGE, h * HD : (h + 1) * HD] for h in range(g * count, (g + 1) * count)],
+                    axis=0,
+                )
+                for g in range(groups)
+            ]
+            size = count * PAGE
+
+            def step(at, state, last, CHUNK):
                 k = k_sc[pl.ds(at, CHUNK), :]
                 v = v_sc[pl.ds(at, CHUNK), :]
-                s = lax.dot_general(q, k, (((1,), (1,)), ((), ())), preferred_element_type=jnp.float32)
                 if last:
-                    row = lax.broadcasted_iota(jnp.int32, s.shape, 0) % PAGE + page * PAGE
-                    col = lax.broadcasted_iota(jnp.int32, s.shape, 1) + at
-                    s = jnp.where(col <= row, s, jnp.float32(-1e30))
-                new = jnp.maximum(best, jnp.max(s, axis=1, keepdims=True))
-                p = jnp.exp((s - new) * SCALE)
-                fade = jnp.exp((best - new) * SCALE)
-                total = total * fade + jnp.sum(p, axis=1, keepdims=True)
-                accum = accum * fade + jnp.dot(p.astype(jnp.bfloat16), v, preferred_element_type=jnp.float32)
-                return new, total, accum
-
-            state = (
-                jnp.full((HEADS * PAGE, 1), -1e30, jnp.float32),
-                jnp.zeros((HEADS * PAGE, 1), jnp.float32),
-                jnp.zeros((HEADS * PAGE, HD), jnp.float32),
+                    row = lax.broadcasted_iota(jnp.int32, (size, CHUNK), 0) % PAGE + page * PAGE
+                    seen = lax.broadcasted_iota(jnp.int32, (size, CHUNK), 1) + at <= row
+                out = []
+                for g in range(groups):
+                    best, total, accum = state[g]
+                    s = lax.dot_general(q[g], k, (((1,), (1,)), ((), ())), preferred_element_type=jnp.float32)
+                    if last:
+                        s = jnp.where(seen, s, jnp.float32(-1e30))
+                    new = jnp.maximum(best, jnp.max(s, axis=1, keepdims=True))
+                    p = jnp.exp2((s - new) * SCALE)
+                    fade = jnp.exp2((best - new) * SCALE)
+                    total = total * fade + jnp.sum(p, axis=1, keepdims=True)
+                    accum = accum * fade + jnp.dot(p.astype(jnp.bfloat16), v, preferred_element_type=jnp.float32)
+                    out.append((new, total, accum))
+                return tuple(out)
+
+            state = tuple(
+                (
+                    jnp.full((size, 1), -1e30, jnp.float32),
+                    jnp.zeros((size, 1), jnp.float32),
+                    jnp.zeros((size, HD), jnp.float32),
+                )
+                for _ in range(groups)
             )
             full = page // (CHUNK // PAGE)
-            state = lax.fori_loop(0, full, lambda i, s: step(i, s, False), state)
-            _, total, accum = step(full, state, True)
-            out = (accum / total).astype(jnp.bfloat16)
+            state = lax.fori_loop(
+                0, full, lambda i, s: step(pl.multiple_of(i * CHUNK, CHUNK), s, False, CHUNK), state
+            )
+            rest = pl.multiple_of(full * CHUNK, CHUNK)
+            state = lax.cond(
+                page % (CHUNK // PAGE) < CHUNK // PAGE // 2,
+                lambda s: step(rest, s, True, CHUNK // 2),
+                lambda s: step(rest, s, True, CHUNK),
+                state,
+            )
+            out = jnp.concatenate([(accum / total).astype(jnp.bfloat16) for _, total, accum in state], axis=0)
             store(j, lambda h, b: out[h * PAGE + b * 32 : h * PAGE + b * 32 + 32, :])
 
         @pl.when(j >= live)
@@ -150,6 +169,10 @@
 
 def quad(piece, step):
     return lax.ppermute(piece, ("zb", "zq"), [(i, i ^ step) for i in range(QUAD)])
+
+
+def around(piece, axis, count, shift):
+    return lax.ppermute(piece, axis, [((i + shift) % count, i) for i in range(count)])
 
 
 def along(piece, step):
@@ -200,24 +223,32 @@
         place = jnp.stack([zl * Y + y, c, zh]).astype(jnp.int32)
         heads = attend(counts, order, place, queries, own, other)
 
-    def sum_x(mine, wide):
+    def projected(mine):
         with jax.named_scope("rows_gather"):
             theirs = swap(mine, "c")
         with jax.named_scope("projection"):
             here = jnp.reshape(zb * ZQ + zq, (1,)).astype(jnp.int32)
-            parts = project(here, mine, theirs, wide)
-        with jax.named_scope("sum_x"):
-            parts = lax.all_to_all(parts, "x", 0, 0)
-            return jnp.sum(parts.astype(jnp.float32), axis=0)
+            return project(here, mine, theirs, wide)
+
+    def part_of(parts, shift):
+        return lax.dynamic_index_in_dim(parts, (x + shift) % X, 0, keepdims=False)
 
     with jax.named_scope("rows_gather"):
         first, second = (jnp.stack([rows] + [quad(rows, step) for step in range(1, QUAD)]) for rows in heads)
         first, wide = lax.optimization_barrier((first, wide))
-    away = sum_x(first, wide)
+    parts = projected(first)
+    with jax.named_scope("sum_x"):
+        away = lax.all_to_all(parts, "x", 0, 0)
+        away = jnp.sum(away.astype(jnp.float32), axis=0).astype(jnp.bfloat16)
+        away, second = lax.optimization_barrier((away, second))
     with jax.named_scope("sum_zh"):
-        away, second = lax.optimization_barrier((away.astype(jnp.bfloat16), second))
-        back = swap(away, "zh")
-    stay = sum_x(second, wide)
+        back = spread(away, "zh", ZH)
+        back = lax.dynamic_index_in_dim(back, 1 - zh, 0, keepdims=False)
+    parts = projected(second)
+    with jax.named_scope("sum_x"):
+        stay = part_of(parts, 0).astype(jnp.float32)
+        for shift in range(1, X):
+            stay += around(part_of(parts, X - shift), "x", X, shift).astype(jnp.float32)
     with jax.named_scope("columns"):
         mixed = (stay + back.astype(jnp.float32)).astype(jnp.bfloat16)
         mixed = lax.all_to_all(mixed.reshape(QUAD * C, 16, ZL * HD), ("zb", "zq", "c"), 0, 0)

time: 195 us -> 189 us (0.969)
  the two profiles are of different devices: /device:TPU:10 before, /device:TPU:1 now
where the time goes in v4:
time: 189 us; the launch traced here: 188 us
  starting transfers between devices  88.1 us (47%)
  waiting for transfers between devices  58.9 us (31%)
  blocking collectives  14.5 us (8%)
  Pallas kernels  11.9 us (6%)
  local copies, waits for them, and re-layouts  9.51 us (5%)
  other arithmetic  4.38 us (2%)
    ppermute x6, waiting for transfers between devices, swap(): return lax.ppermute(piece, axis, [(0, 1), (1, 0)])  29.4 us
    ppermute x6, starting transfers between devices, swap(): return lax.ppermute(piece, axis, [(0, 1), (1, 0)])  22.5 us
    ppermute x6, starting transfers between devices, quad(): lax.ppermute(piece, ('zb', 'zq'), [(i, i ^ step) for i in range(QUAD)])  18.5 us
    ppermute x3, starting transfers between devices, along(): return lax.ppermute(piece, LINE, perm)  16.4 us
    all_to_all x3, starting transfers between devices, spread(): lax.all_to_all(jnp.broadcast_to(piece[None], (count, *piece.shape)), axis...  15.8 us
    all_to_all x1, blocking collectives, body(): lax.all_to_all(mixed.reshape(QUAD * C, 16, ZL * HD), ('zb', 'zq', 'c'), 0...  14.5 us
    ppermute x6, waiting for transfers between devices, quad(): lax.ppermute(piece, ('zb', 'zq'), [(i, i ^ step) for i in range(QUAD)])  11.6 us
    ppermute x3, starting transfers between devices, around(): lax.ppermute(piece, axis, [((i + shift) % count, i) for i in range(count)])  10.7 us
  transfers between devices with their start and end apart: 22, of which 12 were waited for; matrix products, arithmetic and copies ran while one was open for 2% of the time, Pallas kernels for 5%

profile of v4, /device:TPU:1, one launch (start us, length us, event | category | flops | bytes accessed | tf_op | source)
XLA Modules:
  0.0 187.8 jit_solution(17831482209174420326)
XLA Ops:
  1.3 12.3 %collective-permute-start = (bf16[256,128]{1,0:T(8,128)(2,1)S(1)}, bf16[256,128]{1,0:T(8,128)(2,1)S(1)}, u32[]{:S(2)}, u32[]{:S(2)}) collective-permute-start(bf16[256,128]{1,0:T(8,128)(2,1)S(1)} %get-tuple-element.37), channel_id=1, source_target_pairs={{0,392},{1,393},{64,456},{65,457},{128,0},{129,1},{192,64},{193,65... | collective-permute-start | bytes 196616 | tf_op jit(solution)/shard_map/cache_gather/ppermute | solution.py:183
  13.6 1.9 %collective-permute-start.1 = (bf16[256,128]{1,0:T(8,128)(2,1)S(1)}, bf16[256,128]{1,0:T(8,128)(2,1)S(1)}, u32[]{:S(2)}, u32[]{:S(2)}) collective-permute-start(bf16[256,128]{1,0:T(8,128)(2,1)S(1)} %get-tuple-element.39), channel_id=1, source_target_pairs={{0,264},{1,257},{64,328},{65,321},{128,392},{129,385},{192,456},{1... | collective-permute-start | bytes 196616 | tf_op jit(solution)/shard_map/cache_gather/ppermute | solution.py:183
  15.5 2.1 %collective-permute-start.2 = (bf16[256,128]{1,0:T(8,128)(2,1)S(1)}, bf16[256,128]{1,0:T(8,128)(2,1)S(1)}, u32[]{:S(2)}, u32[]{:S(2)}) collective-permute-start(bf16[256,128]{1,0:T(8,128)(2,1)S(1)} %get-tuple-element.36), channel_id=1, source_target_pairs={{0,128},{1,129},{64,192},{65,193},{128,256},{129,257},{192,320},{1... | collective-permute-start | bytes 196616 | tf_op jit(solution)/shard_map/cache_gather/ppermute | solution.py:183
  17.7 6.6 %collective-permute-done.1 = bf16[256,128]{1,0:T(8,128)(2,1)S(1)} collective-permute-done((bf16[256,128]{1,0:T(8,128)(2,1)S(1)}, bf16[256,128]{1,0:T(8,128)(2,1)S(1)}, u32[]{:S(2)}, u32[]{:S(2)}) %collective-permute-start.1) | collective-permute-done | bytes 65568 | tf_op jit(solution)/shard_map/cache_gather/ppermute | solution.py:183
  24.3 3.6 %collective-permute-start.3 = (bf16[1024,128]{1,0:T(8,128)(2,1)S(1)}, bf16[1024,128]{1,0:T(8,128)(2,1)S(1)}, u32[]{:S(2)}, u32[]{:S(2)}) collective-permute-start(bf16[1024,128]{1,0:T(8,128)(2,1)S(1)} %pad_maximum_fusion.3), channel_id=1, source_target_pairs={{0,64},{64,0},{1,65},{65,1},{2,66},{66,2},{3,67},{67,3},{4,68},{68... | collective-permute-start | bytes 786440 | tf_op jit(solution)/shard_map/cache_gather/ppermute | solution.py:167
  28.9 5.9 %collective-permute-start.4 = (bf16[512,128]{1,0:T(8,128)(2,1)S(1)}, bf16[512,128]{1,0:T(8,128)(2,1)S(1)}, u32[]{:S(2)}, u32[]{:S(2)}) collective-permute-start(bf16[512,128]{1,0:T(8,128)(2,1)S(1)} %get-tuple-element.47), channel_id=1, source_target_pairs={{0,1},{1,0},{2,3},{3,2},{4,5},{5,4},{6,7},{7,6},{8,9},{9,8},{10,11... | collective-permute-start | bytes 393224 | tf_op jit(solution)/shard_map/weight_gather/ppermute | solution.py:167
  37.5 4.4 %all-to-all-start = ((bf16[4,2048,128]{2,1,0:T(8,128)(2,1)}), bf16[4,2048,128]{2,1,0:T(8,128)(2,1)}, u32[]{:S(2)}, u32[]{:S(2)}) async-start(bf16[4,2048,128]{2,1,0:T(8,128)(2,1)} %broadcast_in_dim.6), calls=%async_computation | async-start | bytes 4194304 | tf_op jit(solution)/shard_map/cache_gather/all_to_all | solution.py:163
  41.9 4.0 %collective-permute-start.5 = (bf16[1024,128]{1,0:T(8,128)(2,1)S(1)}, bf16[1024,128]{1,0:T(8,128)(2,1)S(1)}, u32[]{:S(2)}, u32[]{:S(2)}) collective-permute-start(bf16[1024,128]{1,0:T(8,128)(2,1)S(1)} %pad_maximum_fusion.4), channel_id=1, source_target_pairs={{0,256},{256,0},{1,257},{257,1},{2,258},{258,2},{3,259},{259,3},{4... | collective-permute-start | bytes 786440 | tf_op jit(solution)/shard_map/weight_gather/ppermute | solution.py:167
  45.9 25.5 %collective-permute-done.5 = bf16[1024,128]{1,0:T(8,128)(2,1)S(1)} collective-permute-done((bf16[1024,128]{1,0:T(8,128)(2,1)S(1)}, bf16[1024,128]{1,0:T(8,128)(2,1)S(1)}, u32[]{:S(2)}, u32[]{:S(2)}) %collective-permute-start.5) | collective-permute-done | bytes 262176 | tf_op jit(solution)/shard_map/weight_gather/ppermute | solution.py:167
  71.4 2.4 %collective-permute-start.6 = (bf16[8192,128]{1,0:T(8,128)(2,1)}, bf16[8192,128]{1,0:T(8,128)(2,1)}, u32[]{:S(2)}, u32[]{:S(2)}) collective-permute-start(bf16[8192,128]{1,0:T(8,128)(2,1)} %bitcast.4.own_ref), channel_id=1, source_target_pairs={{0,1},{1,0},{2,3},{3,2},{4,5},{5,4},{6,7},{7,6},{8,9},{9,8},{10,11... | collective-permute-start | bytes 6291464 | tf_op jit(solution)/shard_map/cache_gather/ppermute | solution.py:167
  75.6 4.3 %all-to-all-start.1 = ((bf16[4,2,1024,128]{3,2,1,0:T(8,128)(2,1)}), bf16[4,2,1024,128]{3,2,1,0:T(8,128)(2,1)S(1)}, u32[]{:S(2)}, u32[]{:S(2)}) async-start(bf16[4,2,1024,128]{3,2,1,0:T(8,128)(2,1)} %broadcast_in_dim.7), calls=%async_computation.1 | async-start | bytes 4194304 | tf_op jit(solution)/shard_map/weight_gather/all_to_all | solution.py:163
  80.0 7.2 %attention.1 = bf16[2,4,32,512]{3,2,1,0:T(8,128)(2,1)S(1)} custom-call(s32[32]{0:T(128)S(1)} %copy-done.5, s32[64]{0:T(128)S(1)} %copy-done.6, s32[3]{0:T(128)S(1)} %pad_add_fusion.place, bf16[256,512]{1,0:T(8,128)(2,1)S(1)} %copy-done.4, bf16[8192,128]{1,0:T(8,128)(2,1)} %bitcast.4.own_ref, bf16[8192,128]{1,0:T(8,128)(2,1)} %collective-permute-done.6.other_ref), custom_call_target="tpu_custom_call" | custom-call | tf_op jit(solution)/shard_map/attention/pallas_call | solution.py:130
  87.2 1.9 %collective-permute-start.9 = (bf16[4,32,512]{2,1,0:T(8,128)(2,1)S(1)}, bf16[4,32,512]{2,1,0:T(8,128)(2,1)S(1)}, u32[]{:S(2)}, u32[]{:S(2)}) collective-permute-start(bf16[4,32,512]{2,1,0:T(8,128)(2,1)S(1)} %get-tuple-element.43), channel_id=1, source_target_pairs={{0,192},{64,128},{128,64},{192,0},{1,193},{65,129},{129,65},{193,1... | collective-permute-start | bytes 393224 | tf_op jit(solution)/shard_map/rows_gather/ppermute | solution.py:171
  89.1 1.9 %collective-permute-start.8 = (bf16[4,32,512]{2,1,0:T(8,128)(2,1)S(1)}, bf16[4,32,512]{2,1,0:T(8,128)(2,1)S(1)}, u32[]{:S(2)}, u32[]{:S(2)}) collective-permute-start(bf16[4,32,512]{2,1,0:T(8,128)(2,1)S(1)} %get-tuple-element.43), channel_id=1, source_target_pairs={{0,128},{64,192},{128,0},{192,64},{1,129},{65,193},{129,1},{193,65... | collective-permute-start | bytes 393224 | tf_op jit(solution)/shard_map/rows_gather/ppermute | solution.py:171
  91.1 5.4 %collective-permute-start.7 = (bf16[4,32,512]{2,1,0:T(8,128)(2,1)S(1)}, bf16[4,32,512]{2,1,0:T(8,128)(2,1)S(1)}, u32[]{:S(2)}, u32[]{:S(2)}) collective-permute-start(bf16[4,32,512]{2,1,0:T(8,128)(2,1)S(1)} %get-tuple-element.43), channel_id=1, source_target_pairs={{0,64},{64,0},{128,192},{192,128},{1,65},{65,1},{129,193},{193,129... | collective-permute-start | bytes 393224 | tf_op jit(solution)/shard_map/rows_gather/ppermute | solution.py:171
  96.5 5.5 %collective-permute-done.8 = bf16[4,32,512]{2,1,0:T(8,128)(2,1)S(1)} collective-permute-done((bf16[4,32,512]{2,1,0:T(8,128)(2,1)S(1)}, bf16[4,32,512]{2,1,0:T(8,128)(2,1)S(1)}, u32[]{:S(2)}, u32[]{:S(2)}) %collective-permute-start.8) | collective-permute-done | bytes 131104 | tf_op jit(solution)/shard_map/rows_gather/ppermute | solution.py:171
  102.3 3.7 %all-to-all-done.1.w_ref = bf16[4,2,1024,128]{3,2,1,0:T(8,128)(2,1)S(1)} async-done(((bf16[4,2,1024,128]{3,2,1,0:T(8,128)(2,1)}), bf16[4,2,1024,128]{3,2,1,0:T(8,128)(2,1)S(1)}, u32[]{:S(2)}, u32[]{:S(2)}) %all-to-all-start.1) | async-done | bytes 2097184 | tf_op jit(solution)/shard_map/weight_gather/all_to_all | solution.py:163
  106.1 3.0 %collective-permute-start.10 = (bf16[4,4,32,512]{3,2,1,0:T(8,128)(2,1)S(1)}, bf16[4,4,32,512]{3,2,1,0:T(8,128)(2,1)S(1)}, u32[]{:S(2)}, u32[]{:S(2)}) collective-permute-start(bf16[4,4,32,512]{3,2,1,0:T(8,128)(2,1)S(1)} %pad_maximum_fusion.a_ref), channel_id=1, source_target_pairs={{0,1},{1,0},{2,3},{3,2},{4,5},{5,4},{6,7},{7,6},{8,9},{9,8},{10,11... | collective-permute-start | bytes 1572872 | tf_op jit(solution)/shard_map/rows_gather/ppermute | solution.py:167
  110.6 2.8 %projection.2 = bf16[4,4,32,1024]{3,2,1,0:T(8,128)(2,1)} custom-call(s32[1]{0:T(128)} %bitcast.me, bf16[4,4,32,512]{3,2,1,0:T(8,128)(2,1)S(1)} %pad_maximum_fusion.a_ref, bf16[4,4,32,512]{3,2,1,0:T(8,128)(2,1)S(1)} %collective-permute-done.10.b_ref, bf16[4,2,1024,128]{3,2,1,0:T(8,128)(2,1)S(1)} %all-to-all-done.1.w_ref), custom_call_target="tpu_custom_call" | custom-call | tf_op jit(solution)/shard_map/projection/pallas_call | solution.py:152
  113.4 4.2 %all-to-all-start.2 = ((bf16[4,4,32,1024]{3,2,1,0:T(8,128)(2,1)}), bf16[4,4,32,1024]{3,2,1,0:T(8,128)(2,1)}, u32[]{:S(2)}, u32[]{:S(2)}) async-start(bf16[4,4,32,1024]{3,2,1,0:T(8,128)(2,1)} %projection.2), calls=%async_computation.2 | async-start | bytes 2097152 | tf_op jit(solution)/shard_map/sum_x/all_to_all | solution.py:241
  117.7 1.9 %collective-permute-start.13 = (bf16[4,32,512]{2,1,0:T(8,128)(2,1)S(1)}, bf16[4,32,512]{2,1,0:T(8,128)(2,1)S(1)}, u32[]{:S(2)}, u32[]{:S(2)}) collective-permute-start(bf16[4,32,512]{2,1,0:T(8,128)(2,1)S(1)} %get-tuple-element.44), channel_id=1, source_target_pairs={{0,192},{64,128},{128,64},{192,0},{1,193},{65,129},{129,65},{193,1... | collective-permute-start | bytes 393224 | tf_op jit(solution)/shard_map/rows_gather/ppermute | solution.py:171
  119.6 1.9 %collective-permute-start.12 = (bf16[4,32,512]{2,1,0:T(8,128)(2,1)S(1)}, bf16[4,32,512]{2,1,0:T(8,128)(2,1)S(1)}, u32[]{:S(2)}, u32[]{:S(2)}) collective-permute-start(bf16[4,32,512]{2,1,0:T(8,128)(2,1)S(1)} %get-tuple-element.44), channel_id=1, source_target_pairs={{0,128},{64,192},{128,0},{192,64},{1,129},{65,193},{129,1},{193,65... | collective-permute-start | bytes 393224 | tf_op jit(solution)/shard_map/rows_gather/ppermute | solution.py:171
  121.5 5.4 %collective-permute-start.11 = (bf16[4,32,512]{2,1,0:T(8,128)(2,1)S(1)}, bf16[4,32,512]{2,1,0:T(8,128)(2,1)S(1)}, u32[]{:S(2)}, u32[]{:S(2)}) collective-permute-start(bf16[4,32,512]{2,1,0:T(8,128)(2,1)S(1)} %get-tuple-element.44), channel_id=1, source_target_pairs={{0,64},{64,0},{128,192},{192,128},{1,65},{65,1},{129,193},{193,129... | collective-permute-start | bytes 393224 | tf_op jit(solution)/shard_map/rows_gather/ppermute | solution.py:171
  127.0 5.6 %collective-permute-done.12 = bf16[4,32,512]{2,1,0:T(8,128)(2,1)S(1)} collective-permute-done((bf16[4,32,512]{2,1,0:T(8,128)(2,1)S(1)}, bf16[4,32,512]{2,1,0:T(8,128)(2,1)S(1)}, u32[]{:S(2)}, u32[]{:S(2)}) %collective-permute-start.12) | collective-permute-done | bytes 131104 | tf_op jit(solution)/shard_map/rows_gather/ppermute | solution.py:171
  135.4 7.1 %all-to-all-start.3 = ((bf16[2,4,32,1024]{3,2,1,0:T(8,128)(2,1)}), bf16[2,4,32,1024]{3,2,1,0:T(8,128)(2,1)}, u32[]{:S(2)}, u32[]{:S(2)}) async-start(bf16[2,4,32,1024]{3,2,1,0:T(8,128)(2,1)} %broadcast_in_dim.8), calls=%async_computation.3 | async-start | bytes 1048576 | tf_op jit(solution)/shard_map/sum_zh/all_to_all | solution.py:163
  142.5 3.5 %collective-permute-start.14 = (bf16[4,4,32,512]{3,2,1,0:T(8,128)(2,1)S(1)}, bf16[4,4,32,512]{3,2,1,0:T(8,128)(2,1)S(1)}, u32[]{:S(2)}, u32[]{:S(2)}) collective-permute-start(bf16[4,4,32,512]{3,2,1,0:T(8,128)(2,1)S(1)} %pad_maximum_fusion.2.a_ref), channel_id=1, source_target_pairs={{0,1},{1,0},{2,3},{3,2},{4,5},{5,4},{6,7},{7,6},{8,9},{9,8},{10,11... | collective-permute-start | bytes 1572872 | tf_op jit(solution)/shard_map/rows_gather/ppermute | solution.py:167
  150.4 1.9 %projection.3 = bf16[4,4,32,1024]{3,2,1,0:T(8,128)(2,1)S(1)} custom-call(s32[1]{0:T(128)} %bitcast.me, bf16[4,4,32,512]{3,2,1,0:T(8,128)(2,1)S(1)} %copy-done.1, bf16[4,4,32,512]{3,2,1,0:T(8,128)(2,1)S(1)} %copy-done.3, bf16[4,2,1024,128]{3,2,1,0:T(8,128)(2,1)S(1)} %all-to-all-done.1.w_ref), custom_call_target="tpu_custom_call" | custom-call | tf_op jit(solution)/shard_map/projection/pallas_call | solution.py:152
  152.4 3.3 %collective-permute-start.17 = (bf16[4,32,1024]{2,1,0:T(8,128)(2,1)S(1)}, bf16[4,32,1024]{2,1,0:T(8,128)(2,1)S(1)}, u32[]{:S(2)}, u32[]{:S(2)}) collective-permute-start(bf16[4,32,1024]{2,1,0:T(8,128)(2,1)S(1)} %get-tuple-element.34), channel_id=1, source_target_pairs={{6,0},{0,2},{2,4},{4,6},{7,1},{1,3},{3,5},{5,7},{14,8},{8,10},{10,... | collective-permute-start | bytes 786440 | tf_op jit(solution)/shard_map/sum_x/ppermute | solution.py:175
  155.7 4.3 %collective-permute-start.16 = (bf16[4,32,1024]{2,1,0:T(8,128)(2,1)S(1)}, bf16[4,32,1024]{2,1,0:T(8,128)(2,1)S(1)}, u32[]{:S(2)}, u32[]{:S(2)}) collective-permute-start(bf16[4,32,1024]{2,1,0:T(8,128)(2,1)S(1)} %get-tuple-element.35), channel_id=1, source_target_pairs={{4,0},{6,2},{0,4},{2,6},{5,1},{7,3},{1,5},{3,7},{12,8},{14,10},{8,... | collective-permute-start | bytes 786440 | tf_op jit(solution)/shard_map/sum_x/ppermute | solution.py:175
  160.0 3.1 %collective-permute-start.15 = (bf16[4,32,1024]{2,1,0:T(8,128)(2,1)S(1)}, bf16[4,32,1024]{2,1,0:T(8,128)(2,1)S(1)}, u32[]{:S(2)}, u32[]{:S(2)}) collective-permute-start(bf16[4,32,1024]{2,1,0:T(8,128)(2,1)S(1)} %get-tuple-element.33), channel_id=1, source_target_pairs={{2,0},{4,2},{6,4},{0,6},{3,1},{5,3},{7,5},{1,7},{10,8},{12,10},{14... | collective-permute-start | bytes 786440 | tf_op jit(solution)/shard_map/sum_x/ppermute | solution.py:175
  163.1 6.6 %collective-permute-done.16 = bf16[4,32,1024]{2,1,0:T(8,128)(2,1)S(1)} collective-permute-done((bf16[4,32,1024]{2,1,0:T(8,128)(2,1)S(1)}, bf16[4,32,1024]{2,1,0:T(8,128)(2,1)S(1)}, u32[]{:S(2)}, u32[]{:S(2)}) %collective-permute-start.16) | collective-permute-done | bytes 262176 | tf_op jit(solution)/shard_map/sum_x/ppermute | solution.py:175
  171.9 14.5 %all_to_all.25 = bf16[8,16,1024]{2,1,0:T(8,128)(2,1)S(1)} all-to-all(bf16[8,16,1024]{2,1,0:T(8,128)(2,1)S(1)} %bitcast.36), channel_id=1, replica_groups=mesh['za'=2,'zb'=2,'zq'=2,'y'=4,'zh'=2,'x'=4,'c'=2] {'zb','zq','c'}, dimensions={0} | all-to-all | bytes 524288 | tf_op jit(solution)/shard_map/columns/all_to_all | solution.py:254
  (54 shorter events, 19.4 us)
Async XLA Ops:
  1.3 16.4 %collective-permute-start = (bf16[256,128]{1,0:T(8,128)(2,1)S(1)}, bf16[256,128]{1,0:T(8,128)(2,1)S(1)}, u32[]{:S(2)}, u32[]{:S(2)}) collective-permute-start(bf16[256,128]{1,0:T(8,128)(2,1)S(1)} %get-tuple-element.37), channel_id=1, source_target_pairs={{0,392},{1,393},{64,456},{65,457},{128,0},{129,1},{192,64},{193,65... | collective-permute-start | bytes 196616 | tf_op jit(solution)/shard_map/cache_gather/ppermute | solution.py:183
  13.6 10.7 %collective-permute-start.1 = (bf16[256,128]{1,0:T(8,128)(2,1)S(1)}, bf16[256,128]{1,0:T(8,128)(2,1)S(1)}, u32[]{:S(2)}, u32[]{:S(2)}) collective-permute-start(bf16[256,128]{1,0:T(8,128)(2,1)S(1)} %get-tuple-element.39), channel_id=1, source_target_pairs={{0,264},{1,257},{64,328},{65,321},{128,392},{129,385},{192,456},{1... | collective-permute-start | bytes 196616 | tf_op jit(solution)/shard_map/cache_gather/ppermute | solution.py:183
  15.5 8.7 %collective-permute-start.2 = (bf16[256,128]{1,0:T(8,128)(2,1)S(1)}, bf16[256,128]{1,0:T(8,128)(2,1)S(1)}, u32[]{:S(2)}, u32[]{:S(2)}) collective-permute-start(bf16[256,128]{1,0:T(8,128)(2,1)S(1)} %get-tuple-element.36), channel_id=1, source_target_pairs={{0,128},{1,129},{64,192},{65,193},{128,256},{129,257},{192,320},{1... | collective-permute-start | bytes 196616 | tf_op jit(solution)/shard_map/cache_gather/ppermute | solution.py:183
  24.3 11.6 %collective-permute-start.3 = (bf16[1024,128]{1,0:T(8,128)(2,1)S(1)}, bf16[1024,128]{1,0:T(8,128)(2,1)S(1)}, u32[]{:S(2)}, u32[]{:S(2)}) collective-permute-start(bf16[1024,128]{1,0:T(8,128)(2,1)S(1)} %pad_maximum_fusion.3), channel_id=1, source_target_pairs={{0,64},{64,0},{1,65},{65,1},{2,66},{66,2},{3,67},{67,3},{4,68},{68... | collective-permute-start | bytes 786440 | tf_op jit(solution)/shard_map/cache_gather/ppermute | solution.py:167
  28.9 6.9 %collective-permute-start.4 = (bf16[512,128]{1,0:T(8,128)(2,1)S(1)}, bf16[512,128]{1,0:T(8,128)(2,1)S(1)}, u32[]{:S(2)}, u32[]{:S(2)}) collective-permute-start(bf16[512,128]{1,0:T(8,128)(2,1)S(1)} %get-tuple-element.47), channel_id=1, source_target_pairs={{0,1},{1,0},{2,3},{3,2},{4,5},{5,4},{6,7},{7,6},{8,9},{9,8},{10,11... | collective-permute-start | bytes 393224 | tf_op jit(solution)/shard_map/weight_gather/ppermute | solution.py:167
  37.5 33.9 %all-to-all-start = ((bf16[4,2048,128]{2,1,0:T(8,128)(2,1)}), bf16[4,2048,128]{2,1,0:T(8,128)(2,1)}, u32[]{:S(2)}, u32[]{:S(2)}) async-start(bf16[4,2048,128]{2,1,0:T(8,128)(2,1)} %broadcast_in_dim.6), calls=%async_computation | async-start | bytes 4194304 | tf_op jit(solution)/shard_map/cache_gather/all_to_all | solution.py:163
  41.9 29.5 %collective-permute-start.5 = (bf16[1024,128]{1,0:T(8,128)(2,1)S(1)}, bf16[1024,128]{1,0:T(8,128)(2,1)S(1)}, u32[]{:S(2)}, u32[]{:S(2)}) collective-permute-start(bf16[1024,128]{1,0:T(8,128)(2,1)S(1)} %pad_maximum_fusion.4), channel_id=1, source_target_pairs={{0,256},{256,0},{1,257},{257,1},{2,258},{258,2},{3,259},{259,3},{4... | collective-permute-start | bytes 786440 | tf_op jit(solution)/shard_map/weight_gather/ppermute | solution.py:167
  71.4 8.6 %collective-permute-start.6 = (bf16[8192,128]{1,0:T(8,128)(2,1)}, bf16[8192,128]{1,0:T(8,128)(2,1)}, u32[]{:S(2)}, u32[]{:S(2)}) collective-permute-start(bf16[8192,128]{1,0:T(8,128)(2,1)} %bitcast.4.own_ref), channel_id=1, source_target_pairs={{0,1},{1,0},{2,3},{3,2},{4,5},{5,4},{6,7},{7,6},{8,9},{9,8},{10,11... | collective-permute-start | bytes 6291464 | tf_op jit(solution)/shard_map/cache_gather/ppermute | solution.py:167
  75.6 4.4 %copy-start.4 = (bf16[256,512]{1,0:T(8,128)(2,1)S(1)}, bf16[256,512]{1,0:T(8,128)(2,1)}, u32[]{:S(2)}) copy-start(bf16[256,512]{1,0:T(8,128)(2,1)} %q_ref.1) | copy-start | bytes 786436
  75.6 4.4 %copy-start.5 = (s32[32]{0:T(128)S(1)}, s32[32]{0:T(128)}, u32[]{:S(2)}) copy-start(s32[32]{0:T(128)} %counts.1) | copy-start | bytes 388
  75.6 4.4 %copy-start.6 = (s32[64]{0:T(128)S(1)}, s32[64]{0:T(128)}, u32[]{:S(2)}) copy-start(s32[64]{0:T(128)} %order.1) | copy-start | bytes 772
  75.6 30.5 %all-to-all-start.1 = ((bf16[4,2,1024,128]{3,2,1,0:T(8,128)(2,1)}), bf16[4,2,1024,128]{3,2,1,0:T(8,128)(2,1)S(1)}, u32[]{:S(2)}, u32[]{:S(2)}) async-start(bf16[4,2,1024,128]{3,2,1,0:T(8,128)(2,1)} %broadcast_in_dim.7), calls=%async_computation.1 | async-start | bytes 4194304 | tf_op jit(solution)/shard_map/weight_gather/all_to_all | solution.py:163
  87.2 9.3 %collective-permute-start.9 = (bf16[4,32,512]{2,1,0:T(8,128)(2,1)S(1)}, bf16[4,32,512]{2,1,0:T(8,128)(2,1)S(1)}, u32[]{:S(2)}, u32[]{:S(2)}) collective-permute-start(bf16[4,32,512]{2,1,0:T(8,128)(2,1)S(1)} %get-tuple-element.43), channel_id=1, source_target_pairs={{0,192},{64,128},{128,64},{192,0},{1,193},{65,129},{129,65},{193,1... | collective-permute-start | bytes 393224 | tf_op jit(solution)/shard_map/rows_gather/ppermute | solution.py:171
  89.1 12.9 %collective-permute-start.8 = (bf16[4,32,512]{2,1,0:T(8,128)(2,1)S(1)}, bf16[4,32,512]{2,1,0:T(8,128)(2,1)S(1)}, u32[]{:S(2)}, u32[]{:S(2)}) collective-permute-start(bf16[4,32,512]{2,1,0:T(8,128)(2,1)S(1)} %get-tuple-element.43), channel_id=1, source_target_pairs={{0,128},{64,192},{128,0},{192,64},{1,129},{65,193},{129,1},{193,65... | collective-permute-start | bytes 393224 | tf_op jit(solution)/shard_map/rows_gather/ppermute | solution.py:171
  91.1 11.2 %collective-permute-start.7 = (bf16[4,32,512]{2,1,0:T(8,128)(2,1)S(1)}, bf16[4,32,512]{2,1,0:T(8,128)(2,1)S(1)}, u32[]{:S(2)}, u32[]{:S(2)}) collective-permute-start(bf16[4,32,512]{2,1,0:T(8,128)(2,1)S(1)} %get-tuple-element.43), channel_id=1, source_target_pairs={{0,64},{64,0},{128,192},{192,128},{1,65},{65,1},{129,193},{193,129... | collective-permute-start | bytes 393224 | tf_op jit(solution)/shard_map/rows_gather/ppermute | solution.py:171
  106.1 4.5 %collective-permute-start.10 = (bf16[4,4,32,512]{3,2,1,0:T(8,128)(2,1)S(1)}, bf16[4,4,32,512]{3,2,1,0:T(8,128)(2,1)S(1)}, u32[]{:S(2)}, u32[]{:S(2)}) collective-permute-start(bf16[4,4,32,512]{3,2,1,0:T(8,128)(2,1)S(1)} %pad_maximum_fusion.a_ref), channel_id=1, source_target_pairs={{0,1},{1,0},{2,3},{3,2},{4,5},{5,4},{6,7},{7,6},{8,9},{9,8},{10,11... | collective-permute-start | bytes 1572872 | tf_op jit(solution)/shard_map/rows_gather/ppermute | solution.py:167
  113.4 19.5 %all-to-all-start.2 = ((bf16[4,4,32,1024]{3,2,1,0:T(8,128)(2,1)}), bf16[4,4,32,1024]{3,2,1,0:T(8,128)(2,1)}, u32[]{:S(2)}, u32[]{:S(2)}) async-start(bf16[4,4,32,1024]{3,2,1,0:T(8,128)(2,1)} %projection.2), calls=%async_computation.2 | async-start | bytes 2097152 | tf_op jit(solution)/shard_map/sum_x/all_to_all | solution.py:241
  117.7 9.3 %collective-permute-start.13 = (bf16[4,32,512]{2,1,0:T(8,128)(2,1)S(1)}, bf16[4,32,512]{2,1,0:T(8,128)(2,1)S(1)}, u32[]{:S(2)}, u32[]{:S(2)}) collective-permute-start(bf16[4,32,512]{2,1,0:T(8,128)(2,1)S(1)} %get-tuple-element.44), channel_id=1, source_target_pairs={{0,192},{64,128},{128,64},{192,0},{1,193},{65,129},{129,65},{193,1... | collective-permute-start | bytes 393224 | tf_op jit(solution)/shard_map/rows_gather/ppermute | solution.py:171
  119.6 13.0 %collective-permute-start.12 = (bf16[4,32,512]{2,1,0:T(8,128)(2,1)S(1)}, bf16[4,32,512]{2,1,0:T(8,128)(2,1)S(1)}, u32[]{:S(2)}, u32[]{:S(2)}) collective-permute-start(bf16[4,32,512]{2,1,0:T(8,128)(2,1)S(1)} %get-tuple-element.44), channel_id=1, source_target_pairs={{0,128},{64,192},{128,0},{192,64},{1,129},{65,193},{129,1},{193,65... | collective-permute-start | bytes 393224 | tf_op jit(solution)/shard_map/rows_gather/ppermute | solution.py:171
  121.5 11.3 %collective-permute-start.11 = (bf16[4,32,512]{2,1,0:T(8,128)(2,1)S(1)}, bf16[4,32,512]{2,1,0:T(8,128)(2,1)S(1)}, u32[]{:S(2)}, u32[]{:S(2)}) collective-permute-start(bf16[4,32,512]{2,1,0:T(8,128)(2,1)S(1)} %get-tuple-element.44), channel_id=1, source_target_pairs={{0,64},{64,0},{128,192},{192,128},{1,65},{65,1},{129,193},{193,129... | collective-permute-start | bytes 393224 | tf_op jit(solution)/shard_map/rows_gather/ppermute | solution.py:171
  132.9 13.1 %copy-start = (bf16[4,4,32,512]{3,2,1,0:T(8,128)(2,1)}, bf16[4,4,32,512]{3,2,1,0:T(8,128)(2,1)S(1)}, u32[]{:S(2)}) copy-start(bf16[4,4,32,512]{3,2,1,0:T(8,128)(2,1)S(1)} %pad_maximum_fusion.2.a_ref) | copy-start | bytes 1572868
  135.4 35.3 %all-to-all-start.3 = ((bf16[2,4,32,1024]{3,2,1,0:T(8,128)(2,1)}), bf16[2,4,32,1024]{3,2,1,0:T(8,128)(2,1)}, u32[]{:S(2)}, u32[]{:S(2)}) async-start(bf16[2,4,32,1024]{3,2,1,0:T(8,128)(2,1)} %broadcast_in_dim.8), calls=%async_computation.3 | async-start | bytes 1048576 | tf_op jit(solution)/shard_map/sum_zh/all_to_all | solution.py:163
  142.5 5.0 %collective-permute-start.14 = (bf16[4,4,32,512]{3,2,1,0:T(8,128)(2,1)S(1)}, bf16[4,4,32,512]{3,2,1,0:T(8,128)(2,1)S(1)}, u32[]{:S(2)}, u32[]{:S(2)}) collective-permute-start(bf16[4,4,32,512]{3,2,1,0:T(8,128)(2,1)S(1)} %pad_maximum_fusion.2.a_ref), channel_id=1, source_target_pairs={{0,1},{1,0},{2,3},{3,2},{4,5},{5,4},{6,7},{7,6},{8,9},{9,8},{10,11... | collective-permute-start | bytes 1572872 | tf_op jit(solution)/shard_map/rows_gather/ppermute | solution.py:167
  147.5 0.8 copy-start.2
  148.3 1.0 copy-start.1
  149.3 1.0 copy-start.3
  152.4 10.7 %collective-permute-start.17 = (bf16[4,32,1024]{2,1,0:T(8,128)(2,1)S(1)}, bf16[4,32,1024]{2,1,0:T(8,128)(2,1)S(1)}, u32[]{:S(2)}, u32[]{:S(2)}) collective-permute-start(bf16[4,32,1024]{2,1,0:T(8,128)(2,1)S(1)} %get-tuple-element.34), channel_id=1, source_target_pairs={{6,0},{0,2},{2,4},{4,6},{7,1},{1,3},{3,5},{5,7},{14,8},{8,10},{10,... | collective-permute-start | bytes 786440 | tf_op jit(solution)/shard_map/sum_x/ppermute | solution.py:175
  155.7 14.1 %collective-permute-start.16 = (bf16[4,32,1024]{2,1,0:T(8,128)(2,1)S(1)}, bf16[4,32,1024]{2,1,0:T(8,128)(2,1)S(1)}, u32[]{:S(2)}, u32[]{:S(2)}) collective-permute-start(bf16[4,32,1024]{2,1,0:T(8,128)(2,1)S(1)} %get-tuple-element.35), channel_id=1, source_target_pairs={{4,0},{6,2},{0,4},{2,6},{5,1},{7,3},{1,5},{3,7},{12,8},{14,10},{8,... | collective-permute-start | bytes 786440 | tf_op jit(solution)/shard_map/sum_x/ppermute | solution.py:175
  160.0 10.8 %collective-permute-start.15 = (bf16[4,32,1024]{2,1,0:T(8,128)(2,1)S(1)}, bf16[4,32,1024]{2,1,0:T(8,128)(2,1)S(1)}, u32[]{:S(2)}, u32[]{:S(2)}) collective-permute-start(bf16[4,32,1024]{2,1,0:T(8,128)(2,1)S(1)} %get-tuple-element.33), channel_id=1, source_target_pairs={{2,0},{4,2},{6,4},{0,6},{3,1},{5,3},{7,5},{1,7},{10,8},{12,10},{14... | collective-permute-start | bytes 786440 | tf_op jit(solution)/shard_map/sum_x/ppermute | solution.py:175

commit v5 on v4

--- a/solution.py
+++ b/solution.py
@@ -144,7 +144,7 @@
     part += jnp.dot(b_ref[...].reshape(-1, half), w[half:], preferred_element_type=jnp.float32)
     part = part.astype(jnp.bfloat16).reshape(QUAD, X, 32, 2 * HD)
     for i in range(QUAD):
-        o_ref[:, me[0] ^ i] = part[i]
+        o_ref[:, me[0] ^ ((QUAD - i) % QUAD)] = part[i]
 
 
 def project(me, a, b, w):
@@ -197,15 +197,17 @@
         )
 
     with jax.named_scope("cache_gather"):
-        near = [
-            piece(0),
-            along(piece(-2), lambda z, c: -2),
-            along(piece(8 * c - 4), lambda z, c: 8 * c - 4),
-            along(piece(2), lambda z, c: 2),
-        ]
+        here = piece(0)
+        up = along(piece(-2), lambda z, c: -2)
+        down = along(piece(2), lambda z, c: 2)
+        far = along(piece(8 * c - 4), lambda z, c: 8 * c - 4)
+        side = along(piece(jnp.where(zq == 1, 3, -3)), lambda z, c: 3 if z % 2 else -3)
+        near = jnp.concatenate([here, up, down], axis=0)
         near, weight = lax.optimization_barrier((near, weight))
-        near = jnp.concatenate(near, axis=0)
-        near = jnp.concatenate([near, swap(near, "zq")], axis=0)
+        beside = swap(near, "zq")
+        near = jnp.concatenate(
+            [near[: 2 * ROWS], far, near[2 * ROWS :], beside[: 2 * ROWS], side, beside[2 * ROWS :]], axis=0
+        )
     with jax.named_scope("weight_gather"):
         given = swap(lax.dynamic_slice_in_dim(weight, (1 - c) * HD, HD, 1), "c")
         kept = lax.dynamic_slice_in_dim(weight, c * HD, HD, 1)
@@ -223,9 +225,7 @@
         place = jnp.stack([zl * Y + y, c, zh]).astype(jnp.int32)
         heads = attend(counts, order, place, queries, own, other)
 
-    def projected(mine):
-        with jax.named_scope("rows_gather"):
-            theirs = swap(mine, "c")
+    def projected(mine, theirs):
         with jax.named_scope("projection"):
             here = jnp.reshape(zb * ZQ + zq, (1,)).astype(jnp.int32)
             return project(here, mine, theirs, wide)
@@ -234,20 +234,25 @@
         return lax.dynamic_index_in_dim(parts, (x + shift) % X, 0, keepdims=False)
 
     with jax.named_scope("rows_gather"):
-        first, second = (jnp.stack([rows] + [quad(rows, step) for step in range(1, QUAD)]) for rows in heads)
-        first, wide = lax.optimization_barrier((first, wide))
-    parts = projected(first)
+        first, second = (
+            jnp.stack([rows] + [quad(rows, step) for step in range(QUAD - 1, 0, -1)]) for rows in heads
+        )
+        theirs = swap(first, "c")
+        first, theirs, wide = lax.optimization_barrier((first, theirs, wide))
+    parts = projected(first, theirs)
     with jax.named_scope("sum_x"):
         away = lax.all_to_all(parts, "x", 0, 0)
         away = jnp.sum(away.astype(jnp.float32), axis=0).astype(jnp.bfloat16)
+        away = jnp.broadcast_to(away[None], (ZH, *away.shape))
         away, second = lax.optimization_barrier((away, second))
+        theirs = swap(second, "c")
     with jax.named_scope("sum_zh"):
-        back = spread(away, "zh", ZH)
+        back = lax.all_to_all(away, "zh", 0, 0)
         back = lax.dynamic_index_in_dim(back, 1 - zh, 0, keepdims=False)
-    parts = projected(second)
+    parts = projected(second, theirs)
     with jax.named_scope("sum_x"):
         stay = part_of(parts, 0).astype(jnp.float32)
-        for shift in range(1, X):
+        for shift in range(X - 1, 0, -1):
             stay += around(part_of(parts, X - shift), "x", X, shift).astype(jnp.float32)
     with jax.named_scope("columns"):
         mixed = (stay + back.astype(jnp.float32)).astype(jnp.bfloat16)

time: 189 us -> 188 us (level)
  the two profiles are of different devices: /device:TPU:1 before, /device:TPU:18 now
where the time goes in v5:
time: 188 us; the launch traced here: 187 us
  starting transfers between devices  90.9 us (48%)
  waiting for transfers between devices  53.7 us (29%)
  Pallas kernels  16.2 us (9%)
  blocking collectives  12.4 us (7%)
  local copies, waits for them, and re-layouts  8.56 us (5%)
  other arithmetic  4.38 us (2%)
    ppermute x6, waiting for transfers between devices, swap(): return lax.ppermute(piece, axis, [(0, 1), (1, 0)])  32.4 us
    ppermute x4, starting transfers between devices, along(): return lax.ppermute(piece, LINE, perm)  24.5 us
    ppermute x6, starting transfers between devices, quad(): lax.ppermute(piece, ('zb', 'zq'), [(i, i ^ step) for i in range(QUAD)])  20.2 us
    ppermute x6, starting transfers between devices, swap(): return lax.ppermute(piece, axis, [(0, 1), (1, 0)])  13.6 us
    all_to_all x1, blocking collectives, body(): lax.all_to_all(mixed.reshape(QUAD * C, 16, ZL * HD), ('zb', 'zq', 'c'), 0...  12.4 us
    pallas_call x1, Pallas kernels, attend(): pl.pallas_call(attention_kernel, out_shape=jax.ShapeDtypeStruct((ZH, X, 3...  11.4 us
    ppermute x6, waiting for transfers between devices, quad(): lax.ppermute(piece, ('zb', 'zq'), [(i, i ^ step) for i in range(QUAD)])  11.3 us
    ppermute x3, starting transfers between devices, around(): lax.ppermute(piece, axis, [((i + shift) % count, i) for i in range(count)])  10.4 us
  transfers between devices with their start and end apart: 23, of which 12 were waited for; matrix products, arithmetic and copies ran while one was open for 1% of the time, Pallas kernels for 7%

profile of v5, /device:TPU:18, one launch (start us, length us, event | category | flops | bytes accessed | tf_op | source)
XLA Modules:
  0.0 186.5 jit_solution(6357280424462392877)
XLA Ops:
  1.3 11.9 %collective-permute-start = (bf16[256,128]{1,0:T(8,128)(2,1)S(1)}, bf16[256,128]{1,0:T(8,128)(2,1)S(1)}, u32[]{:S(2)}, u32[]{:S(2)}) collective-permute-start(bf16[256,128]{1,0:T(8,128)(2,1)S(1)} %get-tuple-element.34), channel_id=1, source_target_pairs={{0,392},{1,393},{64,456},{65,457},{128,0},{129,1},{192,64},{193,65... | collective-permute-start | bytes 196616 | tf_op jit(solution)/shard_map/cache_gather/ppermute | solution.py:183
  13.2 1.9 %collective-permute-start.1 = (bf16[256,128]{1,0:T(8,128)(2,1)S(1)}, bf16[256,128]{1,0:T(8,128)(2,1)S(1)}, u32[]{:S(2)}, u32[]{:S(2)}) collective-permute-start(bf16[256,128]{1,0:T(8,128)(2,1)S(1)} %get-tuple-element.33), channel_id=1, source_target_pairs={{0,128},{1,129},{64,192},{65,193},{128,256},{129,257},{192,320},{1... | collective-permute-start | bytes 196616 | tf_op jit(solution)/shard_map/cache_gather/ppermute | solution.py:183
  15.1 5.9 %collective-permute-start.2 = (bf16[256,128]{1,0:T(8,128)(2,1)S(1)}, bf16[256,128]{1,0:T(8,128)(2,1)S(1)}, u32[]{:S(2)}, u32[]{:S(2)}) collective-permute-start(bf16[256,128]{1,0:T(8,128)(2,1)S(1)} %get-tuple-element.36), channel_id=1, source_target_pairs={{0,264},{1,257},{64,328},{65,321},{128,392},{129,385},{192,456},{1... | collective-permute-start | bytes 196616 | tf_op jit(solution)/shard_map/cache_gather/ppermute | solution.py:183
  21.0 4.8 %collective-permute-start.4 = (bf16[256,128]{1,0:T(8,128)(2,1)S(1)}, bf16[256,128]{1,0:T(8,128)(2,1)S(1)}, u32[]{:S(2)}, u32[]{:S(2)}) collective-permute-start(bf16[256,128]{1,0:T(8,128)(2,1)S(1)} %get-tuple-element.32), channel_id=1, source_target_pairs={{0,328},{1,329},{64,256},{65,257},{128,456},{129,457},{192,384},{1... | collective-permute-start | bytes 196616 | tf_op jit(solution)/shard_map/cache_gather/ppermute | solution.py:183
  25.9 1.9 %collective-permute-start.3 = (bf16[768,128]{1,0:T(8,128)(2,1)S(1)}, bf16[768,128]{1,0:T(8,128)(2,1)S(1)}, u32[]{:S(2)}, u32[]{:S(2)}) collective-permute-start(bf16[768,128]{1,0:T(8,128)(2,1)S(1)} %pad_maximum_fusion.4), channel_id=1, source_target_pairs={{0,64},{64,0},{1,65},{65,1},{2,66},{66,2},{3,67},{67,3},{4,68},{68... | collective-permute-start | bytes 589832 | tf_op jit(solution)/shard_map/cache_gather/ppermute | solution.py:167
  27.8 1.9 %collective-permute-start.5 = (bf16[512,128]{1,0:T(8,128)(2,1)S(1)}, bf16[512,128]{1,0:T(8,128)(2,1)S(1)}, u32[]{:S(2)}, u32[]{:S(2)}) collective-permute-start(bf16[512,128]{1,0:T(8,128)(2,1)S(1)} %get-tuple-element.44), channel_id=1, source_target_pairs={{0,1},{1,0},{2,3},{3,2},{4,5},{5,4},{6,7},{7,6},{8,9},{9,8},{10,11... | collective-permute-start | bytes 393224 | tf_op jit(solution)/shard_map/weight_gather/ppermute | solution.py:167
  31.1 2.7 %collective-permute-done.3 = bf16[768,128]{1,0:T(8,128)(2,1)S(1)} collective-permute-done((bf16[768,128]{1,0:T(8,128)(2,1)S(1)}, bf16[768,128]{1,0:T(8,128)(2,1)S(1)}, u32[]{:S(2)}, u32[]{:S(2)}) %collective-permute-start.3) | collective-permute-done | bytes 196640 | tf_op jit(solution)/shard_map/cache_gather/ppermute | solution.py:167
  35.4 4.8 %all-to-all-start = ((bf16[4,2048,128]{2,1,0:T(8,128)(2,1)}), bf16[4,2048,128]{2,1,0:T(8,128)(2,1)}, u32[]{:S(2)}, u32[]{:S(2)}) async-start(bf16[4,2048,128]{2,1,0:T(8,128)(2,1)} %broadcast_in_dim.6), calls=%async_computation | async-start | bytes 4194304 | tf_op jit(solution)/shard_map/cache_gather/all_to_all | solution.py:163
  40.2 4.0 %collective-permute-start.6 = (bf16[1024,128]{1,0:T(8,128)(2,1)S(1)}, bf16[1024,128]{1,0:T(8,128)(2,1)S(1)}, u32[]{:S(2)}, u32[]{:S(2)}) collective-permute-start(bf16[1024,128]{1,0:T(8,128)(2,1)S(1)} %pad_maximum_fusion.3), channel_id=1, source_target_pairs={{0,256},{256,0},{1,257},{257,1},{2,258},{258,2},{3,259},{259,3},{4... | collective-permute-start | bytes 786440 | tf_op jit(solution)/shard_map/weight_gather/ppermute | solution.py:167
  44.2 24.8 %collective-permute-done.6 = bf16[1024,128]{1,0:T(8,128)(2,1)S(1)} collective-permute-done((bf16[1024,128]{1,0:T(8,128)(2,1)S(1)}, bf16[1024,128]{1,0:T(8,128)(2,1)S(1)}, u32[]{:S(2)}, u32[]{:S(2)}) %collective-permute-start.6) | collective-permute-done | bytes 262176 | tf_op jit(solution)/shard_map/weight_gather/ppermute | solution.py:167
  69.0 1.9 %collective-permute-start.7 = (bf16[8192,128]{1,0:T(8,128)(2,1)}, bf16[8192,128]{1,0:T(8,128)(2,1)}, u32[]{:S(2)}, u32[]{:S(2)}) collective-permute-start(bf16[8192,128]{1,0:T(8,128)(2,1)} %bitcast.4.own_ref), channel_id=1, source_target_pairs={{0,1},{1,0},{2,3},{3,2},{4,5},{5,4},{6,7},{7,6},{8,9},{9,8},{10,11... | collective-permute-start | bytes 6291464 | tf_op jit(solution)/shard_map/cache_gather/ppermute | solution.py:167
  72.7 4.9 %all-to-all-start.1 = ((bf16[4,2,1024,128]{3,2,1,0:T(8,128)(2,1)}), bf16[4,2,1024,128]{3,2,1,0:T(8,128)(2,1)S(1)}, u32[]{:S(2)}, u32[]{:S(2)}) async-start(bf16[4,2,1024,128]{3,2,1,0:T(8,128)(2,1)} %broadcast_in_dim.7), calls=%async_computation.1 | async-start | bytes 4194304 | tf_op jit(solution)/shard_map/weight_gather/all_to_all | solution.py:163
  77.7 11.4 %attention.1 = bf16[2,4,32,512]{3,2,1,0:T(8,128)(2,1)S(1)} custom-call(s32[32]{0:T(128)S(1)} %copy-done.5, s32[64]{0:T(128)S(1)} %copy-done.6, s32[3]{0:T(128)S(1)} %pad_add_fusion.place, bf16[256,512]{1,0:T(8,128)(2,1)S(1)} %copy-done.4, bf16[8192,128]{1,0:T(8,128)(2,1)} %bitcast.4.own_ref, bf16[8192,128]{1,0:T(8,128)(2,1)} %collective-permute-done.7.other_ref), custom_call_target="tpu_custom_call" | custom-call | tf_op jit(solution)/shard_map/attention/pallas_call | solution.py:130
  89.2 1.9 %collective-permute-start.8 = (bf16[4,32,512]{2,1,0:T(8,128)(2,1)S(1)}, bf16[4,32,512]{2,1,0:T(8,128)(2,1)S(1)}, u32[]{:S(2)}, u32[]{:S(2)}) collective-permute-start(bf16[4,32,512]{2,1,0:T(8,128)(2,1)S(1)} %get-tuple-element.40), channel_id=1, source_target_pairs={{0,192},{64,128},{128,64},{192,0},{1,193},{65,129},{129,65},{193,1... | collective-permute-start | bytes 393224 | tf_op jit(solution)/shard_map/rows_gather/ppermute | solution.py:171
  91.1 1.9 %collective-permute-start.9 = (bf16[4,32,512]{2,1,0:T(8,128)(2,1)S(1)}, bf16[4,32,512]{2,1,0:T(8,128)(2,1)S(1)}, u32[]{:S(2)}, u32[]{:S(2)}) collective-permute-start(bf16[4,32,512]{2,1,0:T(8,128)(2,1)S(1)} %get-tuple-element.40), channel_id=1, source_target_pairs={{0,128},{64,192},{128,0},{192,64},{1,129},{65,193},{129,1},{193,65... | collective-permute-start | bytes 393224 | tf_op jit(solution)/shard_map/rows_gather/ppermute | solution.py:171
  93.1 6.3 %collective-permute-start.10 = (bf16[4,32,512]{2,1,0:T(8,128)(2,1)S(1)}, bf16[4,32,512]{2,1,0:T(8,128)(2,1)S(1)}, u32[]{:S(2)}, u32[]{:S(2)}) collective-permute-start(bf16[4,32,512]{2,1,0:T(8,128)(2,1)S(1)} %get-tuple-element.40), channel_id=1, source_target_pairs={{0,64},{64,0},{128,192},{192,128},{1,65},{65,1},{129,193},{193,129... | collective-permute-start | bytes 393224 | tf_op jit(solution)/shard_map/rows_gather/ppermute | solution.py:171
  99.4 4.6 %collective-permute-done.9 = bf16[4,32,512]{2,1,0:T(8,128)(2,1)S(1)} collective-permute-done((bf16[4,32,512]{2,1,0:T(8,128)(2,1)S(1)}, bf16[4,32,512]{2,1,0:T(8,128)(2,1)S(1)}, u32[]{:S(2)}, u32[]{:S(2)}) %collective-permute-start.9) | collective-permute-done | bytes 131104 | tf_op jit(solution)/shard_map/rows_gather/ppermute | solution.py:171
  105.2 1.9 %collective-permute-start.11 = (bf16[4,4,32,512]{3,2,1,0:T(8,128)(2,1)S(1)}, bf16[4,4,32,512]{3,2,1,0:T(8,128)(2,1)S(1)}, u32[]{:S(2)}, u32[]{:S(2)}) collective-permute-start(bf16[4,4,32,512]{3,2,1,0:T(8,128)(2,1)S(1)} %pad_maximum_fusion.a_ref), channel_id=1, source_target_pairs={{0,1},{1,0},{2,3},{3,2},{4,5},{5,4},{6,7},{7,6},{8,9},{9,8},{10,11... | collective-permute-start | bytes 1572872 | tf_op jit(solution)/shard_map/rows_gather/ppermute | solution.py:167
  109.0 2.8 %projection.2 = bf16[4,4,32,1024]{3,2,1,0:T(8,128)(2,1)} custom-call(s32[1]{0:T(128)} %bitcast.me, bf16[4,4,32,512]{3,2,1,0:T(8,128)(2,1)S(1)} %pad_maximum_fusion.a_ref, bf16[4,4,32,512]{3,2,1,0:T(8,128)(2,1)S(1)} %collective-permute-done.11.b_ref, bf16[4,2,1024,128]{3,2,1,0:T(8,128)(2,1)S(1)} %all-to-all-done.1.w_ref), custom_call_target="tpu_custom_call" | custom-call | tf_op jit(solution)/shard_map/projection/pallas_call | solution.py:152
  111.8 4.8 %all-to-all-start.2 = ((bf16[4,4,32,1024]{3,2,1,0:T(8,128)(2,1)}), bf16[4,4,32,1024]{3,2,1,0:T(8,128)(2,1)}, u32[]{:S(2)}, u32[]{:S(2)}) async-start(bf16[4,4,32,1024]{3,2,1,0:T(8,128)(2,1)} %projection.2), calls=%async_computation.2 | async-start | bytes 2097152 | tf_op jit(solution)/shard_map/sum_x/all_to_all | solution.py:244
  116.6 3.4 %collective-permute-start.12 = (bf16[4,32,512]{2,1,0:T(8,128)(2,1)S(1)}, bf16[4,32,512]{2,1,0:T(8,128)(2,1)S(1)}, u32[]{:S(2)}, u32[]{:S(2)}) collective-permute-start(bf16[4,32,512]{2,1,0:T(8,128)(2,1)S(1)} %get-tuple-element.41), channel_id=1, source_target_pairs={{0,192},{64,128},{128,64},{192,0},{1,193},{65,129},{129,65},{193,1... | collective-permute-start | bytes 393224 | tf_op jit(solution)/shard_map/rows_gather/ppermute | solution.py:171
  120.0 1.9 %collective-permute-start.13 = (bf16[4,32,512]{2,1,0:T(8,128)(2,1)S(1)}, bf16[4,32,512]{2,1,0:T(8,128)(2,1)S(1)}, u32[]{:S(2)}, u32[]{:S(2)}) collective-permute-start(bf16[4,32,512]{2,1,0:T(8,128)(2,1)S(1)} %get-tuple-element.41), channel_id=1, source_target_pairs={{0,128},{64,192},{128,0},{192,64},{1,129},{65,193},{129,1},{193,65... | collective-permute-start | bytes 393224 | tf_op jit(solution)/shard_map/rows_gather/ppermute | solution.py:171
  121.9 4.8 %collective-permute-start.14 = (bf16[4,32,512]{2,1,0:T(8,128)(2,1)S(1)}, bf16[4,32,512]{2,1,0:T(8,128)(2,1)S(1)}, u32[]{:S(2)}, u32[]{:S(2)}) collective-permute-start(bf16[4,32,512]{2,1,0:T(8,128)(2,1)S(1)} %get-tuple-element.41), channel_id=1, source_target_pairs={{0,64},{64,0},{128,192},{192,128},{1,65},{65,1},{129,193},{193,129... | collective-permute-start | bytes 393224 | tf_op jit(solution)/shard_map/rows_gather/ppermute | solution.py:171
  126.8 4.4 %collective-permute-done.13 = bf16[4,32,512]{2,1,0:T(8,128)(2,1)S(1)} collective-permute-done((bf16[4,32,512]{2,1,0:T(8,128)(2,1)S(1)}, bf16[4,32,512]{2,1,0:T(8,128)(2,1)S(1)}, u32[]{:S(2)}, u32[]{:S(2)}) %collective-permute-start.13) | collective-permute-done | bytes 131104 | tf_op jit(solution)/shard_map/rows_gather/ppermute | solution.py:171
  134.9 7.6 %all-to-all-start.3 = ((bf16[2,4,32,1024]{3,2,1,0:T(8,128)(2,1)}), bf16[2,4,32,1024]{3,2,1,0:T(8,128)(2,1)}, u32[]{:S(2)}, u32[]{:S(2)}) async-start(bf16[2,4,32,1024]{3,2,1,0:T(8,128)(2,1)} %broadcast_in_dim.8), calls=%async_computation.3 | async-start | bytes 1048576 | tf_op jit(solution)/shard_map/sum_zh/all_to_all | solution.py:250
  149.2 1.9 %projection.3 = bf16[4,4,32,1024]{3,2,1,0:T(8,128)(2,1)S(1)} custom-call(s32[1]{0:T(128)} %bitcast.me, bf16[4,4,32,512]{3,2,1,0:T(8,128)(2,1)S(1)} %copy-done.1, bf16[4,4,32,512]{3,2,1,0:T(8,128)(2,1)S(1)} %copy-done.3, bf16[4,2,1024,128]{3,2,1,0:T(8,128)(2,1)S(1)} %all-to-all-done.1.w_ref), custom_call_target="tpu_custom_call" | custom-call | tf_op jit(solution)/shard_map/projection/pallas_call | solution.py:152
  151.2 3.4 %collective-permute-start.16 = (bf16[4,32,1024]{2,1,0:T(8,128)(2,1)S(1)}, bf16[4,32,1024]{2,1,0:T(8,128)(2,1)S(1)}, u32[]{:S(2)}, u32[]{:S(2)}) collective-permute-start(bf16[4,32,1024]{2,1,0:T(8,128)(2,1)S(1)} %get-tuple-element.29), channel_id=1, source_target_pairs={{6,0},{0,2},{2,4},{4,6},{7,1},{1,3},{3,5},{5,7},{14,8},{8,10},{10,... | collective-permute-start | bytes 786440 | tf_op jit(solution)/shard_map/sum_x/ppermute | solution.py:175
  154.6 2.8 %collective-permute-start.17 = (bf16[4,32,1024]{2,1,0:T(8,128)(2,1)S(1)}, bf16[4,32,1024]{2,1,0:T(8,128)(2,1)S(1)}, u32[]{:S(2)}, u32[]{:S(2)}) collective-permute-start(bf16[4,32,1024]{2,1,0:T(8,128)(2,1)S(1)} %get-tuple-element.31), channel_id=1, source_target_pairs={{4,0},{6,2},{0,4},{2,6},{5,1},{7,3},{1,5},{3,7},{12,8},{14,10},{8,... | collective-permute-start | bytes 786440 | tf_op jit(solution)/shard_map/sum_x/ppermute | solution.py:175
  157.4 4.3 %collective-permute-start.18 = (bf16[4,32,1024]{2,1,0:T(8,128)(2,1)S(1)}, bf16[4,32,1024]{2,1,0:T(8,128)(2,1)S(1)}, u32[]{:S(2)}, u32[]{:S(2)}) collective-permute-start(bf16[4,32,1024]{2,1,0:T(8,128)(2,1)S(1)} %get-tuple-element.30), channel_id=1, source_target_pairs={{2,0},{4,2},{6,4},{0,6},{3,1},{5,3},{7,5},{1,7},{10,8},{12,10},{14... | collective-permute-start | bytes 786440 | tf_op jit(solution)/shard_map/sum_x/ppermute | solution.py:175
  162.2 5.0 %collective-permute-done.17 = bf16[4,32,1024]{2,1,0:T(8,128)(2,1)S(1)} collective-permute-done((bf16[4,32,1024]{2,1,0:T(8,128)(2,1)S(1)}, bf16[4,32,1024]{2,1,0:T(8,128)(2,1)S(1)}, u32[]{:S(2)}, u32[]{:S(2)}) %collective-permute-start.17) | collective-permute-done | bytes 262176 | tf_op jit(solution)/shard_map/sum_x/ppermute | solution.py:175
  167.2 4.5 %collective-permute-done.18 = bf16[4,32,1024]{2,1,0:T(8,128)(2,1)S(1)} collective-permute-done((bf16[4,32,1024]{2,1,0:T(8,128)(2,1)S(1)}, bf16[4,32,1024]{2,1,0:T(8,128)(2,1)S(1)}, u32[]{:S(2)}, u32[]{:S(2)}) %collective-permute-start.18) | collective-permute-done | bytes 262176 | tf_op jit(solution)/shard_map/sum_x/ppermute | solution.py:175
  172.8 12.4 %all_to_all.25 = bf16[8,16,1024]{2,1,0:T(8,128)(2,1)S(1)} all-to-all(bf16[8,16,1024]{2,1,0:T(8,128)(2,1)S(1)} %bitcast.36), channel_id=1, replica_groups=mesh['za'=2,'zb'=2,'zq'=2,'y'=4,'zh'=2,'x'=4,'c'=2] {'zb','zq','c'}, dimensions={0} | all-to-all | bytes 524288 | tf_op jit(solution)/shard_map/columns/all_to_all | solution.py:259
  (59 shorter events, 22.6 us)
Async XLA Ops:
  0.0 27.8 %copy-start.7 = (bf16[512,256]{1,0:T(8,128)(2,1)S(1)}, bf16[512,256]{1,0:T(8,128)(2,1)}, u32[]{:S(2)}) copy-start(bf16[512,256]{1,0:T(8,128)(2,1)} %param.11) | copy-start | bytes 786436
  1.3 24.5 %collective-permute-start = (bf16[256,128]{1,0:T(8,128)(2,1)S(1)}, bf16[256,128]{1,0:T(8,128)(2,1)S(1)}, u32[]{:S(2)}, u32[]{:S(2)}) collective-permute-start(bf16[256,128]{1,0:T(8,128)(2,1)S(1)} %get-tuple-element.34), channel_id=1, source_target_pairs={{0,392},{1,393},{64,456},{65,457},{128,0},{129,1},{192,64},{193,65... | collective-permute-start | bytes 196616 | tf_op jit(solution)/shard_map/cache_gather/ppermute | solution.py:183
  13.2 12.6 %collective-permute-start.1 = (bf16[256,128]{1,0:T(8,128)(2,1)S(1)}, bf16[256,128]{1,0:T(8,128)(2,1)S(1)}, u32[]{:S(2)}, u32[]{:S(2)}) collective-permute-start(bf16[256,128]{1,0:T(8,128)(2,1)S(1)} %get-tuple-element.33), channel_id=1, source_target_pairs={{0,128},{1,129},{64,192},{65,193},{128,256},{129,257},{192,320},{1... | collective-permute-start | bytes 196616 | tf_op jit(solution)/shard_map/cache_gather/ppermute | solution.py:183
  15.1 14.7 %collective-permute-start.2 = (bf16[256,128]{1,0:T(8,128)(2,1)S(1)}, bf16[256,128]{1,0:T(8,128)(2,1)S(1)}, u32[]{:S(2)}, u32[]{:S(2)}) collective-permute-start(bf16[256,128]{1,0:T(8,128)(2,1)S(1)} %get-tuple-element.36), channel_id=1, source_target_pairs={{0,264},{1,257},{64,328},{65,321},{128,392},{129,385},{192,456},{1... | collective-permute-start | bytes 196616 | tf_op jit(solution)/shard_map/cache_gather/ppermute | solution.py:183
  21.0 12.8 %collective-permute-start.4 = (bf16[256,128]{1,0:T(8,128)(2,1)S(1)}, bf16[256,128]{1,0:T(8,128)(2,1)S(1)}, u32[]{:S(2)}, u32[]{:S(2)}) collective-permute-start(bf16[256,128]{1,0:T(8,128)(2,1)S(1)} %get-tuple-element.32), channel_id=1, source_target_pairs={{0,328},{1,329},{64,256},{65,257},{128,456},{129,457},{192,384},{1... | collective-permute-start | bytes 196616 | tf_op jit(solution)/shard_map/cache_gather/ppermute | solution.py:183
  25.9 7.9 %collective-permute-start.3 = (bf16[768,128]{1,0:T(8,128)(2,1)S(1)}, bf16[768,128]{1,0:T(8,128)(2,1)S(1)}, u32[]{:S(2)}, u32[]{:S(2)}) collective-permute-start(bf16[768,128]{1,0:T(8,128)(2,1)S(1)} %pad_maximum_fusion.4), channel_id=1, source_target_pairs={{0,64},{64,0},{1,65},{65,1},{2,66},{66,2},{3,67},{67,3},{4,68},{68... | collective-permute-start | bytes 589832 | tf_op jit(solution)/shard_map/cache_gather/ppermute | solution.py:167
  27.8 3.2 %collective-permute-start.5 = (bf16[512,128]{1,0:T(8,128)(2,1)S(1)}, bf16[512,128]{1,0:T(8,128)(2,1)S(1)}, u32[]{:S(2)}, u32[]{:S(2)}) collective-permute-start(bf16[512,128]{1,0:T(8,128)(2,1)S(1)} %get-tuple-element.44), channel_id=1, source_target_pairs={{0,1},{1,0},{2,3},{3,2},{4,5},{5,4},{6,7},{7,6},{8,9},{9,8},{10,11... | collective-permute-start | bytes 393224 | tf_op jit(solution)/shard_map/weight_gather/ppermute | solution.py:167
  35.4 33.6 %all-to-all-start = ((bf16[4,2048,128]{2,1,0:T(8,128)(2,1)}), bf16[4,2048,128]{2,1,0:T(8,128)(2,1)}, u32[]{:S(2)}, u32[]{:S(2)}) async-start(bf16[4,2048,128]{2,1,0:T(8,128)(2,1)} %broadcast_in_dim.6), calls=%async_computation | async-start | bytes 4194304 | tf_op jit(solution)/shard_map/cache_gather/all_to_all | solution.py:163
  40.2 28.8 %collective-permute-start.6 = (bf16[1024,128]{1,0:T(8,128)(2,1)S(1)}, bf16[1024,128]{1,0:T(8,128)(2,1)S(1)}, u32[]{:S(2)}, u32[]{:S(2)}) collective-permute-start(bf16[1024,128]{1,0:T(8,128)(2,1)S(1)} %pad_maximum_fusion.3), channel_id=1, source_target_pairs={{0,256},{256,0},{1,257},{257,1},{2,258},{258,2},{3,259},{259,3},{4... | collective-permute-start | bytes 786440 | tf_op jit(solution)/shard_map/weight_gather/ppermute | solution.py:167
  69.0 8.7 %collective-permute-start.7 = (bf16[8192,128]{1,0:T(8,128)(2,1)}, bf16[8192,128]{1,0:T(8,128)(2,1)}, u32[]{:S(2)}, u32[]{:S(2)}) collective-permute-start(bf16[8192,128]{1,0:T(8,128)(2,1)} %bitcast.4.own_ref), channel_id=1, source_target_pairs={{0,1},{1,0},{2,3},{3,2},{4,5},{5,4},{6,7},{7,6},{8,9},{9,8},{10,11... | collective-permute-start | bytes 6291464 | tf_op jit(solution)/shard_map/cache_gather/ppermute | solution.py:167
  72.7 5.0 %copy-start.4 = (bf16[256,512]{1,0:T(8,128)(2,1)S(1)}, bf16[256,512]{1,0:T(8,128)(2,1)}, u32[]{:S(2)}) copy-start(bf16[256,512]{1,0:T(8,128)(2,1)} %q_ref.1) | copy-start | bytes 786436
  72.7 5.0 %copy-start.5 = (s32[32]{0:T(128)S(1)}, s32[32]{0:T(128)}, u32[]{:S(2)}) copy-start(s32[32]{0:T(128)} %counts.1) | copy-start | bytes 388
  72.7 5.0 %copy-start.6 = (s32[64]{0:T(128)S(1)}, s32[64]{0:T(128)}, u32[]{:S(2)}) copy-start(s32[64]{0:T(128)} %order.1) | copy-start | bytes 772
  72.7 34.4 %all-to-all-start.1 = ((bf16[4,2,1024,128]{3,2,1,0:T(8,128)(2,1)}), bf16[4,2,1024,128]{3,2,1,0:T(8,128)(2,1)S(1)}, u32[]{:S(2)}, u32[]{:S(2)}) async-start(bf16[4,2,1024,128]{3,2,1,0:T(8,128)(2,1)} %broadcast_in_dim.7), calls=%async_computation.1 | async-start | bytes 4194304 | tf_op jit(solution)/shard_map/weight_gather/all_to_all | solution.py:163
  89.2 10.1 %collective-permute-start.8 = (bf16[4,32,512]{2,1,0:T(8,128)(2,1)S(1)}, bf16[4,32,512]{2,1,0:T(8,128)(2,1)S(1)}, u32[]{:S(2)}, u32[]{:S(2)}) collective-permute-start(bf16[4,32,512]{2,1,0:T(8,128)(2,1)S(1)} %get-tuple-element.40), channel_id=1, source_target_pairs={{0,192},{64,128},{128,64},{192,0},{1,193},{65,129},{129,65},{193,1... | collective-permute-start | bytes 393224 | tf_op jit(solution)/shard_map/rows_gather/ppermute | solution.py:171
  91.1 12.8 %collective-permute-start.9 = (bf16[4,32,512]{2,1,0:T(8,128)(2,1)S(1)}, bf16[4,32,512]{2,1,0:T(8,128)(2,1)S(1)}, u32[]{:S(2)}, u32[]{:S(2)}) collective-permute-start(bf16[4,32,512]{2,1,0:T(8,128)(2,1)S(1)} %get-tuple-element.40), channel_id=1, source_target_pairs={{0,128},{64,192},{128,0},{192,64},{1,129},{65,193},{129,1},{193,65... | collective-permute-start | bytes 393224 | tf_op jit(solution)/shard_map/rows_gather/ppermute | solution.py:171
  93.1 12.0 %collective-permute-start.10 = (bf16[4,32,512]{2,1,0:T(8,128)(2,1)S(1)}, bf16[4,32,512]{2,1,0:T(8,128)(2,1)S(1)}, u32[]{:S(2)}, u32[]{:S(2)}) collective-permute-start(bf16[4,32,512]{2,1,0:T(8,128)(2,1)S(1)} %get-tuple-element.40), channel_id=1, source_target_pairs={{0,64},{64,0},{128,192},{192,128},{1,65},{65,1},{129,193},{193,129... | collective-permute-start | bytes 393224 | tf_op jit(solution)/shard_map/rows_gather/ppermute | solution.py:171
  105.2 3.8 %collective-permute-start.11 = (bf16[4,4,32,512]{3,2,1,0:T(8,128)(2,1)S(1)}, bf16[4,4,32,512]{3,2,1,0:T(8,128)(2,1)S(1)}, u32[]{:S(2)}, u32[]{:S(2)}) collective-permute-start(bf16[4,4,32,512]{3,2,1,0:T(8,128)(2,1)S(1)} %pad_maximum_fusion.a_ref), channel_id=1, source_target_pairs={{0,1},{1,0},{2,3},{3,2},{4,5},{5,4},{6,7},{7,6},{8,9},{9,8},{10,11... | collective-permute-start | bytes 1572872 | tf_op jit(solution)/shard_map/rows_gather/ppermute | solution.py:167
  111.8 20.6 %all-to-all-start.2 = ((bf16[4,4,32,1024]{3,2,1,0:T(8,128)(2,1)}), bf16[4,4,32,1024]{3,2,1,0:T(8,128)(2,1)}, u32[]{:S(2)}, u32[]{:S(2)}) async-start(bf16[4,4,32,1024]{3,2,1,0:T(8,128)(2,1)} %projection.2), calls=%async_computation.2 | async-start | bytes 2097152 | tf_op jit(solution)/shard_map/sum_x/all_to_all | solution.py:244
  116.6 10.1 %collective-permute-start.12 = (bf16[4,32,512]{2,1,0:T(8,128)(2,1)S(1)}, bf16[4,32,512]{2,1,0:T(8,128)(2,1)S(1)}, u32[]{:S(2)}, u32[]{:S(2)}) collective-permute-start(bf16[4,32,512]{2,1,0:T(8,128)(2,1)S(1)} %get-tuple-element.41), channel_id=1, source_target_pairs={{0,192},{64,128},{128,64},{192,0},{1,193},{65,129},{129,65},{193,1... | collective-permute-start | bytes 393224 | tf_op jit(solution)/shard_map/rows_gather/ppermute | solution.py:171
  120.0 11.2 %collective-permute-start.13 = (bf16[4,32,512]{2,1,0:T(8,128)(2,1)S(1)}, bf16[4,32,512]{2,1,0:T(8,128)(2,1)S(1)}, u32[]{:S(2)}, u32[]{:S(2)}) collective-permute-start(bf16[4,32,512]{2,1,0:T(8,128)(2,1)S(1)} %get-tuple-element.41), channel_id=1, source_target_pairs={{0,128},{64,192},{128,0},{192,64},{1,129},{65,193},{129,1},{193,65... | collective-permute-start | bytes 393224 | tf_op jit(solution)/shard_map/rows_gather/ppermute | solution.py:171
  121.9 10.4 %collective-permute-start.14 = (bf16[4,32,512]{2,1,0:T(8,128)(2,1)S(1)}, bf16[4,32,512]{2,1,0:T(8,128)(2,1)S(1)}, u32[]{:S(2)}, u32[]{:S(2)}) collective-permute-start(bf16[4,32,512]{2,1,0:T(8,128)(2,1)S(1)} %get-tuple-element.41), channel_id=1, source_target_pairs={{0,64},{64,0},{128,192},{192,128},{1,65},{65,1},{129,193},{193,129... | collective-permute-start | bytes 393224 | tf_op jit(solution)/shard_map/rows_gather/ppermute | solution.py:171
  132.4 12.1 %copy-start = (bf16[4,4,32,512]{3,2,1,0:T(8,128)(2,1)}, bf16[4,4,32,512]{3,2,1,0:T(8,128)(2,1)S(1)}, u32[]{:S(2)}) copy-start(bf16[4,4,32,512]{3,2,1,0:T(8,128)(2,1)S(1)} %pad_maximum_fusion.2.a_ref) | copy-start | bytes 1572868
  134.9 36.7 %all-to-all-start.3 = ((bf16[2,4,32,1024]{3,2,1,0:T(8,128)(2,1)}), bf16[2,4,32,1024]{3,2,1,0:T(8,128)(2,1)}, u32[]{:S(2)}, u32[]{:S(2)}) async-start(bf16[2,4,32,1024]{3,2,1,0:T(8,128)(2,1)} %broadcast_in_dim.8), calls=%async_computation.3 | async-start | bytes 1048576 | tf_op jit(solution)/shard_map/sum_zh/all_to_all | solution.py:250
  142.5 3.8 %collective-permute-start.15 = (bf16[4,4,32,512]{3,2,1,0:T(8,128)(2,1)S(1)}, bf16[4,4,32,512]{3,2,1,0:T(8,128)(2,1)S(1)}, u32[]{:S(2)}, u32[]{:S(2)}) collective-permute-start(bf16[4,4,32,512]{3,2,1,0:T(8,128)(2,1)S(1)} %pad_maximum_fusion.2.a_ref), channel_id=1, source_target_pairs={{0,1},{1,0},{2,3},{3,2},{4,5},{5,4},{6,7},{7,6},{8,9},{9,8},{10,11... | collective-permute-start | bytes 1572872 | tf_op jit(solution)/shard_map/sum_x/ppermute | solution.py:167
  146.3 0.8 copy-start.2
  147.1 1.0 copy-start.1
  148.2 1.0 copy-start.3
  151.2 11.0 %collective-permute-start.16 = (bf16[4,32,1024]{2,1,0:T(8,128)(2,1)S(1)}, bf16[4,32,1024]{2,1,0:T(8,128)(2,1)S(1)}, u32[]{:S(2)}, u32[]{:S(2)}) collective-permute-start(bf16[4,32,1024]{2,1,0:T(8,128)(2,1)S(1)} %get-tuple-element.29), channel_id=1, source_target_pairs={{6,0},{0,2},{2,4},{4,6},{7,1},{1,3},{3,5},{5,7},{14,8},{8,10},{10,... | collective-permute-start | bytes 786440 | tf_op jit(solution)/shard_map/sum_x/ppermute | solution.py:175
  154.6 12.6 %collective-permute-start.17 = (bf16[4,32,1024]{2,1,0:T(8,128)(2,1)S(1)}, bf16[4,32,1024]{2,1,0:T(8,128)(2,1)S(1)}, u32[]{:S(2)}, u32[]{:S(2)}) collective-permute-start(bf16[4,32,1024]{2,1,0:T(8,128)(2,1)S(1)} %get-tuple-element.31), channel_id=1, source_target_pairs={{4,0},{6,2},{0,4},{2,6},{5,1},{7,3},{1,5},{3,7},{12,8},{14,10},{8,... | collective-permute-start | bytes 786440 | tf_op jit(solution)/shard_map/sum_x/ppermute | solution.py:175
  157.4 14.3 %collective-permute-start.18 = (bf16[4,32,1024]{2,1,0:T(8,128)(2,1)S(1)}, bf16[4,32,1024]{2,1,0:T(8,128)(2,1)S(1)}, u32[]{:S(2)}, u32[]{:S(2)}) collective-permute-start(bf16[4,32,1024]{2,1,0:T(8,128)(2,1)S(1)} %get-tuple-element.30), channel_id=1, source_target_pairs={{2,0},{4,2},{6,4},{0,6},{3,1},{5,3},{7,5},{1,7},{10,8},{12,10},{14... | collective-permute-start | bytes 786440 | tf_op jit(solution)/shard_map/sum_x/ppermute | solution.py:175

commit v6 on v5

--- a/solution.py
+++ b/solution.py
@@ -25,7 +25,6 @@
 def attention_kernel(counts, order, place, q_ref, own_ref, other_ref, o_ref, k_sc, v_sc):
     me = place[0]
     core = place[1]
-    my_zh = place[2]
     my_z = me // Y
 
     def sort_pages(k_ref, v_ref):
@@ -44,66 +43,53 @@
 
         lax.fori_loop(0, PAGES, one, (jnp.int32(0), jnp.int32(0)), unroll=4)
 
-    @pl.when(core == 0)
+    before = lax.fori_loop(0, me, lambda d, s: s + counts[d], jnp.int32(0))
+    live = counts[me]
+    head = place[2] * 2
+
+    @pl.when((head < live) & (core == 0))
     def _():
         sort_pages(own_ref, other_ref)
 
-    @pl.when(core == 1)
+    @pl.when((head < live) & (core == 1))
     def _():
         sort_pages(other_ref, own_ref)
 
-    before = lax.fori_loop(0, me, lambda d, s: s + counts[d], jnp.int32(0))
-    live = counts[me]
-
-    def store(j, rows):
-        kept = (my_zh == j // 2).astype(jnp.int32)
+    def store(i, rows):
         for b in range(2):
             for h in range(HEADS):
-                o_ref[kept, 2 * (j % 2) + b, :, h * HD : (h + 1) * HD] = rows(h, b)
-
-    for j in range(SLOTS):
+                o_ref[2 * i + b, :, h * HD : (h + 1) * HD] = rows(h, b)
+
+    for i in range(2):
+        j = head + i
+        here = pl.ds(pl.multiple_of(j * PAGE, PAGE), PAGE)
 
         @pl.when(j < live)
         def _():
             page = order[before + j]
-            groups = 1
-            count = HEADS // groups
-            q = [
-                jnp.concatenate(
-                    [q_ref[j * PAGE : (j + 1) * PAGE, h * HD : (h + 1) * HD] for h in range(g * count, (g + 1) * count)],
-                    axis=0,
-                )
-                for g in range(groups)
-            ]
-            size = count * PAGE
-
-            def step(at, state, last, CHUNK):
-                k = k_sc[pl.ds(at, CHUNK), :]
-                v = v_sc[pl.ds(at, CHUNK), :]
-                if last:
-                    row = lax.broadcasted_iota(jnp.int32, (size, CHUNK), 0) % PAGE + page * PAGE
-                    seen = lax.broadcasted_iota(jnp.int32, (size, CHUNK), 1) + at <= row
-                out = []
-                for g in range(groups):
-                    best, total, accum = state[g]
-                    s = lax.dot_general(q[g], k, (((1,), (1,)), ((), ())), preferred_element_type=jnp.float32)
-                    if last:
-                        s = jnp.where(seen, s, jnp.float32(-1e30))
-                    new = jnp.maximum(best, jnp.max(s, axis=1, keepdims=True))
-                    p = jnp.exp2((s - new) * SCALE)
-                    fade = jnp.exp2((best - new) * SCALE)
-                    total = total * fade + jnp.sum(p, axis=1, keepdims=True)
-                    accum = accum * fade + jnp.dot(p.astype(jnp.bfloat16), v, preferred_element_type=jnp.float32)
-                    out.append((new, total, accum))
-                return tuple(out)
-
-            state = tuple(
-                (
-                    jnp.full((size, 1), -1e30, jnp.float32),
-                    jnp.zeros((size, 1), jnp.float32),
-                    jnp.zeros((size, HD), jnp.float32),
-                )
-                for _ in range(groups)
+            q = jnp.concatenate([q_ref[here, h * HD : (h + 1) * HD] for h in range(HEADS)], axis=0)
+            size = HEADS * PAGE
+
+            def step(at, state, masked, width):
+                best, total, accum = state
+                k = k_sc[pl.ds(at, width), :]
+                v = v_sc[pl.ds(at, width), :]
+                s = lax.dot_general(q, k, (((1,), (1,)), ((), ())), preferred_element_type=jnp.float32)
+                if masked:
+                    row = lax.broadcasted_iota(jnp.int32, s.shape, 0) % PAGE + page * PAGE
+                    seen = lax.broadcasted_iota(jnp.int32, s.shape, 1) + at <= row
+                    s = jnp.where(seen, s, jnp.float32(-1e30))
+                new = jnp.maximum(best, jnp.max(s, axis=1, keepdims=True))
+                p = jnp.exp2((s - new) * SCALE)
+                fade = jnp.exp2((best - new) * SCALE)
+                total = total * fade + jnp.sum(p, axis=1, keepdims=True)
+                accum = accum * fade + jnp.dot(p.astype(jnp.bfloat16), v, preferred_element_type=jnp.float32)
+                return new, total, accum
+
+            state = (
+                jnp.full((size, 1), -1e30, jnp.float32),
+                jnp.zeros((size, 1), jnp.float32),
+                jnp.zeros((size, HD), jnp.float32),
             )
             full = page // (CHUNK // PAGE)
             state = lax.fori_loop(
@@ -116,12 +102,13 @@
                 lambda s: step(rest, s, True, CHUNK),
                 state,
             )
-            out = jnp.concatenate([(accum / total).astype(jnp.bfloat16) for _, total, accum in state], axis=0)
-            store(j, lambda h, b: out[h * PAGE + b * 32 : h * PAGE + b * 32 + 32, :])
+            _, total, accum = state
+            out = (accum / total).astype(jnp.bfloat16)
+            store(i, lambda h, b: out[h * PAGE + b * 32 : h * PAGE + b * 32 + 32, :])
 
         @pl.when(j >= live)
         def _():
-            store(j, lambda h, b: jnp.zeros((32, HD), jnp.bfloat16))
+            store(i, lambda h, b: jnp.zeros((32, HD), jnp.bfloat16))
 
 
 def attend(counts, order, place, q, own, other):
@@ -129,7 +116,7 @@
     vmem = pl.BlockSpec(memory_space=pltpu.VMEM)
     return pl.pallas_call(
         attention_kernel,
-        out_shape=jax.ShapeDtypeStruct((ZH, X, 32, HEADS * HD), jnp.bfloat16),
+        out_shape=jax.ShapeDtypeStruct((X, 32, HEADS * HD), jnp.bfloat16),
         in_specs=[smem, smem, smem, vmem, vmem, vmem],
         out_specs=vmem,
         scratch_shapes=[pltpu.VMEM((PAGES * PAGE, HD), jnp.bfloat16) for _ in range(2)],
@@ -157,6 +144,25 @@
         out_specs=pl.BlockSpec((X, QUAD, 32, 2 * HD), lambda i: (0, 0, 0, i)),
         compiler_params=pltpu.CompilerParams(vmem_limit_bytes=24 << 20),
     )(me, a, b, w)
+
+
+def add_kernel(p_ref, o_ref):
+    total = p_ref[0].astype(jnp.float32)
+    for i in range(1, X):
+        total += p_ref[i].astype(jnp.float32)
+    o_ref[0] = total.astype(jnp.bfloat16)
+    o_ref[1] = total.astype(jnp.bfloat16)
+
+
+def add_parts(parts):
+    return pl.pallas_call(
+        add_kernel,
+        grid=(QUAD,),
+        out_shape=jax.ShapeDtypeStruct((ZH, *parts.shape[1:]), jnp.bfloat16),
+        in_specs=[pl.BlockSpec((X, 1, *parts.shape[2:]), lambda i: (0, i, 0, 0))],
+        out_specs=pl.BlockSpec((ZH, 1, *parts.shape[2:]), lambda i: (0, i, 0, 0)),
+        compiler_params=pltpu.CompilerParams(vmem_limit_bytes=16 << 20),
+    )(parts)
 
 
 def spread(piece, axis, count):
@@ -222,8 +228,10 @@
         wide = jnp.stack([jnp.where(za == 0, narrow, facing), jnp.where(za == 0, facing, narrow)])
         wide = spread(wide, "y", Y)
     with jax.named_scope("attention"):
-        place = jnp.stack([zl * Y + y, c, zh]).astype(jnp.int32)
-        heads = attend(counts, order, place, queries, own, other)
+        heads = [
+            attend(counts, order, jnp.stack([zl * Y + y, c, half]).astype(jnp.int32), queries, own, other)
+            for half in (1 - zh, zh)
+        ]
 
     def projected(mine, theirs):
         with jax.named_scope("projection"):
@@ -233,17 +241,18 @@
     def part_of(parts, shift):
         return lax.dynamic_index_in_dim(parts, (x + shift) % X, 0, keepdims=False)
 
+    def gather_rows(rows):
+        return jnp.stack([rows] + [quad(rows, step) for step in range(QUAD - 1, 0, -1)])
+
     with jax.named_scope("rows_gather"):
-        first, second = (
-            jnp.stack([rows] + [quad(rows, step) for step in range(QUAD - 1, 0, -1)]) for rows in heads
-        )
+        first = gather_rows(heads[0])
+        first, later = lax.optimization_barrier((first, heads[1]))
         theirs = swap(first, "c")
         first, theirs, wide = lax.optimization_barrier((first, theirs, wide))
+        second = gather_rows(later)
     parts = projected(first, theirs)
     with jax.named_scope("sum_x"):
-        away = lax.all_to_all(parts, "x", 0, 0)
-        away = jnp.sum(away.astype(jnp.float32), axis=0).astype(jnp.bfloat16)
-        away = jnp.broadcast_to(away[None], (ZH, *away.shape))
+        away = add_parts(lax.all_to_all(parts, "x", 0, 0))
         away, second = lax.optimization_barrier((away, second))
         theirs = swap(second, "c")
     with jax.named_scope("sum_zh"):

time: 188 us -> 184 us (0.979)
  the two profiles are of different devices: /device:TPU:18 before, /device:TPU:1 now
where the time goes in v6:
time: 184 us; the launch traced here: 182 us
  starting transfers between devices  94.4 us (51%)
  waiting for transfers between devices  47.3 us (26%)
  blocking collectives  14 us (8%)
  Pallas kernels  13.2 us (7%)
  local copies, waits for them, and re-layouts  8.44 us (5%)
  other arithmetic  3.65 us (2%)
    ppermute x6, waiting for transfers between devices, swap(): return lax.ppermute(piece, axis, [(0, 1), (1, 0)])  29.2 us
    ppermute x4, starting transfers between devices, along(): return lax.ppermute(piece, LINE, perm)  23.1 us
    ppermute x6, starting transfers between devices, swap(): return lax.ppermute(piece, axis, [(0, 1), (1, 0)])  21 us
    ppermute x6, starting transfers between devices, quad(): lax.ppermute(piece, ('zb', 'zq'), [(i, i ^ step) for i in range(QUAD)])  18.5 us
    all_to_all x1, blocking collectives, body(): lax.all_to_all(mixed.reshape(QUAD * C, 16, ZL * HD), ('zb', 'zq', 'c'), 0...  14 us
    ppermute x3, starting transfers between devices, around(): lax.ppermute(piece, axis, [((i + shift) % count, i) for i in range(count)])  10.9 us
    all_to_all x2, starting transfers between devices, spread(): lax.all_to_all(jnp.broadcast_to(piece[None], (count, *piece.shape)), axis...  8.76 us
    pallas_call x2, Pallas kernels, attend(): pl.pallas_call(attention_kernel, out_shape=jax.ShapeDtypeStruct((X, 32, H...  8.22 us
  transfers between devices with their start and end apart: 23, of which 9 were waited for; matrix products, arithmetic and copies ran while one was open for 2% of the time, Pallas kernels for 6%

profile of v6, /device:TPU:1, one launch (start us, length us, event | category | flops | bytes accessed | tf_op | source)
XLA Modules:
  0.0 181.5 jit_solution(12349749491058712553)
XLA Ops:
  1.3 12.4 %collective-permute-start = (bf16[256,128]{1,0:T(8,128)(2,1)S(1)}, bf16[256,128]{1,0:T(8,128)(2,1)S(1)}, u32[]{:S(2)}, u32[]{:S(2)}) collective-permute-start(bf16[256,128]{1,0:T(8,128)(2,1)S(1)} %get-tuple-element.38), channel_id=1, source_target_pairs={{0,392},{1,393},{64,456},{65,457},{128,0},{129,1},{192,64},{193,65... | collective-permute-start | bytes 196616 | tf_op jit(solution)/shard_map/cache_gather/ppermute | solution.py:189
  13.7 1.9 %collective-permute-start.1 = (bf16[256,128]{1,0:T(8,128)(2,1)S(1)}, bf16[256,128]{1,0:T(8,128)(2,1)S(1)}, u32[]{:S(2)}, u32[]{:S(2)}) collective-permute-start(bf16[256,128]{1,0:T(8,128)(2,1)S(1)} %get-tuple-element.37), channel_id=1, source_target_pairs={{0,128},{1,129},{64,192},{65,193},{128,256},{129,257},{192,320},{1... | collective-permute-start | bytes 196616 | tf_op jit(solution)/shard_map/cache_gather/ppermute | solution.py:189
  15.6 2.2 %collective-permute-start.2 = (bf16[256,128]{1,0:T(8,128)(2,1)S(1)}, bf16[256,128]{1,0:T(8,128)(2,1)S(1)}, u32[]{:S(2)}, u32[]{:S(2)}) collective-permute-start(bf16[256,128]{1,0:T(8,128)(2,1)S(1)} %get-tuple-element.40), channel_id=1, source_target_pairs={{0,264},{1,257},{64,328},{65,321},{128,392},{129,385},{192,456},{1... | collective-permute-start | bytes 196616 | tf_op jit(solution)/shard_map/cache_gather/ppermute | solution.py:189
  17.8 6.6 %collective-permute-start.4 = (bf16[256,128]{1,0:T(8,128)(2,1)S(1)}, bf16[256,128]{1,0:T(8,128)(2,1)S(1)}, u32[]{:S(2)}, u32[]{:S(2)}) collective-permute-start(bf16[256,128]{1,0:T(8,128)(2,1)S(1)} %get-tuple-element.36), channel_id=1, source_target_pairs={{0,328},{1,329},{64,256},{65,257},{128,456},{129,457},{192,384},{1... | collective-permute-start | bytes 196616 | tf_op jit(solution)/shard_map/cache_gather/ppermute | solution.py:189
  24.4 3.8 %collective-permute-start.3 = (bf16[768,128]{1,0:T(8,128)(2,1)S(1)}, bf16[768,128]{1,0:T(8,128)(2,1)S(1)}, u32[]{:S(2)}, u32[]{:S(2)}) collective-permute-start(bf16[768,128]{1,0:T(8,128)(2,1)S(1)} %pad_maximum_fusion.4), channel_id=1, source_target_pairs={{0,64},{64,0},{1,65},{65,1},{2,66},{66,2},{3,67},{67,3},{4,68},{68... | collective-permute-start | bytes 589832 | tf_op jit(solution)/shard_map/cache_gather/ppermute | solution.py:173
  28.3 3.0 %collective-permute-start.5 = (bf16[512,128]{1,0:T(8,128)(2,1)S(1)}, bf16[512,128]{1,0:T(8,128)(2,1)S(1)}, u32[]{:S(2)}, u32[]{:S(2)}) collective-permute-start(bf16[512,128]{1,0:T(8,128)(2,1)S(1)} %get-tuple-element.44), channel_id=1, source_target_pairs={{0,1},{1,0},{2,3},{3,2},{4,5},{5,4},{6,7},{7,6},{8,9},{9,8},{10,11... | collective-permute-start | bytes 393224 | tf_op jit(solution)/shard_map/weight_gather/ppermute | solution.py:173
  34.7 4.4 %all-to-all-start = ((bf16[4,2048,128]{2,1,0:T(8,128)(2,1)}), bf16[4,2048,128]{2,1,0:T(8,128)(2,1)}, u32[]{:S(2)}, u32[]{:S(2)}) async-start(bf16[4,2048,128]{2,1,0:T(8,128)(2,1)} %broadcast_in_dim.4), calls=%async_computation | async-start | bytes 4194304 | tf_op jit(solution)/shard_map/cache_gather/all_to_all | solution.py:169
  39.2 3.7 %collective-permute-start.6 = (bf16[1024,128]{1,0:T(8,128)(2,1)S(1)}, bf16[1024,128]{1,0:T(8,128)(2,1)S(1)}, u32[]{:S(2)}, u32[]{:S(2)}) collective-permute-start(bf16[1024,128]{1,0:T(8,128)(2,1)S(1)} %pad_maximum_fusion.3), channel_id=1, source_target_pairs={{0,256},{256,0},{1,257},{257,1},{2,258},{258,2},{3,259},{259,3},{4... | collective-permute-start | bytes 786440 | tf_op jit(solution)/shard_map/weight_gather/ppermute | solution.py:173
  42.9 25.8 %collective-permute-done.6 = bf16[1024,128]{1,0:T(8,128)(2,1)S(1)} collective-permute-done((bf16[1024,128]{1,0:T(8,128)(2,1)S(1)}, bf16[1024,128]{1,0:T(8,128)(2,1)S(1)}, u32[]{:S(2)}, u32[]{:S(2)}) %collective-permute-start.6) | collective-permute-done | bytes 262176 | tf_op jit(solution)/shard_map/weight_gather/ppermute | solution.py:173
  68.7 3.8 %collective-permute-start.7 = (bf16[8192,128]{1,0:T(8,128)(2,1)}, bf16[8192,128]{1,0:T(8,128)(2,1)}, u32[]{:S(2)}, u32[]{:S(2)}) collective-permute-start(bf16[8192,128]{1,0:T(8,128)(2,1)} %bitcast.4.own_ref), channel_id=1, source_target_pairs={{0,1},{1,0},{2,3},{3,2},{4,5},{5,4},{6,7},{7,6},{8,9},{9,8},{10,11... | collective-permute-start | bytes 6291464 | tf_op jit(solution)/shard_map/cache_gather/ppermute | solution.py:173
  74.2 4.3 %all-to-all-start.1 = ((bf16[4,2,1024,128]{3,2,1,0:T(8,128)(2,1)}), bf16[4,2,1024,128]{3,2,1,0:T(8,128)(2,1)S(1)}, u32[]{:S(2)}, u32[]{:S(2)}) async-start(bf16[4,2,1024,128]{3,2,1,0:T(8,128)(2,1)} %broadcast_in_dim.5), calls=%async_computation.1 | async-start | bytes 4194304 | tf_op jit(solution)/shard_map/weight_gather/all_to_all | solution.py:169
  78.6 2.3 %attention.2 = bf16[4,32,512]{2,1,0:T(8,128)(2,1)S(1)} custom-call(s32[32]{0:T(128)S(1)} %copy-done.5, s32[64]{0:T(128)S(1)} %copy-done.6, s32[3]{0:T(128)S(1)} %pad_add_fusion.place, bf16[256,512]{1,0:T(8,128)(2,1)S(1)} %copy-done.2, bf16[8192,128]{1,0:T(8,128)(2,1)} %bitcast.4.own_ref, bf16[8192,128]{1,0:T(8,128)(2,1)} %collective-permute-done.7.other_ref), custom_call_target="tpu_custom_call" | custom-call | tf_op jit(solution)/shard_map/attention/pallas_call | solution.py:117
  80.9 1.9 %collective-permute-start.8 = (bf16[4,32,512]{2,1,0:T(8,128)(2,1)S(1)}, bf16[4,32,512]{2,1,0:T(8,128)(2,1)S(1)}, u32[]{:S(2)}, u32[]{:S(2)}) collective-permute-start(bf16[4,32,512]{2,1,0:T(8,128)(2,1)S(1)} %attention.2), channel_id=1, source_target_pairs={{0,192},{64,128},{128,64},{192,0},{1,193},{65,129},{129,65},{193,1... | collective-permute-start | bytes 393224 | tf_op jit(solution)/shard_map/rows_gather/ppermute | solution.py:177
  82.9 1.9 %collective-permute-start.9 = (bf16[4,32,512]{2,1,0:T(8,128)(2,1)S(1)}, bf16[4,32,512]{2,1,0:T(8,128)(2,1)S(1)}, u32[]{:S(2)}, u32[]{:S(2)}) collective-permute-start(bf16[4,32,512]{2,1,0:T(8,128)(2,1)S(1)} %attention.2), channel_id=1, source_target_pairs={{0,128},{64,192},{128,0},{192,64},{1,129},{65,193},{129,1},{193,65... | collective-permute-start | bytes 393224 | tf_op jit(solution)/shard_map/rows_gather/ppermute | solution.py:177
  84.8 5.4 %collective-permute-start.10 = (bf16[4,32,512]{2,1,0:T(8,128)(2,1)S(1)}, bf16[4,32,512]{2,1,0:T(8,128)(2,1)S(1)}, u32[]{:S(2)}, u32[]{:S(2)}) collective-permute-start(bf16[4,32,512]{2,1,0:T(8,128)(2,1)S(1)} %attention.2), channel_id=1, source_target_pairs={{0,64},{64,0},{128,192},{192,128},{1,65},{65,1},{129,193},{193,129... | collective-permute-start | bytes 393224 | tf_op jit(solution)/shard_map/rows_gather/ppermute | solution.py:177
  90.3 5.9 %attention.3 = bf16[4,32,512]{2,1,0:T(8,128)(2,1)S(1)} custom-call(s32[32]{0:T(128)S(1)} %copy-done.5, s32[64]{0:T(128)S(1)} %copy-done.6, s32[3]{0:T(128)S(1)} %pad_add_fusion.2.place, bf16[256,512]{1,0:T(8,128)(2,1)S(1)} %copy-done.2, bf16[8192,128]{1,0:T(8,128)(2,1)} %bitcast.4.own_ref, bf16[8192,128]{1,0:T(8,128)(2,1)} %collective-permute-done.7.other_ref), custom_call_target="tpu_custom_call" | custom-call | tf_op jit(solution)/shard_map/attention/pallas_call | solution.py:117
  96.4 3.0 %collective-permute-start.11 = (bf16[4,4,32,512]{3,2,1,0:T(8,128)(2,1)S(1)}, bf16[4,4,32,512]{3,2,1,0:T(8,128)(2,1)S(1)}, u32[]{:S(2)}, u32[]{:S(2)}) collective-permute-start(bf16[4,4,32,512]{3,2,1,0:T(8,128)(2,1)S(1)} %pad_maximum_fusion.a_ref), channel_id=1, source_target_pairs={{0,1},{1,0},{2,3},{3,2},{4,5},{5,4},{6,7},{7,6},{8,9},{9,8},{10,11... | collective-permute-start | bytes 1572872 | tf_op jit(solution)/shard_map/rows_gather/ppermute | solution.py:173
  99.4 5.3 %all-to-all-done.1.w_ref = bf16[4,2,1024,128]{3,2,1,0:T(8,128)(2,1)S(1)} async-done(((bf16[4,2,1024,128]{3,2,1,0:T(8,128)(2,1)}), bf16[4,2,1024,128]{3,2,1,0:T(8,128)(2,1)S(1)}, u32[]{:S(2)}, u32[]{:S(2)}) %all-to-all-start.1) | async-done | bytes 2097184 | tf_op jit(solution)/shard_map/weight_gather/all_to_all | solution.py:169
  104.7 2.8 %projection.2 = bf16[4,4,32,1024]{3,2,1,0:T(8,128)(2,1)} custom-call(s32[1]{0:T(128)} %bitcast.me, bf16[4,4,32,512]{3,2,1,0:T(8,128)(2,1)S(1)} %pad_maximum_fusion.a_ref, bf16[4,4,32,512]{3,2,1,0:T(8,128)(2,1)S(1)} %collective-permute-done.11.b_ref, bf16[4,2,1024,128]{3,2,1,0:T(8,128)(2,1)S(1)} %all-to-all-done.1.w_ref), custom_call_target="tpu_custom_call" | custom-call | tf_op jit(solution)/shard_map/projection/pallas_call | solution.py:139
  107.5 4.0 %all-to-all-start.2 = ((bf16[4,4,32,1024]{3,2,1,0:T(8,128)(2,1)}), bf16[4,4,32,1024]{3,2,1,0:T(8,128)(2,1)S(1)}, u32[]{:S(2)}, u32[]{:S(2)}) async-start(bf16[4,4,32,1024]{3,2,1,0:T(8,128)(2,1)} %projection.2), calls=%async_computation.2 | async-start | bytes 2097152 | tf_op jit(solution)/shard_map/sum_x/all_to_all | solution.py:255
  111.5 1.9 %collective-permute-start.12 = (bf16[4,32,512]{2,1,0:T(8,128)(2,1)S(1)}, bf16[4,32,512]{2,1,0:T(8,128)(2,1)S(1)}, u32[]{:S(2)}, u32[]{:S(2)}) collective-permute-start(bf16[4,32,512]{2,1,0:T(8,128)(2,1)S(1)} %attention.3), channel_id=1, source_target_pairs={{0,192},{64,128},{128,64},{192,0},{1,193},{65,129},{129,65},{193,1... | collective-permute-start | bytes 393224 | tf_op jit(solution)/shard_map/rows_gather/ppermute | solution.py:177
  113.4 1.9 %collective-permute-start.13 = (bf16[4,32,512]{2,1,0:T(8,128)(2,1)S(1)}, bf16[4,32,512]{2,1,0:T(8,128)(2,1)S(1)}, u32[]{:S(2)}, u32[]{:S(2)}) collective-permute-start(bf16[4,32,512]{2,1,0:T(8,128)(2,1)S(1)} %attention.3), channel_id=1, source_target_pairs={{0,128},{64,192},{128,0},{192,64},{1,129},{65,193},{129,1},{193,65... | collective-permute-start | bytes 393224 | tf_op jit(solution)/shard_map/rows_gather/ppermute | solution.py:177
  115.3 5.4 %collective-permute-start.14 = (bf16[4,32,512]{2,1,0:T(8,128)(2,1)S(1)}, bf16[4,32,512]{2,1,0:T(8,128)(2,1)S(1)}, u32[]{:S(2)}, u32[]{:S(2)}) collective-permute-start(bf16[4,32,512]{2,1,0:T(8,128)(2,1)S(1)} %attention.3), channel_id=1, source_target_pairs={{0,64},{64,0},{128,192},{192,128},{1,65},{65,1},{129,193},{193,129... | collective-permute-start | bytes 393224 | tf_op jit(solution)/shard_map/rows_gather/ppermute | solution.py:177
  120.8 5.0 %collective-permute-done.13 = bf16[4,32,512]{2,1,0:T(8,128)(2,1)S(1)} collective-permute-done((bf16[4,32,512]{2,1,0:T(8,128)(2,1)S(1)}, bf16[4,32,512]{2,1,0:T(8,128)(2,1)S(1)}, u32[]{:S(2)}, u32[]{:S(2)}) %collective-permute-start.13) | collective-permute-done | bytes 131104 | tf_op jit(solution)/shard_map/rows_gather/ppermute | solution.py:177
  127.8 8.2 %all-to-all-start.3 = ((bf16[2,4,32,1024]{3,2,1,0:T(8,128)(2,1)}), bf16[2,4,32,1024]{3,2,1,0:T(8,128)(2,1)}, u32[]{:S(2)}, u32[]{:S(2)}) async-start(bf16[2,4,32,1024]{3,2,1,0:T(8,128)(2,1)} %copy-done), calls=%async_computation.3 | async-start | bytes 1048576 | tf_op jit(solution)/shard_map/sum_zh/all_to_all | solution.py:259
  136.0 3.8 %collective-permute-start.15 = (bf16[4,4,32,512]{3,2,1,0:T(8,128)(2,1)}, bf16[4,4,32,512]{3,2,1,0:T(8,128)(2,1)S(1)}, u32[]{:S(2)}, u32[]{:S(2)}) collective-permute-start(bf16[4,4,32,512]{3,2,1,0:T(8,128)(2,1)} %pad_maximum_fusion.2.a_ref), channel_id=1, source_target_pairs={{0,1},{1,0},{2,3},{3,2},{4,5},{5,4},{6,7},{7,6},{8,9},{9,8},{10,11... | collective-permute-start | bytes 1572872 | tf_op jit(solution)/shard_map/sum_x/ppermute | solution.py:173
  144.3 1.9 %projection.3 = bf16[4,4,32,1024]{3,2,1,0:T(8,128)(2,1)S(1)} custom-call(s32[1]{0:T(128)} %bitcast.me, bf16[4,4,32,512]{3,2,1,0:T(8,128)(2,1)S(1)} %copy-done.1, bf16[4,4,32,512]{3,2,1,0:T(8,128)(2,1)S(1)} %copy-done.4, bf16[4,2,1024,128]{3,2,1,0:T(8,128)(2,1)S(1)} %all-to-all-done.1.w_ref), custom_call_target="tpu_custom_call" | custom-call | tf_op jit(solution)/shard_map/projection/pallas_call | solution.py:139
  146.3 3.5 %collective-permute-start.16 = (bf16[4,32,1024]{2,1,0:T(8,128)(2,1)S(1)}, bf16[4,32,1024]{2,1,0:T(8,128)(2,1)S(1)}, u32[]{:S(2)}, u32[]{:S(2)}) collective-permute-start(bf16[4,32,1024]{2,1,0:T(8,128)(2,1)S(1)} %get-tuple-element.33), channel_id=1, source_target_pairs={{6,0},{0,2},{2,4},{4,6},{7,1},{1,3},{3,5},{5,7},{14,8},{8,10},{10,... | collective-permute-start | bytes 786440 | tf_op jit(solution)/shard_map/sum_x/ppermute | solution.py:181
  149.8 4.3 %collective-permute-start.17 = (bf16[4,32,1024]{2,1,0:T(8,128)(2,1)S(1)}, bf16[4,32,1024]{2,1,0:T(8,128)(2,1)S(1)}, u32[]{:S(2)}, u32[]{:S(2)}) collective-permute-start(bf16[4,32,1024]{2,1,0:T(8,128)(2,1)S(1)} %get-tuple-element.35), channel_id=1, source_target_pairs={{4,0},{6,2},{0,4},{2,6},{5,1},{7,3},{1,5},{3,7},{12,8},{14,10},{8,... | collective-permute-start | bytes 786440 | tf_op jit(solution)/shard_map/sum_x/ppermute | solution.py:181
  154.1 3.1 %collective-permute-start.18 = (bf16[4,32,1024]{2,1,0:T(8,128)(2,1)S(1)}, bf16[4,32,1024]{2,1,0:T(8,128)(2,1)S(1)}, u32[]{:S(2)}, u32[]{:S(2)}) collective-permute-start(bf16[4,32,1024]{2,1,0:T(8,128)(2,1)S(1)} %get-tuple-element.34), channel_id=1, source_target_pairs={{2,0},{4,2},{6,4},{0,6},{3,1},{5,3},{7,5},{1,7},{10,8},{12,10},{14... | collective-permute-start | bytes 786440 | tf_op jit(solution)/shard_map/sum_x/ppermute | solution.py:181
  157.3 6.6 %collective-permute-done.17 = bf16[4,32,1024]{2,1,0:T(8,128)(2,1)S(1)} collective-permute-done((bf16[4,32,1024]{2,1,0:T(8,128)(2,1)S(1)}, bf16[4,32,1024]{2,1,0:T(8,128)(2,1)S(1)}, u32[]{:S(2)}, u32[]{:S(2)}) %collective-permute-start.17) | collective-permute-done | bytes 262176 | tf_op jit(solution)/shard_map/sum_x/ppermute | solution.py:181
  166.2 14.0 %all_to_all.25 = bf16[8,16,1024]{2,1,0:T(8,128)(2,1)S(1)} all-to-all(bf16[8,16,1024]{2,1,0:T(8,128)(2,1)S(1)} %bitcast.37), channel_id=1, replica_groups=mesh['za'=2,'zb'=2,'zq'=2,'y'=4,'zh'=2,'x'=4,'c'=2] {'zb','zq','c'}, dimensions={0} | all-to-all | bytes 524288 | tf_op jit(solution)/shard_map/columns/all_to_all | solution.py:268
  (59 shorter events, 17.0 us)
Async XLA Ops:
  0.0 28.2 %copy-start.7 = (bf16[512,256]{1,0:T(8,128)(2,1)S(1)}, bf16[512,256]{1,0:T(8,128)(2,1)}, u32[]{:S(2)}) copy-start(bf16[512,256]{1,0:T(8,128)(2,1)} %param.11) | copy-start | bytes 786436
  1.3 23.1 %collective-permute-start = (bf16[256,128]{1,0:T(8,128)(2,1)S(1)}, bf16[256,128]{1,0:T(8,128)(2,1)S(1)}, u32[]{:S(2)}, u32[]{:S(2)}) collective-permute-start(bf16[256,128]{1,0:T(8,128)(2,1)S(1)} %get-tuple-element.38), channel_id=1, source_target_pairs={{0,392},{1,393},{64,456},{65,457},{128,0},{129,1},{192,64},{193,65... | collective-permute-start | bytes 196616 | tf_op jit(solution)/shard_map/cache_gather/ppermute | solution.py:189
  13.7 10.7 %collective-permute-start.1 = (bf16[256,128]{1,0:T(8,128)(2,1)S(1)}, bf16[256,128]{1,0:T(8,128)(2,1)S(1)}, u32[]{:S(2)}, u32[]{:S(2)}) collective-permute-start(bf16[256,128]{1,0:T(8,128)(2,1)S(1)} %get-tuple-element.37), channel_id=1, source_target_pairs={{0,128},{1,129},{64,192},{65,193},{128,256},{129,257},{192,320},{1... | collective-permute-start | bytes 196616 | tf_op jit(solution)/shard_map/cache_gather/ppermute | solution.py:189
  15.6 15.7 %collective-permute-start.2 = (bf16[256,128]{1,0:T(8,128)(2,1)S(1)}, bf16[256,128]{1,0:T(8,128)(2,1)S(1)}, u32[]{:S(2)}, u32[]{:S(2)}) collective-permute-start(bf16[256,128]{1,0:T(8,128)(2,1)S(1)} %get-tuple-element.40), channel_id=1, source_target_pairs={{0,264},{1,257},{64,328},{65,321},{128,392},{129,385},{192,456},{1... | collective-permute-start | bytes 196616 | tf_op jit(solution)/shard_map/cache_gather/ppermute | solution.py:189
  17.8 15.3 %collective-permute-start.4 = (bf16[256,128]{1,0:T(8,128)(2,1)S(1)}, bf16[256,128]{1,0:T(8,128)(2,1)S(1)}, u32[]{:S(2)}, u32[]{:S(2)}) collective-permute-start(bf16[256,128]{1,0:T(8,128)(2,1)S(1)} %get-tuple-element.36), channel_id=1, source_target_pairs={{0,328},{1,329},{64,256},{65,257},{128,456},{129,457},{192,384},{1... | collective-permute-start | bytes 196616 | tf_op jit(solution)/shard_map/cache_gather/ppermute | solution.py:189
  24.4 8.6 %collective-permute-start.3 = (bf16[768,128]{1,0:T(8,128)(2,1)S(1)}, bf16[768,128]{1,0:T(8,128)(2,1)S(1)}, u32[]{:S(2)}, u32[]{:S(2)}) collective-permute-start(bf16[768,128]{1,0:T(8,128)(2,1)S(1)} %pad_maximum_fusion.4), channel_id=1, source_target_pairs={{0,64},{64,0},{1,65},{65,1},{2,66},{66,2},{3,67},{67,3},{4,68},{68... | collective-permute-start | bytes 589832 | tf_op jit(solution)/shard_map/cache_gather/ppermute | solution.py:173
  28.3 4.0 %collective-permute-start.5 = (bf16[512,128]{1,0:T(8,128)(2,1)S(1)}, bf16[512,128]{1,0:T(8,128)(2,1)S(1)}, u32[]{:S(2)}, u32[]{:S(2)}) collective-permute-start(bf16[512,128]{1,0:T(8,128)(2,1)S(1)} %get-tuple-element.44), channel_id=1, source_target_pairs={{0,1},{1,0},{2,3},{3,2},{4,5},{5,4},{6,7},{7,6},{8,9},{9,8},{10,11... | collective-permute-start | bytes 393224 | tf_op jit(solution)/shard_map/weight_gather/ppermute | solution.py:173
  34.7 34.0 %all-to-all-start = ((bf16[4,2048,128]{2,1,0:T(8,128)(2,1)}), bf16[4,2048,128]{2,1,0:T(8,128)(2,1)}, u32[]{:S(2)}, u32[]{:S(2)}) async-start(bf16[4,2048,128]{2,1,0:T(8,128)(2,1)} %broadcast_in_dim.4), calls=%async_computation | async-start | bytes 4194304 | tf_op jit(solution)/shard_map/cache_gather/all_to_all | solution.py:169
  39.2 29.5 %collective-permute-start.6 = (bf16[1024,128]{1,0:T(8,128)(2,1)S(1)}, bf16[1024,128]{1,0:T(8,128)(2,1)S(1)}, u32[]{:S(2)}, u32[]{:S(2)}) collective-permute-start(bf16[1024,128]{1,0:T(8,128)(2,1)S(1)} %pad_maximum_fusion.3), channel_id=1, source_target_pairs={{0,256},{256,0},{1,257},{257,1},{2,258},{258,2},{3,259},{259,3},{4... | collective-permute-start | bytes 786440 | tf_op jit(solution)/shard_map/weight_gather/ppermute | solution.py:173
  68.7 9.9 %collective-permute-start.7 = (bf16[8192,128]{1,0:T(8,128)(2,1)}, bf16[8192,128]{1,0:T(8,128)(2,1)}, u32[]{:S(2)}, u32[]{:S(2)}) collective-permute-start(bf16[8192,128]{1,0:T(8,128)(2,1)} %bitcast.4.own_ref), channel_id=1, source_target_pairs={{0,1},{1,0},{2,3},{3,2},{4,5},{5,4},{6,7},{7,6},{8,9},{9,8},{10,11... | collective-permute-start | bytes 6291464 | tf_op jit(solution)/shard_map/cache_gather/ppermute | solution.py:173
  74.2 4.4 %copy-start.2 = (bf16[256,512]{1,0:T(8,128)(2,1)S(1)}, bf16[256,512]{1,0:T(8,128)(2,1)}, u32[]{:S(2)}) copy-start(bf16[256,512]{1,0:T(8,128)(2,1)} %q_ref.3) | copy-start | bytes 786436
  74.2 4.4 %copy-start.5 = (s32[32]{0:T(128)S(1)}, s32[32]{0:T(128)}, u32[]{:S(2)}) copy-start(s32[32]{0:T(128)} %counts.3) | copy-start | bytes 388
  74.2 4.4 %copy-start.6 = (s32[64]{0:T(128)S(1)}, s32[64]{0:T(128)}, u32[]{:S(2)}) copy-start(s32[64]{0:T(128)} %order.3) | copy-start | bytes 772
  74.2 30.5 %all-to-all-start.1 = ((bf16[4,2,1024,128]{3,2,1,0:T(8,128)(2,1)}), bf16[4,2,1024,128]{3,2,1,0:T(8,128)(2,1)S(1)}, u32[]{:S(2)}, u32[]{:S(2)}) async-start(bf16[4,2,1024,128]{3,2,1,0:T(8,128)(2,1)} %broadcast_in_dim.5), calls=%async_computation.1 | async-start | bytes 4194304 | tf_op jit(solution)/shard_map/weight_gather/all_to_all | solution.py:169
  80.9 15.3 %collective-permute-start.8 = (bf16[4,32,512]{2,1,0:T(8,128)(2,1)S(1)}, bf16[4,32,512]{2,1,0:T(8,128)(2,1)S(1)}, u32[]{:S(2)}, u32[]{:S(2)}) collective-permute-start(bf16[4,32,512]{2,1,0:T(8,128)(2,1)S(1)} %attention.2), channel_id=1, source_target_pairs={{0,192},{64,128},{128,64},{192,0},{1,193},{65,129},{129,65},{193,1... | collective-permute-start | bytes 393224 | tf_op jit(solution)/shard_map/rows_gather/ppermute | solution.py:177
  82.9 13.4 %collective-permute-start.9 = (bf16[4,32,512]{2,1,0:T(8,128)(2,1)S(1)}, bf16[4,32,512]{2,1,0:T(8,128)(2,1)S(1)}, u32[]{:S(2)}, u32[]{:S(2)}) collective-permute-start(bf16[4,32,512]{2,1,0:T(8,128)(2,1)S(1)} %attention.2), channel_id=1, source_target_pairs={{0,128},{64,192},{128,0},{192,64},{1,129},{65,193},{129,1},{193,65... | collective-permute-start | bytes 393224 | tf_op jit(solution)/shard_map/rows_gather/ppermute | solution.py:177
  84.8 11.5 %collective-permute-start.10 = (bf16[4,32,512]{2,1,0:T(8,128)(2,1)S(1)}, bf16[4,32,512]{2,1,0:T(8,128)(2,1)S(1)}, u32[]{:S(2)}, u32[]{:S(2)}) collective-permute-start(bf16[4,32,512]{2,1,0:T(8,128)(2,1)S(1)} %attention.2), channel_id=1, source_target_pairs={{0,64},{64,0},{128,192},{192,128},{1,65},{65,1},{129,193},{193,129... | collective-permute-start | bytes 393224 | tf_op jit(solution)/shard_map/rows_gather/ppermute | solution.py:177
  96.4 8.4 %collective-permute-start.11 = (bf16[4,4,32,512]{3,2,1,0:T(8,128)(2,1)S(1)}, bf16[4,4,32,512]{3,2,1,0:T(8,128)(2,1)S(1)}, u32[]{:S(2)}, u32[]{:S(2)}) collective-permute-start(bf16[4,4,32,512]{3,2,1,0:T(8,128)(2,1)S(1)} %pad_maximum_fusion.a_ref), channel_id=1, source_target_pairs={{0,1},{1,0},{2,3},{3,2},{4,5},{5,4},{6,7},{7,6},{8,9},{9,8},{10,11... | collective-permute-start | bytes 1572872 | tf_op jit(solution)/shard_map/rows_gather/ppermute | solution.py:173
  107.5 19.2 %all-to-all-start.2 = ((bf16[4,4,32,1024]{3,2,1,0:T(8,128)(2,1)}), bf16[4,4,32,1024]{3,2,1,0:T(8,128)(2,1)S(1)}, u32[]{:S(2)}, u32[]{:S(2)}) async-start(bf16[4,4,32,1024]{3,2,1,0:T(8,128)(2,1)} %projection.2), calls=%async_computation.2 | async-start | bytes 2097152 | tf_op jit(solution)/shard_map/sum_x/all_to_all | solution.py:255
  111.5 9.3 %collective-permute-start.12 = (bf16[4,32,512]{2,1,0:T(8,128)(2,1)S(1)}, bf16[4,32,512]{2,1,0:T(8,128)(2,1)S(1)}, u32[]{:S(2)}, u32[]{:S(2)}) collective-permute-start(bf16[4,32,512]{2,1,0:T(8,128)(2,1)S(1)} %attention.3), channel_id=1, source_target_pairs={{0,192},{64,128},{128,64},{192,0},{1,193},{65,129},{129,65},{193,1... | collective-permute-start | bytes 393224 | tf_op jit(solution)/shard_map/rows_gather/ppermute | solution.py:177
  113.4 12.4 %collective-permute-start.13 = (bf16[4,32,512]{2,1,0:T(8,128)(2,1)S(1)}, bf16[4,32,512]{2,1,0:T(8,128)(2,1)S(1)}, u32[]{:S(2)}, u32[]{:S(2)}) collective-permute-start(bf16[4,32,512]{2,1,0:T(8,128)(2,1)S(1)} %attention.3), channel_id=1, source_target_pairs={{0,128},{64,192},{128,0},{192,64},{1,129},{65,193},{129,1},{193,65... | collective-permute-start | bytes 393224 | tf_op jit(solution)/shard_map/rows_gather/ppermute | solution.py:177
  115.3 10.5 %collective-permute-start.14 = (bf16[4,32,512]{2,1,0:T(8,128)(2,1)S(1)}, bf16[4,32,512]{2,1,0:T(8,128)(2,1)S(1)}, u32[]{:S(2)}, u32[]{:S(2)}) collective-permute-start(bf16[4,32,512]{2,1,0:T(8,128)(2,1)S(1)} %attention.3), channel_id=1, source_target_pairs={{0,64},{64,0},{128,192},{192,128},{1,65},{65,1},{129,193},{193,129... | collective-permute-start | bytes 393224 | tf_op jit(solution)/shard_map/rows_gather/ppermute | solution.py:177
  127.0 0.8 copy-start
  127.8 37.2 %all-to-all-start.3 = ((bf16[2,4,32,1024]{3,2,1,0:T(8,128)(2,1)}), bf16[2,4,32,1024]{3,2,1,0:T(8,128)(2,1)}, u32[]{:S(2)}, u32[]{:S(2)}) async-start(bf16[2,4,32,1024]{3,2,1,0:T(8,128)(2,1)} %copy-done), calls=%async_computation.3 | async-start | bytes 1048576 | tf_op jit(solution)/shard_map/sum_zh/all_to_all | solution.py:259
  136.0 5.5 %collective-permute-start.15 = (bf16[4,4,32,512]{3,2,1,0:T(8,128)(2,1)}, bf16[4,4,32,512]{3,2,1,0:T(8,128)(2,1)S(1)}, u32[]{:S(2)}, u32[]{:S(2)}) collective-permute-start(bf16[4,4,32,512]{3,2,1,0:T(8,128)(2,1)} %pad_maximum_fusion.2.a_ref), channel_id=1, source_target_pairs={{0,1},{1,0},{2,3},{3,2},{4,5},{5,4},{6,7},{7,6},{8,9},{9,8},{10,11... | collective-permute-start | bytes 1572872 | tf_op jit(solution)/shard_map/sum_x/ppermute | solution.py:173
  141.5 0.8 copy-start.3
  142.3 1.0 copy-start.1
  143.3 1.0 copy-start.4
  146.3 11.0 %collective-permute-start.16 = (bf16[4,32,1024]{2,1,0:T(8,128)(2,1)S(1)}, bf16[4,32,1024]{2,1,0:T(8,128)(2,1)S(1)}, u32[]{:S(2)}, u32[]{:S(2)}) collective-permute-start(bf16[4,32,1024]{2,1,0:T(8,128)(2,1)S(1)} %get-tuple-element.33), channel_id=1, source_target_pairs={{6,0},{0,2},{2,4},{4,6},{7,1},{1,3},{3,5},{5,7},{14,8},{8,10},{10,... | collective-permute-start | bytes 786440 | tf_op jit(solution)/shard_map/sum_x/ppermute | solution.py:181
  149.8 14.0 %collective-permute-start.17 = (bf16[4,32,1024]{2,1,0:T(8,128)(2,1)S(1)}, bf16[4,32,1024]{2,1,0:T(8,128)(2,1)S(1)}, u32[]{:S(2)}, u32[]{:S(2)}) collective-permute-start(bf16[4,32,1024]{2,1,0:T(8,128)(2,1)S(1)} %get-tuple-element.35), channel_id=1, source_target_pairs={{4,0},{6,2},{0,4},{2,6},{5,1},{7,3},{1,5},{3,7},{12,8},{14,10},{8,... | collective-permute-start | bytes 786440 | tf_op jit(solution)/shard_map/sum_x/ppermute | solution.py:181
  154.1 10.9 %collective-permute-start.18 = (bf16[4,32,1024]{2,1,0:T(8,128)(2,1)S(1)}, bf16[4,32,1024]{2,1,0:T(8,128)(2,1)S(1)}, u32[]{:S(2)}, u32[]{:S(2)}) collective-permute-start(bf16[4,32,1024]{2,1,0:T(8,128)(2,1)S(1)} %get-tuple-element.34), channel_id=1, source_target_pairs={{2,0},{4,2},{6,4},{0,6},{3,1},{5,3},{7,5},{1,7},{10,8},{12,10},{14... | collective-permute-start | bytes 786440 | tf_op jit(solution)/shard_map/sum_x/ppermute | solution.py:181

commit v7 on v6

--- a/solution.py
+++ b/solution.py
@@ -126,10 +126,10 @@
 
 def project_kernel(me, a_ref, b_ref, w_ref, o_ref):
     half = a_ref.shape[-1]
-    w = jnp.concatenate([w_ref[0, 0], w_ref[0, 1]], axis=1)
-    part = jnp.dot(a_ref[...].reshape(-1, half), w[:half], preferred_element_type=jnp.float32)
-    part += jnp.dot(b_ref[...].reshape(-1, half), w[half:], preferred_element_type=jnp.float32)
-    part = part.astype(jnp.bfloat16).reshape(QUAD, X, 32, 2 * HD)
+    w = jnp.concatenate([w_ref[i, j] for i in range(2) for j in range(ZA)], axis=1)
+    rows = jnp.concatenate([a_ref[...].reshape(-1, half), b_ref[...].reshape(-1, half)], axis=1)
+    part = jnp.dot(rows, w, preferred_element_type=jnp.float32)
+    part = part.astype(jnp.bfloat16).reshape(QUAD, X, 32, 4 * HD)
     for i in range(QUAD):
         o_ref[:, me[0] ^ ((QUAD - i) % QUAD)] = part[i]
 
@@ -138,10 +138,10 @@
     rows = pl.BlockSpec(a.shape, lambda i: (0, 0, 0, 0))
     return pl.pallas_call(
         project_kernel,
-        grid=(Y,),
+        grid=(Y // 2,),
         out_shape=jax.ShapeDtypeStruct((X, QUAD, 32, ZL * HD), jnp.bfloat16),
-        in_specs=[pl.BlockSpec(memory_space=pltpu.SMEM), rows, rows, pl.BlockSpec((1, *w.shape[1:]), lambda i: (i, 0, 0, 0))],
-        out_specs=pl.BlockSpec((X, QUAD, 32, 2 * HD), lambda i: (0, 0, 0, i)),
+        in_specs=[pl.BlockSpec(memory_space=pltpu.SMEM), rows, rows, pl.BlockSpec((2, *w.shape[1:]), lambda i: (i, 0, 0, 0))],
+        out_specs=pl.BlockSpec((X, QUAD, 32, 4 * HD), lambda i: (0, 0, 0, i)),
         compiler_params=pltpu.CompilerParams(vmem_limit_bytes=24 << 20),
     )(me, a, b, w)
 

time: 184 us -> 183 us (level)
  Pallas kernels: 13.2 us -> 17 us
  waiting for transfers between devices: 47.3 us -> 43.8 us
    all_to_all x2, waiting for transfers between devices: 5.29 us -> 0.63 us  [spread(): lax.all_to_all(jnp.broadcast_to(piece[None], (count, *piece.shape)), axis...]
    pallas_call x2, Pallas kernels: 8.22 us -> 12.9 us  [attend(): pl.pallas_call(attention_kernel, out_shape=jax.ShapeDtypeStruct((X, 32, H...]
  transfers between devices with their start and end apart: 23 -> 23, of which waited for: 9 -> 9; matrix products, arithmetic and copies ran while one was open for 2% -> 2% of each run, Pallas kernels for 6% -> 8%
where the time goes in v7:
time: 183 us; the launch traced here: 182 us
  starting transfers between devices  93.5 us (51%)
  waiting for transfers between devices  43.8 us (24%)
  Pallas kernels  17 us (9%)
  blocking collectives  14.8 us (8%)
  local copies, waits for them, and re-layouts  8.44 us (5%)
  other arithmetic  3.65 us (2%)
    ppermute x6, waiting for transfers between devices, swap(): return lax.ppermute(piece, axis, [(0, 1), (1, 0)])  30.1 us
    ppermute x4, starting transfers between devices, along(): return lax.ppermute(piece, LINE, perm)  23.1 us
    ppermute x6, starting transfers between devices, swap(): return lax.ppermute(piece, axis, [(0, 1), (1, 0)])  21.1 us
    ppermute x6, starting transfers between devices, quad(): lax.ppermute(piece, ('zb', 'zq'), [(i, i ^ step) for i in range(QUAD)])  18.5 us
    all_to_all x1, blocking collectives, body(): lax.all_to_all(mixed.reshape(QUAD * C, 16, ZL * HD), ('zb', 'zq', 'c'), 0...  14.8 us
    pallas_call x2, Pallas kernels, attend(): pl.pallas_call(attention_kernel, out_shape=jax.ShapeDtypeStruct((X, 32, H...  12.9 us
    ppermute x3, starting transfers between devices, around(): lax.ppermute(piece, axis, [((i + shift) % count, i) for i in range(count)])  10.8 us
    all_to_all x2, starting transfers between devices, spread(): lax.all_to_all(jnp.broadcast_to(piece[None], (count, *piece.shape)), axis...  8.76 us
  transfers between devices with their start and end apart: 23, of which 9 were waited for; matrix products, arithmetic and copies ran while one was open for 2% of the time, Pallas kernels for 8%

profile of v7, /device:TPU:1, one launch (start us, length us, event | category | flops | bytes accessed | tf_op | source)
XLA Modules:
  0.0 181.7 jit_solution(12208747414845904282)
XLA Ops:
  1.3 12.4 %collective-permute-start = (bf16[256,128]{1,0:T(8,128)(2,1)S(1)}, bf16[256,128]{1,0:T(8,128)(2,1)S(1)}, u32[]{:S(2)}, u32[]{:S(2)}) collective-permute-start(bf16[256,128]{1,0:T(8,128)(2,1)S(1)} %get-tuple-element.38), channel_id=1, source_target_pairs={{0,392},{1,393},{64,456},{65,457},{128,0},{129,1},{192,64},{193,65... | collective-permute-start | bytes 196616 | tf_op jit(solution)/shard_map/cache_gather/ppermute | solution.py:189
  13.7 1.9 %collective-permute-start.1 = (bf16[256,128]{1,0:T(8,128)(2,1)S(1)}, bf16[256,128]{1,0:T(8,128)(2,1)S(1)}, u32[]{:S(2)}, u32[]{:S(2)}) collective-permute-start(bf16[256,128]{1,0:T(8,128)(2,1)S(1)} %get-tuple-element.37), channel_id=1, source_target_pairs={{0,128},{1,129},{64,192},{65,193},{128,256},{129,257},{192,320},{1... | collective-permute-start | bytes 196616 | tf_op jit(solution)/shard_map/cache_gather/ppermute | solution.py:189
  15.6 2.2 %collective-permute-start.2 = (bf16[256,128]{1,0:T(8,128)(2,1)S(1)}, bf16[256,128]{1,0:T(8,128)(2,1)S(1)}, u32[]{:S(2)}, u32[]{:S(2)}) collective-permute-start(bf16[256,128]{1,0:T(8,128)(2,1)S(1)} %get-tuple-element.40), channel_id=1, source_target_pairs={{0,264},{1,257},{64,328},{65,321},{128,392},{129,385},{192,456},{1... | collective-permute-start | bytes 196616 | tf_op jit(solution)/shard_map/cache_gather/ppermute | solution.py:189
  17.8 6.6 %collective-permute-start.4 = (bf16[256,128]{1,0:T(8,128)(2,1)S(1)}, bf16[256,128]{1,0:T(8,128)(2,1)S(1)}, u32[]{:S(2)}, u32[]{:S(2)}) collective-permute-start(bf16[256,128]{1,0:T(8,128)(2,1)S(1)} %get-tuple-element.36), channel_id=1, source_target_pairs={{0,328},{1,329},{64,256},{65,257},{128,456},{129,457},{192,384},{1... | collective-permute-start | bytes 196616 | tf_op jit(solution)/shard_map/cache_gather/ppermute | solution.py:189
  24.4 3.8 %collective-permute-start.3 = (bf16[768,128]{1,0:T(8,128)(2,1)S(1)}, bf16[768,128]{1,0:T(8,128)(2,1)S(1)}, u32[]{:S(2)}, u32[]{:S(2)}) collective-permute-start(bf16[768,128]{1,0:T(8,128)(2,1)S(1)} %pad_maximum_fusion.4), channel_id=1, source_target_pairs={{0,64},{64,0},{1,65},{65,1},{2,66},{66,2},{3,67},{67,3},{4,68},{68... | collective-permute-start | bytes 589832 | tf_op jit(solution)/shard_map/cache_gather/ppermute | solution.py:173
  28.3 3.0 %collective-permute-start.5 = (bf16[512,128]{1,0:T(8,128)(2,1)S(1)}, bf16[512,128]{1,0:T(8,128)(2,1)S(1)}, u32[]{:S(2)}, u32[]{:S(2)}) collective-permute-start(bf16[512,128]{1,0:T(8,128)(2,1)S(1)} %get-tuple-element.44), channel_id=1, source_target_pairs={{0,1},{1,0},{2,3},{3,2},{4,5},{5,4},{6,7},{7,6},{8,9},{9,8},{10,11... | collective-permute-start | bytes 393224 | tf_op jit(solution)/shard_map/weight_gather/ppermute | solution.py:173
  34.7 4.4 %all-to-all-start = ((bf16[4,2048,128]{2,1,0:T(8,128)(2,1)}), bf16[4,2048,128]{2,1,0:T(8,128)(2,1)}, u32[]{:S(2)}, u32[]{:S(2)}) async-start(bf16[4,2048,128]{2,1,0:T(8,128)(2,1)} %broadcast_in_dim.4), calls=%async_computation | async-start | bytes 4194304 | tf_op jit(solution)/shard_map/cache_gather/all_to_all | solution.py:169
  39.2 3.7 %collective-permute-start.6 = (bf16[1024,128]{1,0:T(8,128)(2,1)S(1)}, bf16[1024,128]{1,0:T(8,128)(2,1)S(1)}, u32[]{:S(2)}, u32[]{:S(2)}) collective-permute-start(bf16[1024,128]{1,0:T(8,128)(2,1)S(1)} %pad_maximum_fusion.3), channel_id=1, source_target_pairs={{0,256},{256,0},{1,257},{257,1},{2,258},{258,2},{3,259},{259,3},{4... | collective-permute-start | bytes 786440 | tf_op jit(solution)/shard_map/weight_gather/ppermute | solution.py:173
  42.9 25.8 %collective-permute-done.6 = bf16[1024,128]{1,0:T(8,128)(2,1)S(1)} collective-permute-done((bf16[1024,128]{1,0:T(8,128)(2,1)S(1)}, bf16[1024,128]{1,0:T(8,128)(2,1)S(1)}, u32[]{:S(2)}, u32[]{:S(2)}) %collective-permute-start.6) | collective-permute-done | bytes 262176 | tf_op jit(solution)/shard_map/weight_gather/ppermute | solution.py:173
  68.7 3.8 %collective-permute-start.7 = (bf16[8192,128]{1,0:T(8,128)(2,1)}, bf16[8192,128]{1,0:T(8,128)(2,1)}, u32[]{:S(2)}, u32[]{:S(2)}) collective-permute-start(bf16[8192,128]{1,0:T(8,128)(2,1)} %bitcast.4.own_ref), channel_id=1, source_target_pairs={{0,1},{1,0},{2,3},{3,2},{4,5},{5,4},{6,7},{7,6},{8,9},{9,8},{10,11... | collective-permute-start | bytes 6291464 | tf_op jit(solution)/shard_map/cache_gather/ppermute | solution.py:173
  72.6 1.6 broadcast_in_dim.5
  74.2 4.3 %all-to-all-start.1 = ((bf16[4,2,1024,128]{3,2,1,0:T(8,128)(2,1)}), bf16[4,2,1024,128]{3,2,1,0:T(8,128)(2,1)S(1)}, u32[]{:S(2)}, u32[]{:S(2)}) async-start(bf16[4,2,1024,128]{3,2,1,0:T(8,128)(2,1)} %broadcast_in_dim.5), calls=%async_computation.1 | async-start | bytes 4194304 | tf_op jit(solution)/shard_map/weight_gather/all_to_all | solution.py:169
  78.6 6.2 %attention.2 = bf16[4,32,512]{2,1,0:T(8,128)(2,1)S(1)} custom-call(s32[32]{0:T(128)S(1)} %copy-done.5, s32[64]{0:T(128)S(1)} %copy-done.6, s32[3]{0:T(128)S(1)} %pad_add_fusion.place, bf16[256,512]{1,0:T(8,128)(2,1)S(1)} %copy-done.2, bf16[8192,128]{1,0:T(8,128)(2,1)} %bitcast.4.own_ref, bf16[8192,128]{1,0:T(8,128)(2,1)} %collective-permute-done.7.other_ref), custom_call_target="tpu_custom_call" | custom-call | tf_op jit(solution)/shard_map/attention/pallas_call | solution.py:117
  84.8 1.9 %collective-permute-start.8 = (bf16[4,32,512]{2,1,0:T(8,128)(2,1)S(1)}, bf16[4,32,512]{2,1,0:T(8,128)(2,1)S(1)}, u32[]{:S(2)}, u32[]{:S(2)}) collective-permute-start(bf16[4,32,512]{2,1,0:T(8,128)(2,1)S(1)} %attention.2), channel_id=1, source_target_pairs={{0,192},{64,128},{128,64},{192,0},{1,193},{65,129},{129,65},{193,1... | collective-permute-start | bytes 393224 | tf_op jit(solution)/shard_map/rows_gather/ppermute | solution.py:177
  86.8 1.9 %collective-permute-start.9 = (bf16[4,32,512]{2,1,0:T(8,128)(2,1)S(1)}, bf16[4,32,512]{2,1,0:T(8,128)(2,1)S(1)}, u32[]{:S(2)}, u32[]{:S(2)}) collective-permute-start(bf16[4,32,512]{2,1,0:T(8,128)(2,1)S(1)} %attention.2), channel_id=1, source_target_pairs={{0,128},{64,192},{128,0},{192,64},{1,129},{65,193},{129,1},{193,65... | collective-permute-start | bytes 393224 | tf_op jit(solution)/shard_map/rows_gather/ppermute | solution.py:177
  88.7 5.4 %collective-permute-start.10 = (bf16[4,32,512]{2,1,0:T(8,128)(2,1)S(1)}, bf16[4,32,512]{2,1,0:T(8,128)(2,1)S(1)}, u32[]{:S(2)}, u32[]{:S(2)}) collective-permute-start(bf16[4,32,512]{2,1,0:T(8,128)(2,1)S(1)} %attention.2), channel_id=1, source_target_pairs={{0,64},{64,0},{128,192},{192,128},{1,65},{65,1},{129,193},{193,129... | collective-permute-start | bytes 393224 | tf_op jit(solution)/shard_map/rows_gather/ppermute | solution.py:177
  94.2 6.7 %attention.3 = bf16[4,32,512]{2,1,0:T(8,128)(2,1)S(1)} custom-call(s32[32]{0:T(128)S(1)} %copy-done.5, s32[64]{0:T(128)S(1)} %copy-done.6, s32[3]{0:T(128)S(1)} %pad_add_fusion.2.place, bf16[256,512]{1,0:T(8,128)(2,1)S(1)} %copy-done.2, bf16[8192,128]{1,0:T(8,128)(2,1)} %bitcast.4.own_ref, bf16[8192,128]{1,0:T(8,128)(2,1)} %collective-permute-done.7.other_ref), custom_call_target="tpu_custom_call" | custom-call | tf_op jit(solution)/shard_map/attention/pallas_call | solution.py:117
  101.0 3.1 %collective-permute-start.11 = (bf16[4,4,32,512]{3,2,1,0:T(8,128)(2,1)S(1)}, bf16[4,4,32,512]{3,2,1,0:T(8,128)(2,1)S(1)}, u32[]{:S(2)}, u32[]{:S(2)}) collective-permute-start(bf16[4,4,32,512]{3,2,1,0:T(8,128)(2,1)S(1)} %pad_maximum_fusion.a_ref), channel_id=1, source_target_pairs={{0,1},{1,0},{2,3},{3,2},{4,5},{5,4},{6,7},{7,6},{8,9},{9,8},{10,11... | collective-permute-start | bytes 1572872 | tf_op jit(solution)/shard_map/rows_gather/ppermute | solution.py:173
  105.6 2.3 %projection.2 = bf16[4,4,32,1024]{3,2,1,0:T(8,128)(2,1)} custom-call(s32[1]{0:T(128)} %bitcast.me, bf16[4,4,32,512]{3,2,1,0:T(8,128)(2,1)S(1)} %pad_maximum_fusion.a_ref, bf16[4,4,32,512]{3,2,1,0:T(8,128)(2,1)S(1)} %collective-permute-done.11.b_ref, bf16[4,2,1024,128]{3,2,1,0:T(8,128)(2,1)S(1)} %all-to-all-done.1.w_ref), custom_call_target="tpu_custom_call" | custom-call | tf_op jit(solution)/shard_map/projection/pallas_call | solution.py:139
  107.9 4.0 %all-to-all-start.2 = ((bf16[4,4,32,1024]{3,2,1,0:T(8,128)(2,1)}), bf16[4,4,32,1024]{3,2,1,0:T(8,128)(2,1)S(1)}, u32[]{:S(2)}, u32[]{:S(2)}) async-start(bf16[4,4,32,1024]{3,2,1,0:T(8,128)(2,1)} %projection.2), calls=%async_computation.2 | async-start | bytes 2097152 | tf_op jit(solution)/shard_map/sum_x/all_to_all | solution.py:255
  111.9 2.3 %collective-permute-start.12 = (bf16[4,32,512]{2,1,0:T(8,128)(2,1)S(1)}, bf16[4,32,512]{2,1,0:T(8,128)(2,1)S(1)}, u32[]{:S(2)}, u32[]{:S(2)}) collective-permute-start(bf16[4,32,512]{2,1,0:T(8,128)(2,1)S(1)} %attention.3), channel_id=1, source_target_pairs={{0,192},{64,128},{128,64},{192,0},{1,193},{65,129},{129,65},{193,1... | collective-permute-start | bytes 393224 | tf_op jit(solution)/shard_map/rows_gather/ppermute | solution.py:177
  114.1 1.9 %collective-permute-start.13 = (bf16[4,32,512]{2,1,0:T(8,128)(2,1)S(1)}, bf16[4,32,512]{2,1,0:T(8,128)(2,1)S(1)}, u32[]{:S(2)}, u32[]{:S(2)}) collective-permute-start(bf16[4,32,512]{2,1,0:T(8,128)(2,1)S(1)} %attention.3), channel_id=1, source_target_pairs={{0,128},{64,192},{128,0},{192,64},{1,129},{65,193},{129,1},{193,65... | collective-permute-start | bytes 393224 | tf_op jit(solution)/shard_map/rows_gather/ppermute | solution.py:177
  116.1 5.1 %collective-permute-start.14 = (bf16[4,32,512]{2,1,0:T(8,128)(2,1)S(1)}, bf16[4,32,512]{2,1,0:T(8,128)(2,1)S(1)}, u32[]{:S(2)}, u32[]{:S(2)}) collective-permute-start(bf16[4,32,512]{2,1,0:T(8,128)(2,1)S(1)} %attention.3), channel_id=1, source_target_pairs={{0,64},{64,0},{128,192},{192,128},{1,65},{65,1},{129,193},{193,129... | collective-permute-start | bytes 393224 | tf_op jit(solution)/shard_map/rows_gather/ppermute | solution.py:177
  121.1 5.5 %collective-permute-done.13 = bf16[4,32,512]{2,1,0:T(8,128)(2,1)S(1)} collective-permute-done((bf16[4,32,512]{2,1,0:T(8,128)(2,1)S(1)}, bf16[4,32,512]{2,1,0:T(8,128)(2,1)S(1)}, u32[]{:S(2)}, u32[]{:S(2)}) %collective-permute-start.13) | collective-permute-done | bytes 131104 | tf_op jit(solution)/shard_map/rows_gather/ppermute | solution.py:177
  128.6 7.3 %all-to-all-start.3 = ((bf16[2,4,32,1024]{3,2,1,0:T(8,128)(2,1)}), bf16[2,4,32,1024]{3,2,1,0:T(8,128)(2,1)}, u32[]{:S(2)}, u32[]{:S(2)}) async-start(bf16[2,4,32,1024]{3,2,1,0:T(8,128)(2,1)} %copy-done), calls=%async_computation.3 | async-start | bytes 1048576 | tf_op jit(solution)/shard_map/sum_zh/all_to_all | solution.py:259
  135.9 3.8 %collective-permute-start.15 = (bf16[4,4,32,512]{3,2,1,0:T(8,128)(2,1)}, bf16[4,4,32,512]{3,2,1,0:T(8,128)(2,1)S(1)}, u32[]{:S(2)}, u32[]{:S(2)}) collective-permute-start(bf16[4,4,32,512]{3,2,1,0:T(8,128)(2,1)} %pad_maximum_fusion.2.a_ref), channel_id=1, source_target_pairs={{0,1},{1,0},{2,3},{3,2},{4,5},{5,4},{6,7},{7,6},{8,9},{9,8},{10,11... | collective-permute-start | bytes 1572872 | tf_op jit(solution)/shard_map/sum_x/ppermute | solution.py:173
  139.8 1.7 collective-permute-done.15.b_ref
  145.9 3.4 %collective-permute-start.16 = (bf16[4,32,1024]{2,1,0:T(8,128)(2,1)S(1)}, bf16[4,32,1024]{2,1,0:T(8,128)(2,1)S(1)}, u32[]{:S(2)}, u32[]{:S(2)}) collective-permute-start(bf16[4,32,1024]{2,1,0:T(8,128)(2,1)S(1)} %get-tuple-element.33), channel_id=1, source_target_pairs={{6,0},{0,2},{2,4},{4,6},{7,1},{1,3},{3,5},{5,7},{14,8},{8,10},{10,... | collective-permute-start | bytes 786440 | tf_op jit(solution)/shard_map/sum_x/ppermute | solution.py:181
  149.3 4.3 %collective-permute-start.17 = (bf16[4,32,1024]{2,1,0:T(8,128)(2,1)S(1)}, bf16[4,32,1024]{2,1,0:T(8,128)(2,1)S(1)}, u32[]{:S(2)}, u32[]{:S(2)}) collective-permute-start(bf16[4,32,1024]{2,1,0:T(8,128)(2,1)S(1)} %get-tuple-element.35), channel_id=1, source_target_pairs={{4,0},{6,2},{0,4},{2,6},{5,1},{7,3},{1,5},{3,7},{12,8},{14,10},{8,... | collective-permute-start | bytes 786440 | tf_op jit(solution)/shard_map/sum_x/ppermute | solution.py:181
  153.6 3.1 %collective-permute-start.18 = (bf16[4,32,1024]{2,1,0:T(8,128)(2,1)S(1)}, bf16[4,32,1024]{2,1,0:T(8,128)(2,1)S(1)}, u32[]{:S(2)}, u32[]{:S(2)}) collective-permute-start(bf16[4,32,1024]{2,1,0:T(8,128)(2,1)S(1)} %get-tuple-element.34), channel_id=1, source_target_pairs={{2,0},{4,2},{6,4},{0,6},{3,1},{5,3},{7,5},{1,7},{10,8},{12,10},{14... | collective-permute-start | bytes 786440 | tf_op jit(solution)/shard_map/sum_x/ppermute | solution.py:181
  156.7 6.6 %collective-permute-done.17 = bf16[4,32,1024]{2,1,0:T(8,128)(2,1)S(1)} collective-permute-done((bf16[4,32,1024]{2,1,0:T(8,128)(2,1)S(1)}, bf16[4,32,1024]{2,1,0:T(8,128)(2,1)S(1)}, u32[]{:S(2)}, u32[]{:S(2)}) %collective-permute-start.17) | collective-permute-done | bytes 262176 | tf_op jit(solution)/shard_map/sum_x/ppermute | solution.py:181
  165.5 14.8 %all_to_all.25 = bf16[8,16,1024]{2,1,0:T(8,128)(2,1)S(1)} all-to-all(bf16[8,16,1024]{2,1,0:T(8,128)(2,1)S(1)} %bitcast.37), channel_id=1, replica_groups=mesh['za'=2,'zb'=2,'zq'=2,'y'=4,'zh'=2,'x'=4,'c'=2] {'zb','zq','c'}, dimensions={0} | all-to-all | bytes 524288 | tf_op jit(solution)/shard_map/columns/all_to_all | solution.py:268
  (59 shorter events, 16.6 us)
Async XLA Ops:
  0.0 28.2 %copy-start.7 = (bf16[512,256]{1,0:T(8,128)(2,1)S(1)}, bf16[512,256]{1,0:T(8,128)(2,1)}, u32[]{:S(2)}) copy-start(bf16[512,256]{1,0:T(8,128)(2,1)} %param.11) | copy-start | bytes 786436
  1.3 23.1 %collective-permute-start = (bf16[256,128]{1,0:T(8,128)(2,1)S(1)}, bf16[256,128]{1,0:T(8,128)(2,1)S(1)}, u32[]{:S(2)}, u32[]{:S(2)}) collective-permute-start(bf16[256,128]{1,0:T(8,128)(2,1)S(1)} %get-tuple-element.38), channel_id=1, source_target_pairs={{0,392},{1,393},{64,456},{65,457},{128,0},{129,1},{192,64},{193,65... | collective-permute-start | bytes 196616 | tf_op jit(solution)/shard_map/cache_gather/ppermute | solution.py:189
  13.7 10.7 %collective-permute-start.1 = (bf16[256,128]{1,0:T(8,128)(2,1)S(1)}, bf16[256,128]{1,0:T(8,128)(2,1)S(1)}, u32[]{:S(2)}, u32[]{:S(2)}) collective-permute-start(bf16[256,128]{1,0:T(8,128)(2,1)S(1)} %get-tuple-element.37), channel_id=1, source_target_pairs={{0,128},{1,129},{64,192},{65,193},{128,256},{129,257},{192,320},{1... | collective-permute-start | bytes 196616 | tf_op jit(solution)/shard_map/cache_gather/ppermute | solution.py:189
  15.6 15.7 %collective-permute-start.2 = (bf16[256,128]{1,0:T(8,128)(2,1)S(1)}, bf16[256,128]{1,0:T(8,128)(2,1)S(1)}, u32[]{:S(2)}, u32[]{:S(2)}) collective-permute-start(bf16[256,128]{1,0:T(8,128)(2,1)S(1)} %get-tuple-element.40), channel_id=1, source_target_pairs={{0,264},{1,257},{64,328},{65,321},{128,392},{129,385},{192,456},{1... | collective-permute-start | bytes 196616 | tf_op jit(solution)/shard_map/cache_gather/ppermute | solution.py:189
  17.8 15.3 %collective-permute-start.4 = (bf16[256,128]{1,0:T(8,128)(2,1)S(1)}, bf16[256,128]{1,0:T(8,128)(2,1)S(1)}, u32[]{:S(2)}, u32[]{:S(2)}) collective-permute-start(bf16[256,128]{1,0:T(8,128)(2,1)S(1)} %get-tuple-element.36), channel_id=1, source_target_pairs={{0,328},{1,329},{64,256},{65,257},{128,456},{129,457},{192,384},{1... | collective-permute-start | bytes 196616 | tf_op jit(solution)/shard_map/cache_gather/ppermute | solution.py:189
  24.4 8.6 %collective-permute-start.3 = (bf16[768,128]{1,0:T(8,128)(2,1)S(1)}, bf16[768,128]{1,0:T(8,128)(2,1)S(1)}, u32[]{:S(2)}, u32[]{:S(2)}) collective-permute-start(bf16[768,128]{1,0:T(8,128)(2,1)S(1)} %pad_maximum_fusion.4), channel_id=1, source_target_pairs={{0,64},{64,0},{1,65},{65,1},{2,66},{66,2},{3,67},{67,3},{4,68},{68... | collective-permute-start | bytes 589832 | tf_op jit(solution)/shard_map/cache_gather/ppermute | solution.py:173
  28.3 4.0 %collective-permute-start.5 = (bf16[512,128]{1,0:T(8,128)(2,1)S(1)}, bf16[512,128]{1,0:T(8,128)(2,1)S(1)}, u32[]{:S(2)}, u32[]{:S(2)}) collective-permute-start(bf16[512,128]{1,0:T(8,128)(2,1)S(1)} %get-tuple-element.44), channel_id=1, source_target_pairs={{0,1},{1,0},{2,3},{3,2},{4,5},{5,4},{6,7},{7,6},{8,9},{9,8},{10,11... | collective-permute-start | bytes 393224 | tf_op jit(solution)/shard_map/weight_gather/ppermute | solution.py:173
  34.7 34.0 %all-to-all-start = ((bf16[4,2048,128]{2,1,0:T(8,128)(2,1)}), bf16[4,2048,128]{2,1,0:T(8,128)(2,1)}, u32[]{:S(2)}, u32[]{:S(2)}) async-start(bf16[4,2048,128]{2,1,0:T(8,128)(2,1)} %broadcast_in_dim.4), calls=%async_computation | async-start | bytes 4194304 | tf_op jit(solution)/shard_map/cache_gather/all_to_all | solution.py:169
  39.2 29.5 %collective-permute-start.6 = (bf16[1024,128]{1,0:T(8,128)(2,1)S(1)}, bf16[1024,128]{1,0:T(8,128)(2,1)S(1)}, u32[]{:S(2)}, u32[]{:S(2)}) collective-permute-start(bf16[1024,128]{1,0:T(8,128)(2,1)S(1)} %pad_maximum_fusion.3), channel_id=1, source_target_pairs={{0,256},{256,0},{1,257},{257,1},{2,258},{258,2},{3,259},{259,3},{4... | collective-permute-start | bytes 786440 | tf_op jit(solution)/shard_map/weight_gather/ppermute | solution.py:173
  68.7 9.9 %collective-permute-start.7 = (bf16[8192,128]{1,0:T(8,128)(2,1)}, bf16[8192,128]{1,0:T(8,128)(2,1)}, u32[]{:S(2)}, u32[]{:S(2)}) collective-permute-start(bf16[8192,128]{1,0:T(8,128)(2,1)} %bitcast.4.own_ref), channel_id=1, source_target_pairs={{0,1},{1,0},{2,3},{3,2},{4,5},{5,4},{6,7},{7,6},{8,9},{9,8},{10,11... | collective-permute-start | bytes 6291464 | tf_op jit(solution)/shard_map/cache_gather/ppermute | solution.py:173
  74.2 4.4 %copy-start.2 = (bf16[256,512]{1,0:T(8,128)(2,1)S(1)}, bf16[256,512]{1,0:T(8,128)(2,1)}, u32[]{:S(2)}) copy-start(bf16[256,512]{1,0:T(8,128)(2,1)} %q_ref.3) | copy-start | bytes 786436
  74.2 4.4 %copy-start.5 = (s32[32]{0:T(128)S(1)}, s32[32]{0:T(128)}, u32[]{:S(2)}) copy-start(s32[32]{0:T(128)} %counts.3) | copy-start | bytes 388
  74.2 4.4 %copy-start.6 = (s32[64]{0:T(128)S(1)}, s32[64]{0:T(128)}, u32[]{:S(2)}) copy-start(s32[64]{0:T(128)} %order.3) | copy-start | bytes 772
  74.2 30.5 %all-to-all-start.1 = ((bf16[4,2,1024,128]{3,2,1,0:T(8,128)(2,1)}), bf16[4,2,1024,128]{3,2,1,0:T(8,128)(2,1)S(1)}, u32[]{:S(2)}, u32[]{:S(2)}) async-start(bf16[4,2,1024,128]{3,2,1,0:T(8,128)(2,1)} %broadcast_in_dim.5), calls=%async_computation.1 | async-start | bytes 4194304 | tf_op jit(solution)/shard_map/weight_gather/all_to_all | solution.py:169
  84.8 16.1 %collective-permute-start.8 = (bf16[4,32,512]{2,1,0:T(8,128)(2,1)S(1)}, bf16[4,32,512]{2,1,0:T(8,128)(2,1)S(1)}, u32[]{:S(2)}, u32[]{:S(2)}) collective-permute-start(bf16[4,32,512]{2,1,0:T(8,128)(2,1)S(1)} %attention.2), channel_id=1, source_target_pairs={{0,192},{64,128},{128,64},{192,0},{1,193},{65,129},{129,65},{193,1... | collective-permute-start | bytes 393224 | tf_op jit(solution)/shard_map/rows_gather/ppermute | solution.py:177
  86.8 14.2 %collective-permute-start.9 = (bf16[4,32,512]{2,1,0:T(8,128)(2,1)S(1)}, bf16[4,32,512]{2,1,0:T(8,128)(2,1)S(1)}, u32[]{:S(2)}, u32[]{:S(2)}) collective-permute-start(bf16[4,32,512]{2,1,0:T(8,128)(2,1)S(1)} %attention.2), channel_id=1, source_target_pairs={{0,128},{64,192},{128,0},{192,64},{1,129},{65,193},{129,1},{193,65... | collective-permute-start | bytes 393224 | tf_op jit(solution)/shard_map/rows_gather/ppermute | solution.py:177
  88.7 12.2 %collective-permute-start.10 = (bf16[4,32,512]{2,1,0:T(8,128)(2,1)S(1)}, bf16[4,32,512]{2,1,0:T(8,128)(2,1)S(1)}, u32[]{:S(2)}, u32[]{:S(2)}) collective-permute-start(bf16[4,32,512]{2,1,0:T(8,128)(2,1)S(1)} %attention.2), channel_id=1, source_target_pairs={{0,64},{64,0},{128,192},{192,128},{1,65},{65,1},{129,193},{193,129... | collective-permute-start | bytes 393224 | tf_op jit(solution)/shard_map/rows_gather/ppermute | solution.py:177
  101.0 4.6 %collective-permute-start.11 = (bf16[4,4,32,512]{3,2,1,0:T(8,128)(2,1)S(1)}, bf16[4,4,32,512]{3,2,1,0:T(8,128)(2,1)S(1)}, u32[]{:S(2)}, u32[]{:S(2)}) collective-permute-start(bf16[4,4,32,512]{3,2,1,0:T(8,128)(2,1)S(1)} %pad_maximum_fusion.a_ref), channel_id=1, source_target_pairs={{0,1},{1,0},{2,3},{3,2},{4,5},{5,4},{6,7},{7,6},{8,9},{9,8},{10,11... | collective-permute-start | bytes 1572872 | tf_op jit(solution)/shard_map/rows_gather/ppermute | solution.py:173
  107.9 19.6 %all-to-all-start.2 = ((bf16[4,4,32,1024]{3,2,1,0:T(8,128)(2,1)}), bf16[4,4,32,1024]{3,2,1,0:T(8,128)(2,1)S(1)}, u32[]{:S(2)}, u32[]{:S(2)}) async-start(bf16[4,4,32,1024]{3,2,1,0:T(8,128)(2,1)} %projection.2), calls=%async_computation.2 | async-start | bytes 2097152 | tf_op jit(solution)/shard_map/sum_x/all_to_all | solution.py:255
  111.9 9.3 %collective-permute-start.12 = (bf16[4,32,512]{2,1,0:T(8,128)(2,1)S(1)}, bf16[4,32,512]{2,1,0:T(8,128)(2,1)S(1)}, u32[]{:S(2)}, u32[]{:S(2)}) collective-permute-start(bf16[4,32,512]{2,1,0:T(8,128)(2,1)S(1)} %attention.3), channel_id=1, source_target_pairs={{0,192},{64,128},{128,64},{192,0},{1,193},{65,129},{129,65},{193,1... | collective-permute-start | bytes 393224 | tf_op jit(solution)/shard_map/rows_gather/ppermute | solution.py:177
  114.1 12.5 %collective-permute-start.13 = (bf16[4,32,512]{2,1,0:T(8,128)(2,1)S(1)}, bf16[4,32,512]{2,1,0:T(8,128)(2,1)S(1)}, u32[]{:S(2)}, u32[]{:S(2)}) collective-permute-start(bf16[4,32,512]{2,1,0:T(8,128)(2,1)S(1)} %attention.3), channel_id=1, source_target_pairs={{0,128},{64,192},{128,0},{192,64},{1,129},{65,193},{129,1},{193,65... | collective-permute-start | bytes 393224 | tf_op jit(solution)/shard_map/rows_gather/ppermute | solution.py:177
  116.1 10.6 %collective-permute-start.14 = (bf16[4,32,512]{2,1,0:T(8,128)(2,1)S(1)}, bf16[4,32,512]{2,1,0:T(8,128)(2,1)S(1)}, u32[]{:S(2)}, u32[]{:S(2)}) collective-permute-start(bf16[4,32,512]{2,1,0:T(8,128)(2,1)S(1)} %attention.3), channel_id=1, source_target_pairs={{0,64},{64,0},{128,192},{192,128},{1,65},{65,1},{129,193},{193,129... | collective-permute-start | bytes 393224 | tf_op jit(solution)/shard_map/rows_gather/ppermute | solution.py:177
  127.8 0.8 copy-start
  128.6 35.8 %all-to-all-start.3 = ((bf16[2,4,32,1024]{3,2,1,0:T(8,128)(2,1)}), bf16[2,4,32,1024]{3,2,1,0:T(8,128)(2,1)}, u32[]{:S(2)}, u32[]{:S(2)}) async-start(bf16[2,4,32,1024]{3,2,1,0:T(8,128)(2,1)} %copy-done), calls=%async_computation.3 | async-start | bytes 1048576 | tf_op jit(solution)/shard_map/sum_zh/all_to_all | solution.py:259
  135.9 5.6 %collective-permute-start.15 = (bf16[4,4,32,512]{3,2,1,0:T(8,128)(2,1)}, bf16[4,4,32,512]{3,2,1,0:T(8,128)(2,1)S(1)}, u32[]{:S(2)}, u32[]{:S(2)}) collective-permute-start(bf16[4,4,32,512]{3,2,1,0:T(8,128)(2,1)} %pad_maximum_fusion.2.a_ref), channel_id=1, source_target_pairs={{0,1},{1,0},{2,3},{3,2},{4,5},{5,4},{6,7},{7,6},{8,9},{9,8},{10,11... | collective-permute-start | bytes 1572872 | tf_op jit(solution)/shard_map/sum_x/ppermute | solution.py:173
  141.4 0.8 copy-start.3
  142.2 1.0 copy-start.1
  143.3 1.0 copy-start.4
  145.9 10.8 %collective-permute-start.16 = (bf16[4,32,1024]{2,1,0:T(8,128)(2,1)S(1)}, bf16[4,32,1024]{2,1,0:T(8,128)(2,1)S(1)}, u32[]{:S(2)}, u32[]{:S(2)}) collective-permute-start(bf16[4,32,1024]{2,1,0:T(8,128)(2,1)S(1)} %get-tuple-element.33), channel_id=1, source_target_pairs={{6,0},{0,2},{2,4},{4,6},{7,1},{1,3},{3,5},{5,7},{14,8},{8,10},{10,... | collective-permute-start | bytes 786440 | tf_op jit(solution)/shard_map/sum_x/ppermute | solution.py:181
  149.3 14.0 %collective-permute-start.17 = (bf16[4,32,1024]{2,1,0:T(8,128)(2,1)S(1)}, bf16[4,32,1024]{2,1,0:T(8,128)(2,1)S(1)}, u32[]{:S(2)}, u32[]{:S(2)}) collective-permute-start(bf16[4,32,1024]{2,1,0:T(8,128)(2,1)S(1)} %get-tuple-element.35), channel_id=1, source_target_pairs={{4,0},{6,2},{0,4},{2,6},{5,1},{7,3},{1,5},{3,7},{12,8},{14,10},{8,... | collective-permute-start | bytes 786440 | tf_op jit(solution)/shard_map/sum_x/ppermute | solution.py:181
  153.6 10.7 %collective-permute-start.18 = (bf16[4,32,1024]{2,1,0:T(8,128)(2,1)S(1)}, bf16[4,32,1024]{2,1,0:T(8,128)(2,1)S(1)}, u32[]{:S(2)}, u32[]{:S(2)}) collective-permute-start(bf16[4,32,1024]{2,1,0:T(8,128)(2,1)S(1)} %get-tuple-element.34), channel_id=1, source_target_pairs={{2,0},{4,2},{6,4},{0,6},{3,1},{5,3},{7,5},{1,7},{10,8},{12,10},{14... | collective-permute-start | bytes 786440 | tf_op jit(solution)/shard_map/sum_x/ppermute | solution.py:181

commit v8 on v7

--- a/solution.py
+++ b/solution.py
@@ -41,7 +41,7 @@
             last = j + 1 >= counts[d]
             return jnp.where(last, jnp.minimum(d + 1, N_SEQ - 1), d), jnp.where(last, 0, j + 1)
 
-        lax.fori_loop(0, PAGES, one, (jnp.int32(0), jnp.int32(0)), unroll=4)
+        lax.fori_loop(0, PAGES, one, (jnp.int32(0), jnp.int32(0)), unroll=PAGES)
 
     before = lax.fori_loop(0, me, lambda d, s: s + counts[d], jnp.int32(0))
     live = counts[me]
@@ -96,10 +96,9 @@
                 0, full, lambda i, s: step(pl.multiple_of(i * CHUNK, CHUNK), s, False, CHUNK), state
             )
             rest = pl.multiple_of(full * CHUNK, CHUNK)
-            state = lax.cond(
-                page % (CHUNK // PAGE) < CHUNK // PAGE // 2,
-                lambda s: step(rest, s, True, CHUNK // 2),
-                lambda s: step(rest, s, True, CHUNK),
+            state = lax.switch(
+                page % (CHUNK // PAGE) // (CHUNK // PAGE // 4),
+                [lambda s, n=n: step(rest, s, True, (n + 1) * CHUNK // 4) for n in range(4)],
                 state,
             )
             _, total, accum = state

time: 183 us -> 184 us (level)
  starting transfers between devices: 93.5 us -> 95.4 us
  transfers between devices with their start and end apart: 23 -> 23, of which waited for: 9 -> 10; matrix products, arithmetic and copies ran while one was open for 2% -> 2% of each run, Pallas kernels for 8% -> 8%
where the time goes in v8:
time: 184 us; the launch traced here: 183 us
  starting transfers between devices  95.4 us (52%)
  waiting for transfers between devices  44 us (24%)
  Pallas kernels  16.4 us (9%)
  blocking collectives  14.4 us (8%)
  local copies, waits for them, and re-layouts  8.44 us (5%)
  other arithmetic  3.66 us (2%)
    ppermute x6, waiting for transfers between devices, swap(): return lax.ppermute(piece, axis, [(0, 1), (1, 0)])  29.6 us
    ppermute x4, starting transfers between devices, along(): return lax.ppermute(piece, LINE, perm)  23.1 us
    ppermute x6, starting transfers between devices, swap(): return lax.ppermute(piece, axis, [(0, 1), (1, 0)])  21 us
    ppermute x6, starting transfers between devices, quad(): lax.ppermute(piece, ('zb', 'zq'), [(i, i ^ step) for i in range(QUAD)])  18.5 us
    all_to_all x1, blocking collectives, body(): lax.all_to_all(mixed.reshape(QUAD * C, 16, ZL * HD), ('zb', 'zq', 'c'), 0...  14.4 us
    pallas_call x2, Pallas kernels, attend(): pl.pallas_call(attention_kernel, out_shape=jax.ShapeDtypeStruct((X, 32, H...  12.3 us
    ppermute x3, starting transfers between devices, around(): lax.ppermute(piece, axis, [((i + shift) % count, i) for i in range(count)])  10.9 us
    all_to_all x1, starting transfers between devices, body(): back = lax.all_to_all(away, 'zh', 0, 0)  9.05 us
  transfers between devices with their start and end apart: 23, of which 10 were waited for; matrix products, arithmetic and copies ran while one was open for 2% of the time, Pallas kernels for 8%

profile of v8, /device:TPU:1, one launch (start us, length us, event | category | flops | bytes accessed | tf_op | source)
XLA Modules:
  0.0 182.8 jit_solution(2335352739887675952)
XLA Ops:
  1.3 12.4 %collective-permute-start = (bf16[256,128]{1,0:T(8,128)(2,1)S(1)}, bf16[256,128]{1,0:T(8,128)(2,1)S(1)}, u32[]{:S(2)}, u32[]{:S(2)}) collective-permute-start(bf16[256,128]{1,0:T(8,128)(2,1)S(1)} %get-tuple-element.38), channel_id=1, source_target_pairs={{0,392},{1,393},{64,456},{65,457},{128,0},{129,1},{192,64},{193,65... | collective-permute-start | bytes 196616 | tf_op jit(solution)/shard_map/cache_gather/ppermute | solution.py:188
  13.7 1.9 %collective-permute-start.1 = (bf16[256,128]{1,0:T(8,128)(2,1)S(1)}, bf16[256,128]{1,0:T(8,128)(2,1)S(1)}, u32[]{:S(2)}, u32[]{:S(2)}) collective-permute-start(bf16[256,128]{1,0:T(8,128)(2,1)S(1)} %get-tuple-element.37), channel_id=1, source_target_pairs={{0,128},{1,129},{64,192},{65,193},{128,256},{129,257},{192,320},{1... | collective-permute-start | bytes 196616 | tf_op jit(solution)/shard_map/cache_gather/ppermute | solution.py:188
  15.6 2.1 %collective-permute-start.2 = (bf16[256,128]{1,0:T(8,128)(2,1)S(1)}, bf16[256,128]{1,0:T(8,128)(2,1)S(1)}, u32[]{:S(2)}, u32[]{:S(2)}) collective-permute-start(bf16[256,128]{1,0:T(8,128)(2,1)S(1)} %get-tuple-element.40), channel_id=1, source_target_pairs={{0,264},{1,257},{64,328},{65,321},{128,392},{129,385},{192,456},{1... | collective-permute-start | bytes 196616 | tf_op jit(solution)/shard_map/cache_gather/ppermute | solution.py:188
  17.8 6.6 %collective-permute-start.4 = (bf16[256,128]{1,0:T(8,128)(2,1)S(1)}, bf16[256,128]{1,0:T(8,128)(2,1)S(1)}, u32[]{:S(2)}, u32[]{:S(2)}) collective-permute-start(bf16[256,128]{1,0:T(8,128)(2,1)S(1)} %get-tuple-element.36), channel_id=1, source_target_pairs={{0,328},{1,329},{64,256},{65,257},{128,456},{129,457},{192,384},{1... | collective-permute-start | bytes 196616 | tf_op jit(solution)/shard_map/cache_gather/ppermute | solution.py:188
  24.4 3.8 %collective-permute-start.3 = (bf16[768,128]{1,0:T(8,128)(2,1)S(1)}, bf16[768,128]{1,0:T(8,128)(2,1)S(1)}, u32[]{:S(2)}, u32[]{:S(2)}) collective-permute-start(bf16[768,128]{1,0:T(8,128)(2,1)S(1)} %pad_maximum_fusion.4), channel_id=1, source_target_pairs={{0,64},{64,0},{1,65},{65,1},{2,66},{66,2},{3,67},{67,3},{4,68},{68... | collective-permute-start | bytes 589832 | tf_op jit(solution)/shard_map/cache_gather/ppermute | solution.py:172
  28.3 3.0 %collective-permute-start.5 = (bf16[512,128]{1,0:T(8,128)(2,1)S(1)}, bf16[512,128]{1,0:T(8,128)(2,1)S(1)}, u32[]{:S(2)}, u32[]{:S(2)}) collective-permute-start(bf16[512,128]{1,0:T(8,128)(2,1)S(1)} %get-tuple-element.44), channel_id=1, source_target_pairs={{0,1},{1,0},{2,3},{3,2},{4,5},{5,4},{6,7},{7,6},{8,9},{9,8},{10,11... | collective-permute-start | bytes 393224 | tf_op jit(solution)/shard_map/weight_gather/ppermute | solution.py:172
  34.7 4.4 %all-to-all-start = ((bf16[4,2048,128]{2,1,0:T(8,128)(2,1)}), bf16[4,2048,128]{2,1,0:T(8,128)(2,1)}, u32[]{:S(2)}, u32[]{:S(2)}) async-start(bf16[4,2048,128]{2,1,0:T(8,128)(2,1)} %broadcast_in_dim.4), calls=%async_computation | async-start | bytes 4194304 | tf_op jit(solution)/shard_map/cache_gather/all_to_all | solution.py:168
  39.2 3.7 %collective-permute-start.6 = (bf16[1024,128]{1,0:T(8,128)(2,1)S(1)}, bf16[1024,128]{1,0:T(8,128)(2,1)S(1)}, u32[]{:S(2)}, u32[]{:S(2)}) collective-permute-start(bf16[1024,128]{1,0:T(8,128)(2,1)S(1)} %pad_maximum_fusion.3), channel_id=1, source_target_pairs={{0,256},{256,0},{1,257},{257,1},{2,258},{258,2},{3,259},{259,3},{4... | collective-permute-start | bytes 786440 | tf_op jit(solution)/shard_map/weight_gather/ppermute | solution.py:172
  42.9 25.9 %collective-permute-done.6 = bf16[1024,128]{1,0:T(8,128)(2,1)S(1)} collective-permute-done((bf16[1024,128]{1,0:T(8,128)(2,1)S(1)}, bf16[1024,128]{1,0:T(8,128)(2,1)S(1)}, u32[]{:S(2)}, u32[]{:S(2)}) %collective-permute-start.6) | collective-permute-done | bytes 262176 | tf_op jit(solution)/shard_map/weight_gather/ppermute | solution.py:172
  68.8 3.7 %collective-permute-start.7 = (bf16[8192,128]{1,0:T(8,128)(2,1)}, bf16[8192,128]{1,0:T(8,128)(2,1)}, u32[]{:S(2)}, u32[]{:S(2)}) collective-permute-start(bf16[8192,128]{1,0:T(8,128)(2,1)} %bitcast.4.own_ref), channel_id=1, source_target_pairs={{0,1},{1,0},{2,3},{3,2},{4,5},{5,4},{6,7},{7,6},{8,9},{9,8},{10,11... | collective-permute-start | bytes 6291464 | tf_op jit(solution)/shard_map/cache_gather/ppermute | solution.py:172
  72.6 1.6 broadcast_in_dim.5
  74.2 4.3 %all-to-all-start.1 = ((bf16[4,2,1024,128]{3,2,1,0:T(8,128)(2,1)}), bf16[4,2,1024,128]{3,2,1,0:T(8,128)(2,1)S(1)}, u32[]{:S(2)}, u32[]{:S(2)}) async-start(bf16[4,2,1024,128]{3,2,1,0:T(8,128)(2,1)} %broadcast_in_dim.5), calls=%async_computation.1 | async-start | bytes 4194304 | tf_op jit(solution)/shard_map/weight_gather/all_to_all | solution.py:168
  78.6 4.4 %attention.2 = bf16[4,32,512]{2,1,0:T(8,128)(2,1)S(1)} custom-call(s32[32]{0:T(128)S(1)} %copy-done.5, s32[64]{0:T(128)S(1)} %copy-done.6, s32[3]{0:T(128)S(1)} %pad_add_fusion.place, bf16[256,512]{1,0:T(8,128)(2,1)S(1)} %copy-done.2, bf16[8192,128]{1,0:T(8,128)(2,1)} %bitcast.4.own_ref, bf16[8192,128]{1,0:T(8,128)(2,1)} %collective-permute-done.7.other_ref), custom_call_target="tpu_custom_call" | custom-call | tf_op jit(solution)/shard_map/attention/pallas_call | solution.py:116
  83.0 1.9 %collective-permute-start.8 = (bf16[4,32,512]{2,1,0:T(8,128)(2,1)S(1)}, bf16[4,32,512]{2,1,0:T(8,128)(2,1)S(1)}, u32[]{:S(2)}, u32[]{:S(2)}) collective-permute-start(bf16[4,32,512]{2,1,0:T(8,128)(2,1)S(1)} %attention.2), channel_id=1, source_target_pairs={{0,192},{64,128},{128,64},{192,0},{1,193},{65,129},{129,65},{193,1... | collective-permute-start | bytes 393224 | tf_op jit(solution)/shard_map/rows_gather/ppermute | solution.py:176
  84.9 1.9 %collective-permute-start.9 = (bf16[4,32,512]{2,1,0:T(8,128)(2,1)S(1)}, bf16[4,32,512]{2,1,0:T(8,128)(2,1)S(1)}, u32[]{:S(2)}, u32[]{:S(2)}) collective-permute-start(bf16[4,32,512]{2,1,0:T(8,128)(2,1)S(1)} %attention.2), channel_id=1, source_target_pairs={{0,128},{64,192},{128,0},{192,64},{1,129},{65,193},{129,1},{193,65... | collective-permute-start | bytes 393224 | tf_op jit(solution)/shard_map/rows_gather/ppermute | solution.py:176
  86.9 5.4 %collective-permute-start.10 = (bf16[4,32,512]{2,1,0:T(8,128)(2,1)S(1)}, bf16[4,32,512]{2,1,0:T(8,128)(2,1)S(1)}, u32[]{:S(2)}, u32[]{:S(2)}) collective-permute-start(bf16[4,32,512]{2,1,0:T(8,128)(2,1)S(1)} %attention.2), channel_id=1, source_target_pairs={{0,64},{64,0},{128,192},{192,128},{1,65},{65,1},{129,193},{193,129... | collective-permute-start | bytes 393224 | tf_op jit(solution)/shard_map/rows_gather/ppermute | solution.py:176
  92.4 7.9 %attention.3 = bf16[4,32,512]{2,1,0:T(8,128)(2,1)S(1)} custom-call(s32[32]{0:T(128)S(1)} %copy-done.5, s32[64]{0:T(128)S(1)} %copy-done.6, s32[3]{0:T(128)S(1)} %pad_add_fusion.2.place, bf16[256,512]{1,0:T(8,128)(2,1)S(1)} %copy-done.2, bf16[8192,128]{1,0:T(8,128)(2,1)} %bitcast.4.own_ref, bf16[8192,128]{1,0:T(8,128)(2,1)} %collective-permute-done.7.other_ref), custom_call_target="tpu_custom_call" | custom-call | tf_op jit(solution)/shard_map/attention/pallas_call | solution.py:116
  100.5 3.0 %collective-permute-start.11 = (bf16[4,4,32,512]{3,2,1,0:T(8,128)(2,1)S(1)}, bf16[4,4,32,512]{3,2,1,0:T(8,128)(2,1)S(1)}, u32[]{:S(2)}, u32[]{:S(2)}) collective-permute-start(bf16[4,4,32,512]{3,2,1,0:T(8,128)(2,1)S(1)} %pad_maximum_fusion.a_ref), channel_id=1, source_target_pairs={{0,1},{1,0},{2,3},{3,2},{4,5},{5,4},{6,7},{7,6},{8,9},{9,8},{10,11... | collective-permute-start | bytes 1572872 | tf_op jit(solution)/shard_map/rows_gather/ppermute | solution.py:172
  105.0 2.3 %projection.2 = bf16[4,4,32,1024]{3,2,1,0:T(8,128)(2,1)} custom-call(s32[1]{0:T(128)} %bitcast.me, bf16[4,4,32,512]{3,2,1,0:T(8,128)(2,1)S(1)} %pad_maximum_fusion.a_ref, bf16[4,4,32,512]{3,2,1,0:T(8,128)(2,1)S(1)} %collective-permute-done.11.b_ref, bf16[4,2,1024,128]{3,2,1,0:T(8,128)(2,1)S(1)} %all-to-all-done.1.w_ref), custom_call_target="tpu_custom_call" | custom-call | tf_op jit(solution)/shard_map/projection/pallas_call | solution.py:138
  107.3 4.0 %all-to-all-start.2 = ((bf16[4,4,32,1024]{3,2,1,0:T(8,128)(2,1)}), bf16[4,4,32,1024]{3,2,1,0:T(8,128)(2,1)S(1)}, u32[]{:S(2)}, u32[]{:S(2)}) async-start(bf16[4,4,32,1024]{3,2,1,0:T(8,128)(2,1)} %projection.2), calls=%async_computation.2 | async-start | bytes 2097152 | tf_op jit(solution)/shard_map/sum_x/all_to_all | solution.py:254
  111.3 1.9 %collective-permute-start.12 = (bf16[4,32,512]{2,1,0:T(8,128)(2,1)S(1)}, bf16[4,32,512]{2,1,0:T(8,128)(2,1)S(1)}, u32[]{:S(2)}, u32[]{:S(2)}) collective-permute-start(bf16[4,32,512]{2,1,0:T(8,128)(2,1)S(1)} %attention.3), channel_id=1, source_target_pairs={{0,192},{64,128},{128,64},{192,0},{1,193},{65,129},{129,65},{193,1... | collective-permute-start | bytes 393224 | tf_op jit(solution)/shard_map/rows_gather/ppermute | solution.py:176
  113.2 2.2 %collective-permute-start.13 = (bf16[4,32,512]{2,1,0:T(8,128)(2,1)S(1)}, bf16[4,32,512]{2,1,0:T(8,128)(2,1)S(1)}, u32[]{:S(2)}, u32[]{:S(2)}) collective-permute-start(bf16[4,32,512]{2,1,0:T(8,128)(2,1)S(1)} %attention.3), channel_id=1, source_target_pairs={{0,128},{64,192},{128,0},{192,64},{1,129},{65,193},{129,1},{193,65... | collective-permute-start | bytes 393224 | tf_op jit(solution)/shard_map/rows_gather/ppermute | solution.py:176
  115.4 5.2 %collective-permute-start.14 = (bf16[4,32,512]{2,1,0:T(8,128)(2,1)S(1)}, bf16[4,32,512]{2,1,0:T(8,128)(2,1)S(1)}, u32[]{:S(2)}, u32[]{:S(2)}) collective-permute-start(bf16[4,32,512]{2,1,0:T(8,128)(2,1)S(1)} %attention.3), channel_id=1, source_target_pairs={{0,64},{64,0},{128,192},{192,128},{1,65},{65,1},{129,193},{193,129... | collective-permute-start | bytes 393224 | tf_op jit(solution)/shard_map/rows_gather/ppermute | solution.py:176
  120.6 5.4 %collective-permute-done.13 = bf16[4,32,512]{2,1,0:T(8,128)(2,1)S(1)} collective-permute-done((bf16[4,32,512]{2,1,0:T(8,128)(2,1)S(1)}, bf16[4,32,512]{2,1,0:T(8,128)(2,1)S(1)}, u32[]{:S(2)}, u32[]{:S(2)}) %collective-permute-start.13) | collective-permute-done | bytes 131104 | tf_op jit(solution)/shard_map/rows_gather/ppermute | solution.py:176
  128.0 9.1 %all-to-all-start.3 = ((bf16[2,4,32,1024]{3,2,1,0:T(8,128)(2,1)}), bf16[2,4,32,1024]{3,2,1,0:T(8,128)(2,1)}, u32[]{:S(2)}, u32[]{:S(2)}) async-start(bf16[2,4,32,1024]{3,2,1,0:T(8,128)(2,1)} %copy-done), calls=%async_computation.3 | async-start | bytes 1048576 | tf_op jit(solution)/shard_map/sum_zh/all_to_all | solution.py:258
  137.0 3.8 %collective-permute-start.15 = (bf16[4,4,32,512]{3,2,1,0:T(8,128)(2,1)}, bf16[4,4,32,512]{3,2,1,0:T(8,128)(2,1)S(1)}, u32[]{:S(2)}, u32[]{:S(2)}) collective-permute-start(bf16[4,4,32,512]{3,2,1,0:T(8,128)(2,1)} %pad_maximum_fusion.2.a_ref), channel_id=1, source_target_pairs={{0,1},{1,0},{2,3},{3,2},{4,5},{5,4},{6,7},{7,6},{8,9},{9,8},{10,11... | collective-permute-start | bytes 1572872 | tf_op jit(solution)/shard_map/sum_x/ppermute | solution.py:172
  140.9 1.7 collective-permute-done.15.b_ref
  147.1 3.5 %collective-permute-start.16 = (bf16[4,32,1024]{2,1,0:T(8,128)(2,1)S(1)}, bf16[4,32,1024]{2,1,0:T(8,128)(2,1)S(1)}, u32[]{:S(2)}, u32[]{:S(2)}) collective-permute-start(bf16[4,32,1024]{2,1,0:T(8,128)(2,1)S(1)} %get-tuple-element.33), channel_id=1, source_target_pairs={{6,0},{0,2},{2,4},{4,6},{7,1},{1,3},{3,5},{5,7},{14,8},{8,10},{10,... | collective-permute-start | bytes 786440 | tf_op jit(solution)/shard_map/sum_x/ppermute | solution.py:180
  150.6 4.3 %collective-permute-start.17 = (bf16[4,32,1024]{2,1,0:T(8,128)(2,1)S(1)}, bf16[4,32,1024]{2,1,0:T(8,128)(2,1)S(1)}, u32[]{:S(2)}, u32[]{:S(2)}) collective-permute-start(bf16[4,32,1024]{2,1,0:T(8,128)(2,1)S(1)} %get-tuple-element.35), channel_id=1, source_target_pairs={{4,0},{6,2},{0,4},{2,6},{5,1},{7,3},{1,5},{3,7},{12,8},{14,10},{8,... | collective-permute-start | bytes 786440 | tf_op jit(solution)/shard_map/sum_x/ppermute | solution.py:180
  155.0 3.1 %collective-permute-start.18 = (bf16[4,32,1024]{2,1,0:T(8,128)(2,1)S(1)}, bf16[4,32,1024]{2,1,0:T(8,128)(2,1)S(1)}, u32[]{:S(2)}, u32[]{:S(2)}) collective-permute-start(bf16[4,32,1024]{2,1,0:T(8,128)(2,1)S(1)} %get-tuple-element.34), channel_id=1, source_target_pairs={{2,0},{4,2},{6,4},{0,6},{3,1},{5,3},{7,5},{1,7},{10,8},{12,10},{14... | collective-permute-start | bytes 786440 | tf_op jit(solution)/shard_map/sum_x/ppermute | solution.py:180
  158.2 6.5 %collective-permute-done.17 = bf16[4,32,1024]{2,1,0:T(8,128)(2,1)S(1)} collective-permute-done((bf16[4,32,1024]{2,1,0:T(8,128)(2,1)S(1)}, bf16[4,32,1024]{2,1,0:T(8,128)(2,1)S(1)}, u32[]{:S(2)}, u32[]{:S(2)}) %collective-permute-start.17) | collective-permute-done | bytes 262176 | tf_op jit(solution)/shard_map/sum_x/ppermute | solution.py:180
  167.1 14.4 %all_to_all.25 = bf16[8,16,1024]{2,1,0:T(8,128)(2,1)S(1)} all-to-all(bf16[8,16,1024]{2,1,0:T(8,128)(2,1)S(1)} %bitcast.37), channel_id=1, replica_groups=mesh['za'=2,'zb'=2,'zq'=2,'y'=4,'zh'=2,'x'=4,'c'=2] {'zb','zq','c'}, dimensions={0} | all-to-all | bytes 524288 | tf_op jit(solution)/shard_map/columns/all_to_all | solution.py:267
  (59 shorter events, 16.9 us)
Async XLA Ops:
  0.0 28.2 %copy-start.7 = (bf16[512,256]{1,0:T(8,128)(2,1)S(1)}, bf16[512,256]{1,0:T(8,128)(2,1)}, u32[]{:S(2)}) copy-start(bf16[512,256]{1,0:T(8,128)(2,1)} %param.11) | copy-start | bytes 786436
  1.3 23.1 %collective-permute-start = (bf16[256,128]{1,0:T(8,128)(2,1)S(1)}, bf16[256,128]{1,0:T(8,128)(2,1)S(1)}, u32[]{:S(2)}, u32[]{:S(2)}) collective-permute-start(bf16[256,128]{1,0:T(8,128)(2,1)S(1)} %get-tuple-element.38), channel_id=1, source_target_pairs={{0,392},{1,393},{64,456},{65,457},{128,0},{129,1},{192,64},{193,65... | collective-permute-start | bytes 196616 | tf_op jit(solution)/shard_map/cache_gather/ppermute | solution.py:188
  13.7 10.7 %collective-permute-start.1 = (bf16[256,128]{1,0:T(8,128)(2,1)S(1)}, bf16[256,128]{1,0:T(8,128)(2,1)S(1)}, u32[]{:S(2)}, u32[]{:S(2)}) collective-permute-start(bf16[256,128]{1,0:T(8,128)(2,1)S(1)} %get-tuple-element.37), channel_id=1, source_target_pairs={{0,128},{1,129},{64,192},{65,193},{128,256},{129,257},{192,320},{1... | collective-permute-start | bytes 196616 | tf_op jit(solution)/shard_map/cache_gather/ppermute | solution.py:188
  15.6 15.7 %collective-permute-start.2 = (bf16[256,128]{1,0:T(8,128)(2,1)S(1)}, bf16[256,128]{1,0:T(8,128)(2,1)S(1)}, u32[]{:S(2)}, u32[]{:S(2)}) collective-permute-start(bf16[256,128]{1,0:T(8,128)(2,1)S(1)} %get-tuple-element.40), channel_id=1, source_target_pairs={{0,264},{1,257},{64,328},{65,321},{128,392},{129,385},{192,456},{1... | collective-permute-start | bytes 196616 | tf_op jit(solution)/shard_map/cache_gather/ppermute | solution.py:188
  17.8 15.3 %collective-permute-start.4 = (bf16[256,128]{1,0:T(8,128)(2,1)S(1)}, bf16[256,128]{1,0:T(8,128)(2,1)S(1)}, u32[]{:S(2)}, u32[]{:S(2)}) collective-permute-start(bf16[256,128]{1,0:T(8,128)(2,1)S(1)} %get-tuple-element.36), channel_id=1, source_target_pairs={{0,328},{1,329},{64,256},{65,257},{128,456},{129,457},{192,384},{1... | collective-permute-start | bytes 196616 | tf_op jit(solution)/shard_map/cache_gather/ppermute | solution.py:188
  24.4 8.6 %collective-permute-start.3 = (bf16[768,128]{1,0:T(8,128)(2,1)S(1)}, bf16[768,128]{1,0:T(8,128)(2,1)S(1)}, u32[]{:S(2)}, u32[]{:S(2)}) collective-permute-start(bf16[768,128]{1,0:T(8,128)(2,1)S(1)} %pad_maximum_fusion.4), channel_id=1, source_target_pairs={{0,64},{64,0},{1,65},{65,1},{2,66},{66,2},{3,67},{67,3},{4,68},{68... | collective-permute-start | bytes 589832 | tf_op jit(solution)/shard_map/cache_gather/ppermute | solution.py:172
  28.3 4.0 %collective-permute-start.5 = (bf16[512,128]{1,0:T(8,128)(2,1)S(1)}, bf16[512,128]{1,0:T(8,128)(2,1)S(1)}, u32[]{:S(2)}, u32[]{:S(2)}) collective-permute-start(bf16[512,128]{1,0:T(8,128)(2,1)S(1)} %get-tuple-element.44), channel_id=1, source_target_pairs={{0,1},{1,0},{2,3},{3,2},{4,5},{5,4},{6,7},{7,6},{8,9},{9,8},{10,11... | collective-permute-start | bytes 393224 | tf_op jit(solution)/shard_map/weight_gather/ppermute | solution.py:172
  34.7 34.1 %all-to-all-start = ((bf16[4,2048,128]{2,1,0:T(8,128)(2,1)}), bf16[4,2048,128]{2,1,0:T(8,128)(2,1)}, u32[]{:S(2)}, u32[]{:S(2)}) async-start(bf16[4,2048,128]{2,1,0:T(8,128)(2,1)} %broadcast_in_dim.4), calls=%async_computation | async-start | bytes 4194304 | tf_op jit(solution)/shard_map/cache_gather/all_to_all | solution.py:168
  39.2 29.6 %collective-permute-start.6 = (bf16[1024,128]{1,0:T(8,128)(2,1)S(1)}, bf16[1024,128]{1,0:T(8,128)(2,1)S(1)}, u32[]{:S(2)}, u32[]{:S(2)}) collective-permute-start(bf16[1024,128]{1,0:T(8,128)(2,1)S(1)} %pad_maximum_fusion.3), channel_id=1, source_target_pairs={{0,256},{256,0},{1,257},{257,1},{2,258},{258,2},{3,259},{259,3},{4... | collective-permute-start | bytes 786440 | tf_op jit(solution)/shard_map/weight_gather/ppermute | solution.py:172
  68.8 9.8 %collective-permute-start.7 = (bf16[8192,128]{1,0:T(8,128)(2,1)}, bf16[8192,128]{1,0:T(8,128)(2,1)}, u32[]{:S(2)}, u32[]{:S(2)}) collective-permute-start(bf16[8192,128]{1,0:T(8,128)(2,1)} %bitcast.4.own_ref), channel_id=1, source_target_pairs={{0,1},{1,0},{2,3},{3,2},{4,5},{5,4},{6,7},{7,6},{8,9},{9,8},{10,11... | collective-permute-start | bytes 6291464 | tf_op jit(solution)/shard_map/cache_gather/ppermute | solution.py:172
  74.2 4.4 %copy-start.2 = (bf16[256,512]{1,0:T(8,128)(2,1)S(1)}, bf16[256,512]{1,0:T(8,128)(2,1)}, u32[]{:S(2)}) copy-start(bf16[256,512]{1,0:T(8,128)(2,1)} %q_ref.3) | copy-start | bytes 786436
  74.2 4.4 %copy-start.5 = (s32[32]{0:T(128)S(1)}, s32[32]{0:T(128)}, u32[]{:S(2)}) copy-start(s32[32]{0:T(128)} %counts.3) | copy-start | bytes 388
  74.2 4.4 %copy-start.6 = (s32[64]{0:T(128)S(1)}, s32[64]{0:T(128)}, u32[]{:S(2)}) copy-start(s32[64]{0:T(128)} %order.3) | copy-start | bytes 772
  74.2 30.5 %all-to-all-start.1 = ((bf16[4,2,1024,128]{3,2,1,0:T(8,128)(2,1)}), bf16[4,2,1024,128]{3,2,1,0:T(8,128)(2,1)S(1)}, u32[]{:S(2)}, u32[]{:S(2)}) async-start(bf16[4,2,1024,128]{3,2,1,0:T(8,128)(2,1)} %broadcast_in_dim.5), calls=%async_computation.1 | async-start | bytes 4194304 | tf_op jit(solution)/shard_map/weight_gather/all_to_all | solution.py:168
  83.0 17.3 %collective-permute-start.8 = (bf16[4,32,512]{2,1,0:T(8,128)(2,1)S(1)}, bf16[4,32,512]{2,1,0:T(8,128)(2,1)S(1)}, u32[]{:S(2)}, u32[]{:S(2)}) collective-permute-start(bf16[4,32,512]{2,1,0:T(8,128)(2,1)S(1)} %attention.2), channel_id=1, source_target_pairs={{0,192},{64,128},{128,64},{192,0},{1,193},{65,129},{129,65},{193,1... | collective-permute-start | bytes 393224 | tf_op jit(solution)/shard_map/rows_gather/ppermute | solution.py:176
  84.9 15.4 %collective-permute-start.9 = (bf16[4,32,512]{2,1,0:T(8,128)(2,1)S(1)}, bf16[4,32,512]{2,1,0:T(8,128)(2,1)S(1)}, u32[]{:S(2)}, u32[]{:S(2)}) collective-permute-start(bf16[4,32,512]{2,1,0:T(8,128)(2,1)S(1)} %attention.2), channel_id=1, source_target_pairs={{0,128},{64,192},{128,0},{192,64},{1,129},{65,193},{129,1},{193,65... | collective-permute-start | bytes 393224 | tf_op jit(solution)/shard_map/rows_gather/ppermute | solution.py:176
  86.9 13.5 %collective-permute-start.10 = (bf16[4,32,512]{2,1,0:T(8,128)(2,1)S(1)}, bf16[4,32,512]{2,1,0:T(8,128)(2,1)S(1)}, u32[]{:S(2)}, u32[]{:S(2)}) collective-permute-start(bf16[4,32,512]{2,1,0:T(8,128)(2,1)S(1)} %attention.2), channel_id=1, source_target_pairs={{0,64},{64,0},{128,192},{192,128},{1,65},{65,1},{129,193},{193,129... | collective-permute-start | bytes 393224 | tf_op jit(solution)/shard_map/rows_gather/ppermute | solution.py:176
  100.5 4.6 %collective-permute-start.11 = (bf16[4,4,32,512]{3,2,1,0:T(8,128)(2,1)S(1)}, bf16[4,4,32,512]{3,2,1,0:T(8,128)(2,1)S(1)}, u32[]{:S(2)}, u32[]{:S(2)}) collective-permute-start(bf16[4,4,32,512]{3,2,1,0:T(8,128)(2,1)S(1)} %pad_maximum_fusion.a_ref), channel_id=1, source_target_pairs={{0,1},{1,0},{2,3},{3,2},{4,5},{5,4},{6,7},{7,6},{8,9},{9,8},{10,11... | collective-permute-start | bytes 1572872 | tf_op jit(solution)/shard_map/rows_gather/ppermute | solution.py:172
  107.3 19.6 %all-to-all-start.2 = ((bf16[4,4,32,1024]{3,2,1,0:T(8,128)(2,1)}), bf16[4,4,32,1024]{3,2,1,0:T(8,128)(2,1)S(1)}, u32[]{:S(2)}, u32[]{:S(2)}) async-start(bf16[4,4,32,1024]{3,2,1,0:T(8,128)(2,1)} %projection.2), calls=%async_computation.2 | async-start | bytes 2097152 | tf_op jit(solution)/shard_map/sum_x/all_to_all | solution.py:254
  111.3 9.3 %collective-permute-start.12 = (bf16[4,32,512]{2,1,0:T(8,128)(2,1)S(1)}, bf16[4,32,512]{2,1,0:T(8,128)(2,1)S(1)}, u32[]{:S(2)}, u32[]{:S(2)}) collective-permute-start(bf16[4,32,512]{2,1,0:T(8,128)(2,1)S(1)} %attention.3), channel_id=1, source_target_pairs={{0,192},{64,128},{128,64},{192,0},{1,193},{65,129},{129,65},{193,1... | collective-permute-start | bytes 393224 | tf_op jit(solution)/shard_map/rows_gather/ppermute | solution.py:176
  113.2 12.8 %collective-permute-start.13 = (bf16[4,32,512]{2,1,0:T(8,128)(2,1)S(1)}, bf16[4,32,512]{2,1,0:T(8,128)(2,1)S(1)}, u32[]{:S(2)}, u32[]{:S(2)}) collective-permute-start(bf16[4,32,512]{2,1,0:T(8,128)(2,1)S(1)} %attention.3), channel_id=1, source_target_pairs={{0,128},{64,192},{128,0},{192,64},{1,129},{65,193},{129,1},{193,65... | collective-permute-start | bytes 393224 | tf_op jit(solution)/shard_map/rows_gather/ppermute | solution.py:176
  115.4 10.6 %collective-permute-start.14 = (bf16[4,32,512]{2,1,0:T(8,128)(2,1)S(1)}, bf16[4,32,512]{2,1,0:T(8,128)(2,1)S(1)}, u32[]{:S(2)}, u32[]{:S(2)}) collective-permute-start(bf16[4,32,512]{2,1,0:T(8,128)(2,1)S(1)} %attention.3), channel_id=1, source_target_pairs={{0,64},{64,0},{128,192},{192,128},{1,65},{65,1},{129,193},{193,129... | collective-permute-start | bytes 393224 | tf_op jit(solution)/shard_map/rows_gather/ppermute | solution.py:176
  127.2 0.8 copy-start
  128.0 37.9 %all-to-all-start.3 = ((bf16[2,4,32,1024]{3,2,1,0:T(8,128)(2,1)}), bf16[2,4,32,1024]{3,2,1,0:T(8,128)(2,1)}, u32[]{:S(2)}, u32[]{:S(2)}) async-start(bf16[2,4,32,1024]{3,2,1,0:T(8,128)(2,1)} %copy-done), calls=%async_computation.3 | async-start | bytes 1048576 | tf_op jit(solution)/shard_map/sum_zh/all_to_all | solution.py:258
  137.0 5.6 %collective-permute-start.15 = (bf16[4,4,32,512]{3,2,1,0:T(8,128)(2,1)}, bf16[4,4,32,512]{3,2,1,0:T(8,128)(2,1)S(1)}, u32[]{:S(2)}, u32[]{:S(2)}) collective-permute-start(bf16[4,4,32,512]{3,2,1,0:T(8,128)(2,1)} %pad_maximum_fusion.2.a_ref), channel_id=1, source_target_pairs={{0,1},{1,0},{2,3},{3,2},{4,5},{5,4},{6,7},{7,6},{8,9},{9,8},{10,11... | collective-permute-start | bytes 1572872 | tf_op jit(solution)/shard_map/sum_x/ppermute | solution.py:172
  142.6 0.8 copy-start.3
  143.4 1.0 copy-start.1
  144.5 1.0 copy-start.4
  147.1 11.1 %collective-permute-start.16 = (bf16[4,32,1024]{2,1,0:T(8,128)(2,1)S(1)}, bf16[4,32,1024]{2,1,0:T(8,128)(2,1)S(1)}, u32[]{:S(2)}, u32[]{:S(2)}) collective-permute-start(bf16[4,32,1024]{2,1,0:T(8,128)(2,1)S(1)} %get-tuple-element.33), channel_id=1, source_target_pairs={{6,0},{0,2},{2,4},{4,6},{7,1},{1,3},{3,5},{5,7},{14,8},{8,10},{10,... | collective-permute-start | bytes 786440 | tf_op jit(solution)/shard_map/sum_x/ppermute | solution.py:180
  150.6 14.0 %collective-permute-start.17 = (bf16[4,32,1024]{2,1,0:T(8,128)(2,1)S(1)}, bf16[4,32,1024]{2,1,0:T(8,128)(2,1)S(1)}, u32[]{:S(2)}, u32[]{:S(2)}) collective-permute-start(bf16[4,32,1024]{2,1,0:T(8,128)(2,1)S(1)} %get-tuple-element.35), channel_id=1, source_target_pairs={{4,0},{6,2},{0,4},{2,6},{5,1},{7,3},{1,5},{3,7},{12,8},{14,10},{8,... | collective-permute-start | bytes 786440 | tf_op jit(solution)/shard_map/sum_x/ppermute | solution.py:180
  155.0 10.9 %collective-permute-start.18 = (bf16[4,32,1024]{2,1,0:T(8,128)(2,1)S(1)}, bf16[4,32,1024]{2,1,0:T(8,128)(2,1)S(1)}, u32[]{:S(2)}, u32[]{:S(2)}) collective-permute-start(bf16[4,32,1024]{2,1,0:T(8,128)(2,1)S(1)} %get-tuple-element.34), channel_id=1, source_target_pairs={{2,0},{4,2},{6,4},{0,6},{3,1},{5,3},{7,5},{1,7},{10,8},{12,10},{14... | collective-permute-start | bytes 786440 | tf_op jit(solution)/shard_map/sum_x/ppermute | solution.py:180

commit v9 on v8

--- a/solution.py
+++ b/solution.py
@@ -76,8 +76,8 @@
                 v = v_sc[pl.ds(at, width), :]
                 s = lax.dot_general(q, k, (((1,), (1,)), ((), ())), preferred_element_type=jnp.float32)
                 if masked:
-                    row = lax.broadcasted_iota(jnp.int32, s.shape, 0) % PAGE + page * PAGE
-                    seen = lax.broadcasted_iota(jnp.int32, s.shape, 1) + at <= row
+                    row = lax.broadcasted_iota(jnp.int32, (size, 1), 0) % PAGE + (page * PAGE - at)
+                    seen = lax.broadcasted_iota(jnp.int32, s.shape, 1) <= row
                     s = jnp.where(seen, s, jnp.float32(-1e30))
                 new = jnp.maximum(best, jnp.max(s, axis=1, keepdims=True))
                 p = jnp.exp2((s - new) * SCALE)

time: 184 us -> 184 us (level)
  transfers between devices with their start and end apart: 23 -> 23, of which waited for: 10 -> 8; matrix products, arithmetic and copies ran while one was open for 2% -> 2% of each run, Pallas kernels for 8% -> 9%
where the time goes in v9:
time: 184 us; the launch traced here: 183 us
  starting transfers between devices  93.7 us (51%)
  waiting for transfers between devices  43.7 us (24%)
  Pallas kernels  18.2 us (10%)
  blocking collectives  14.8 us (8%)
  local copies, waits for them, and re-layouts  8.44 us (5%)
  other arithmetic  3.66 us (2%)
    ppermute x6, waiting for transfers between devices, swap(): return lax.ppermute(piece, axis, [(0, 1), (1, 0)])  30.6 us
    ppermute x4, starting transfers between devices, along(): return lax.ppermute(piece, LINE, perm)  23.1 us
    ppermute x6, starting transfers between devices, swap(): return lax.ppermute(piece, axis, [(0, 1), (1, 0)])  21.3 us
    ppermute x6, starting transfers between devices, quad(): lax.ppermute(piece, ('zb', 'zq'), [(i, i ^ step) for i in range(QUAD)])  18.5 us
    all_to_all x1, blocking collectives, body(): lax.all_to_all(mixed.reshape(QUAD * C, 16, ZL * HD), ('zb', 'zq', 'c'), 0...  14.8 us
    pallas_call x2, Pallas kernels, attend(): pl.pallas_call(attention_kernel, out_shape=jax.ShapeDtypeStruct((X, 32, H...  14.1 us
    ppermute x3, starting transfers between devices, around(): lax.ppermute(piece, axis, [((i + shift) % count, i) for i in range(count)])  10.8 us
    all_to_all x2, starting transfers between devices, spread(): lax.all_to_all(jnp.broadcast_to(piece[None], (count, *piece.shape)), axis...  8.76 us
  transfers between devices with their start and end apart: 23, of which 8 were waited for; matrix products, arithmetic and copies ran while one was open for 2% of the time, Pallas kernels for 9%

profile of v9, /device:TPU:1, one launch (start us, length us, event | category | flops | bytes accessed | tf_op | source)
XLA Modules:
  0.0 182.9 jit_solution(8754055483000053040)
XLA Ops:
  1.3 12.4 %collective-permute-start = (bf16[256,128]{1,0:T(8,128)(2,1)S(1)}, bf16[256,128]{1,0:T(8,128)(2,1)S(1)}, u32[]{:S(2)}, u32[]{:S(2)}) collective-permute-start(bf16[256,128]{1,0:T(8,128)(2,1)S(1)} %get-tuple-element.38), channel_id=1, source_target_pairs={{0,392},{1,393},{64,456},{65,457},{128,0},{129,1},{192,64},{193,65... | collective-permute-start | bytes 196616 | tf_op jit(solution)/shard_map/cache_gather/ppermute | solution.py:188
  13.7 1.9 %collective-permute-start.1 = (bf16[256,128]{1,0:T(8,128)(2,1)S(1)}, bf16[256,128]{1,0:T(8,128)(2,1)S(1)}, u32[]{:S(2)}, u32[]{:S(2)}) collective-permute-start(bf16[256,128]{1,0:T(8,128)(2,1)S(1)} %get-tuple-element.37), channel_id=1, source_target_pairs={{0,128},{1,129},{64,192},{65,193},{128,256},{129,257},{192,320},{1... | collective-permute-start | bytes 196616 | tf_op jit(solution)/shard_map/cache_gather/ppermute | solution.py:188
  15.6 2.1 %collective-permute-start.2 = (bf16[256,128]{1,0:T(8,128)(2,1)S(1)}, bf16[256,128]{1,0:T(8,128)(2,1)S(1)}, u32[]{:S(2)}, u32[]{:S(2)}) collective-permute-start(bf16[256,128]{1,0:T(8,128)(2,1)S(1)} %get-tuple-element.40), channel_id=1, source_target_pairs={{0,264},{1,257},{64,328},{65,321},{128,392},{129,385},{192,456},{1... | collective-permute-start | bytes 196616 | tf_op jit(solution)/shard_map/cache_gather/ppermute | solution.py:188
  17.8 6.6 %collective-permute-start.4 = (bf16[256,128]{1,0:T(8,128)(2,1)S(1)}, bf16[256,128]{1,0:T(8,128)(2,1)S(1)}, u32[]{:S(2)}, u32[]{:S(2)}) collective-permute-start(bf16[256,128]{1,0:T(8,128)(2,1)S(1)} %get-tuple-element.36), channel_id=1, source_target_pairs={{0,328},{1,329},{64,256},{65,257},{128,456},{129,457},{192,384},{1... | collective-permute-start | bytes 196616 | tf_op jit(solution)/shard_map/cache_gather/ppermute | solution.py:188
  24.4 3.8 %collective-permute-start.3 = (bf16[768,128]{1,0:T(8,128)(2,1)S(1)}, bf16[768,128]{1,0:T(8,128)(2,1)S(1)}, u32[]{:S(2)}, u32[]{:S(2)}) collective-permute-start(bf16[768,128]{1,0:T(8,128)(2,1)S(1)} %pad_maximum_fusion.4), channel_id=1, source_target_pairs={{0,64},{64,0},{1,65},{65,1},{2,66},{66,2},{3,67},{67,3},{4,68},{68... | collective-permute-start | bytes 589832 | tf_op jit(solution)/shard_map/cache_gather/ppermute | solution.py:172
  28.3 3.0 %collective-permute-start.5 = (bf16[512,128]{1,0:T(8,128)(2,1)S(1)}, bf16[512,128]{1,0:T(8,128)(2,1)S(1)}, u32[]{:S(2)}, u32[]{:S(2)}) collective-permute-start(bf16[512,128]{1,0:T(8,128)(2,1)S(1)} %get-tuple-element.44), channel_id=1, source_target_pairs={{0,1},{1,0},{2,3},{3,2},{4,5},{5,4},{6,7},{7,6},{8,9},{9,8},{10,11... | collective-permute-start | bytes 393224 | tf_op jit(solution)/shard_map/weight_gather/ppermute | solution.py:172
  34.7 4.4 %all-to-all-start = ((bf16[4,2048,128]{2,1,0:T(8,128)(2,1)}), bf16[4,2048,128]{2,1,0:T(8,128)(2,1)}, u32[]{:S(2)}, u32[]{:S(2)}) async-start(bf16[4,2048,128]{2,1,0:T(8,128)(2,1)} %broadcast_in_dim.4), calls=%async_computation | async-start | bytes 4194304 | tf_op jit(solution)/shard_map/cache_gather/all_to_all | solution.py:168
  39.2 3.7 %collective-permute-start.6 = (bf16[1024,128]{1,0:T(8,128)(2,1)S(1)}, bf16[1024,128]{1,0:T(8,128)(2,1)S(1)}, u32[]{:S(2)}, u32[]{:S(2)}) collective-permute-start(bf16[1024,128]{1,0:T(8,128)(2,1)S(1)} %pad_maximum_fusion.3), channel_id=1, source_target_pairs={{0,256},{256,0},{1,257},{257,1},{2,258},{258,2},{3,259},{259,3},{4... | collective-permute-start | bytes 786440 | tf_op jit(solution)/shard_map/weight_gather/ppermute | solution.py:172
  42.9 25.9 %collective-permute-done.6 = bf16[1024,128]{1,0:T(8,128)(2,1)S(1)} collective-permute-done((bf16[1024,128]{1,0:T(8,128)(2,1)S(1)}, bf16[1024,128]{1,0:T(8,128)(2,1)S(1)}, u32[]{:S(2)}, u32[]{:S(2)}) %collective-permute-start.6) | collective-permute-done | bytes 262176 | tf_op jit(solution)/shard_map/weight_gather/ppermute | solution.py:172
  68.8 3.7 %collective-permute-start.7 = (bf16[8192,128]{1,0:T(8,128)(2,1)}, bf16[8192,128]{1,0:T(8,128)(2,1)}, u32[]{:S(2)}, u32[]{:S(2)}) collective-permute-start(bf16[8192,128]{1,0:T(8,128)(2,1)} %bitcast.4.own_ref), channel_id=1, source_target_pairs={{0,1},{1,0},{2,3},{3,2},{4,5},{5,4},{6,7},{7,6},{8,9},{9,8},{10,11... | collective-permute-start | bytes 6291464 | tf_op jit(solution)/shard_map/cache_gather/ppermute | solution.py:172
  72.6 1.6 broadcast_in_dim.5
  74.2 4.3 %all-to-all-start.1 = ((bf16[4,2,1024,128]{3,2,1,0:T(8,128)(2,1)}), bf16[4,2,1024,128]{3,2,1,0:T(8,128)(2,1)S(1)}, u32[]{:S(2)}, u32[]{:S(2)}) async-start(bf16[4,2,1024,128]{3,2,1,0:T(8,128)(2,1)} %broadcast_in_dim.5), calls=%async_computation.1 | async-start | bytes 4194304 | tf_op jit(solution)/shard_map/weight_gather/all_to_all | solution.py:168
  78.6 7.4 %attention.2 = bf16[4,32,512]{2,1,0:T(8,128)(2,1)S(1)} custom-call(s32[32]{0:T(128)S(1)} %copy-done.5, s32[64]{0:T(128)S(1)} %copy-done.6, s32[3]{0:T(128)S(1)} %pad_add_fusion.place, bf16[256,512]{1,0:T(8,128)(2,1)S(1)} %copy-done.2, bf16[8192,128]{1,0:T(8,128)(2,1)} %bitcast.4.own_ref, bf16[8192,128]{1,0:T(8,128)(2,1)} %collective-permute-done.7.other_ref), custom_call_target="tpu_custom_call" | custom-call | tf_op jit(solution)/shard_map/attention/pallas_call | solution.py:116
  86.1 1.9 %collective-permute-start.8 = (bf16[4,32,512]{2,1,0:T(8,128)(2,1)S(1)}, bf16[4,32,512]{2,1,0:T(8,128)(2,1)S(1)}, u32[]{:S(2)}, u32[]{:S(2)}) collective-permute-start(bf16[4,32,512]{2,1,0:T(8,128)(2,1)S(1)} %attention.2), channel_id=1, source_target_pairs={{0,192},{64,128},{128,64},{192,0},{1,193},{65,129},{129,65},{193,1... | collective-permute-start | bytes 393224 | tf_op jit(solution)/shard_map/rows_gather/ppermute | solution.py:176
  88.0 1.9 %collective-permute-start.9 = (bf16[4,32,512]{2,1,0:T(8,128)(2,1)S(1)}, bf16[4,32,512]{2,1,0:T(8,128)(2,1)S(1)}, u32[]{:S(2)}, u32[]{:S(2)}) collective-permute-start(bf16[4,32,512]{2,1,0:T(8,128)(2,1)S(1)} %attention.2), channel_id=1, source_target_pairs={{0,128},{64,192},{128,0},{192,64},{1,129},{65,193},{129,1},{193,65... | collective-permute-start | bytes 393224 | tf_op jit(solution)/shard_map/rows_gather/ppermute | solution.py:176
  89.9 5.4 %collective-permute-start.10 = (bf16[4,32,512]{2,1,0:T(8,128)(2,1)S(1)}, bf16[4,32,512]{2,1,0:T(8,128)(2,1)S(1)}, u32[]{:S(2)}, u32[]{:S(2)}) collective-permute-start(bf16[4,32,512]{2,1,0:T(8,128)(2,1)S(1)} %attention.2), channel_id=1, source_target_pairs={{0,64},{64,0},{128,192},{192,128},{1,65},{65,1},{129,193},{193,129... | collective-permute-start | bytes 393224 | tf_op jit(solution)/shard_map/rows_gather/ppermute | solution.py:176
  95.4 6.7 %attention.3 = bf16[4,32,512]{2,1,0:T(8,128)(2,1)S(1)} custom-call(s32[32]{0:T(128)S(1)} %copy-done.5, s32[64]{0:T(128)S(1)} %copy-done.6, s32[3]{0:T(128)S(1)} %pad_add_fusion.2.place, bf16[256,512]{1,0:T(8,128)(2,1)S(1)} %copy-done.2, bf16[8192,128]{1,0:T(8,128)(2,1)} %bitcast.4.own_ref, bf16[8192,128]{1,0:T(8,128)(2,1)} %collective-permute-done.7.other_ref), custom_call_target="tpu_custom_call" | custom-call | tf_op jit(solution)/shard_map/attention/pallas_call | solution.py:116
  102.2 3.3 %collective-permute-start.11 = (bf16[4,4,32,512]{3,2,1,0:T(8,128)(2,1)S(1)}, bf16[4,4,32,512]{3,2,1,0:T(8,128)(2,1)S(1)}, u32[]{:S(2)}, u32[]{:S(2)}) collective-permute-start(bf16[4,4,32,512]{3,2,1,0:T(8,128)(2,1)S(1)} %pad_maximum_fusion.a_ref), channel_id=1, source_target_pairs={{0,1},{1,0},{2,3},{3,2},{4,5},{5,4},{6,7},{7,6},{8,9},{9,8},{10,11... | collective-permute-start | bytes 1572872 | tf_op jit(solution)/shard_map/rows_gather/ppermute | solution.py:172
  106.8 2.3 %projection.2 = bf16[4,4,32,1024]{3,2,1,0:T(8,128)(2,1)} custom-call(s32[1]{0:T(128)} %bitcast.me, bf16[4,4,32,512]{3,2,1,0:T(8,128)(2,1)S(1)} %pad_maximum_fusion.a_ref, bf16[4,4,32,512]{3,2,1,0:T(8,128)(2,1)S(1)} %collective-permute-done.11.b_ref, bf16[4,2,1024,128]{3,2,1,0:T(8,128)(2,1)S(1)} %all-to-all-done.1.w_ref), custom_call_target="tpu_custom_call" | custom-call | tf_op jit(solution)/shard_map/projection/pallas_call | solution.py:138
  109.0 4.0 %all-to-all-start.2 = ((bf16[4,4,32,1024]{3,2,1,0:T(8,128)(2,1)}), bf16[4,4,32,1024]{3,2,1,0:T(8,128)(2,1)S(1)}, u32[]{:S(2)}, u32[]{:S(2)}) async-start(bf16[4,4,32,1024]{3,2,1,0:T(8,128)(2,1)} %projection.2), calls=%async_computation.2 | async-start | bytes 2097152 | tf_op jit(solution)/shard_map/sum_x/all_to_all | solution.py:254
  113.0 2.3 %collective-permute-start.12 = (bf16[4,32,512]{2,1,0:T(8,128)(2,1)S(1)}, bf16[4,32,512]{2,1,0:T(8,128)(2,1)S(1)}, u32[]{:S(2)}, u32[]{:S(2)}) collective-permute-start(bf16[4,32,512]{2,1,0:T(8,128)(2,1)S(1)} %attention.3), channel_id=1, source_target_pairs={{0,192},{64,128},{128,64},{192,0},{1,193},{65,129},{129,65},{193,1... | collective-permute-start | bytes 393224 | tf_op jit(solution)/shard_map/rows_gather/ppermute | solution.py:176
  115.3 1.9 %collective-permute-start.13 = (bf16[4,32,512]{2,1,0:T(8,128)(2,1)S(1)}, bf16[4,32,512]{2,1,0:T(8,128)(2,1)S(1)}, u32[]{:S(2)}, u32[]{:S(2)}) collective-permute-start(bf16[4,32,512]{2,1,0:T(8,128)(2,1)S(1)} %attention.3), channel_id=1, source_target_pairs={{0,128},{64,192},{128,0},{192,64},{1,129},{65,193},{129,1},{193,65... | collective-permute-start | bytes 393224 | tf_op jit(solution)/shard_map/rows_gather/ppermute | solution.py:176
  117.3 5.0 %collective-permute-start.14 = (bf16[4,32,512]{2,1,0:T(8,128)(2,1)S(1)}, bf16[4,32,512]{2,1,0:T(8,128)(2,1)S(1)}, u32[]{:S(2)}, u32[]{:S(2)}) collective-permute-start(bf16[4,32,512]{2,1,0:T(8,128)(2,1)S(1)} %attention.3), channel_id=1, source_target_pairs={{0,64},{64,0},{128,192},{192,128},{1,65},{65,1},{129,193},{193,129... | collective-permute-start | bytes 393224 | tf_op jit(solution)/shard_map/rows_gather/ppermute | solution.py:176
  122.3 5.5 %collective-permute-done.13 = bf16[4,32,512]{2,1,0:T(8,128)(2,1)S(1)} collective-permute-done((bf16[4,32,512]{2,1,0:T(8,128)(2,1)S(1)}, bf16[4,32,512]{2,1,0:T(8,128)(2,1)S(1)}, u32[]{:S(2)}, u32[]{:S(2)}) %collective-permute-start.13) | collective-permute-done | bytes 131104 | tf_op jit(solution)/shard_map/rows_gather/ppermute | solution.py:176
  129.8 7.3 %all-to-all-start.3 = ((bf16[2,4,32,1024]{3,2,1,0:T(8,128)(2,1)}), bf16[2,4,32,1024]{3,2,1,0:T(8,128)(2,1)}, u32[]{:S(2)}, u32[]{:S(2)}) async-start(bf16[2,4,32,1024]{3,2,1,0:T(8,128)(2,1)} %copy-done), calls=%async_computation.3 | async-start | bytes 1048576 | tf_op jit(solution)/shard_map/sum_zh/all_to_all | solution.py:258
  137.1 3.8 %collective-permute-start.15 = (bf16[4,4,32,512]{3,2,1,0:T(8,128)(2,1)}, bf16[4,4,32,512]{3,2,1,0:T(8,128)(2,1)S(1)}, u32[]{:S(2)}, u32[]{:S(2)}) collective-permute-start(bf16[4,4,32,512]{3,2,1,0:T(8,128)(2,1)} %pad_maximum_fusion.2.a_ref), channel_id=1, source_target_pairs={{0,1},{1,0},{2,3},{3,2},{4,5},{5,4},{6,7},{7,6},{8,9},{9,8},{10,11... | collective-permute-start | bytes 1572872 | tf_op jit(solution)/shard_map/sum_x/ppermute | solution.py:172
  141.0 1.7 collective-permute-done.15.b_ref
  147.2 3.4 %collective-permute-start.16 = (bf16[4,32,1024]{2,1,0:T(8,128)(2,1)S(1)}, bf16[4,32,1024]{2,1,0:T(8,128)(2,1)S(1)}, u32[]{:S(2)}, u32[]{:S(2)}) collective-permute-start(bf16[4,32,1024]{2,1,0:T(8,128)(2,1)S(1)} %get-tuple-element.33), channel_id=1, source_target_pairs={{6,0},{0,2},{2,4},{4,6},{7,1},{1,3},{3,5},{5,7},{14,8},{8,10},{10,... | collective-permute-start | bytes 786440 | tf_op jit(solution)/shard_map/sum_x/ppermute | solution.py:180
  150.5 4.3 %collective-permute-start.17 = (bf16[4,32,1024]{2,1,0:T(8,128)(2,1)S(1)}, bf16[4,32,1024]{2,1,0:T(8,128)(2,1)S(1)}, u32[]{:S(2)}, u32[]{:S(2)}) collective-permute-start(bf16[4,32,1024]{2,1,0:T(8,128)(2,1)S(1)} %get-tuple-element.35), channel_id=1, source_target_pairs={{4,0},{6,2},{0,4},{2,6},{5,1},{7,3},{1,5},{3,7},{12,8},{14,10},{8,... | collective-permute-start | bytes 786440 | tf_op jit(solution)/shard_map/sum_x/ppermute | solution.py:180
  154.8 3.1 %collective-permute-start.18 = (bf16[4,32,1024]{2,1,0:T(8,128)(2,1)S(1)}, bf16[4,32,1024]{2,1,0:T(8,128)(2,1)S(1)}, u32[]{:S(2)}, u32[]{:S(2)}) collective-permute-start(bf16[4,32,1024]{2,1,0:T(8,128)(2,1)S(1)} %get-tuple-element.34), channel_id=1, source_target_pairs={{2,0},{4,2},{6,4},{0,6},{3,1},{5,3},{7,5},{1,7},{10,8},{12,10},{14... | collective-permute-start | bytes 786440 | tf_op jit(solution)/shard_map/sum_x/ppermute | solution.py:180
  158.0 6.6 %collective-permute-done.17 = bf16[4,32,1024]{2,1,0:T(8,128)(2,1)S(1)} collective-permute-done((bf16[4,32,1024]{2,1,0:T(8,128)(2,1)S(1)}, bf16[4,32,1024]{2,1,0:T(8,128)(2,1)S(1)}, u32[]{:S(2)}, u32[]{:S(2)}) %collective-permute-start.17) | collective-permute-done | bytes 262176 | tf_op jit(solution)/shard_map/sum_x/ppermute | solution.py:180
  166.8 14.8 %all_to_all.25 = bf16[8,16,1024]{2,1,0:T(8,128)(2,1)S(1)} all-to-all(bf16[8,16,1024]{2,1,0:T(8,128)(2,1)S(1)} %bitcast.37), channel_id=1, replica_groups=mesh['za'=2,'zb'=2,'zq'=2,'y'=4,'zh'=2,'x'=4,'c'=2] {'zb','zq','c'}, dimensions={0} | all-to-all | bytes 524288 | tf_op jit(solution)/shard_map/columns/all_to_all | solution.py:267
  (59 shorter events, 16.4 us)
Async XLA Ops:
  0.0 28.2 %copy-start.7 = (bf16[512,256]{1,0:T(8,128)(2,1)S(1)}, bf16[512,256]{1,0:T(8,128)(2,1)}, u32[]{:S(2)}) copy-start(bf16[512,256]{1,0:T(8,128)(2,1)} %param.11) | copy-start | bytes 786436
  1.3 23.1 %collective-permute-start = (bf16[256,128]{1,0:T(8,128)(2,1)S(1)}, bf16[256,128]{1,0:T(8,128)(2,1)S(1)}, u32[]{:S(2)}, u32[]{:S(2)}) collective-permute-start(bf16[256,128]{1,0:T(8,128)(2,1)S(1)} %get-tuple-element.38), channel_id=1, source_target_pairs={{0,392},{1,393},{64,456},{65,457},{128,0},{129,1},{192,64},{193,65... | collective-permute-start | bytes 196616 | tf_op jit(solution)/shard_map/cache_gather/ppermute | solution.py:188
  13.7 10.7 %collective-permute-start.1 = (bf16[256,128]{1,0:T(8,128)(2,1)S(1)}, bf16[256,128]{1,0:T(8,128)(2,1)S(1)}, u32[]{:S(2)}, u32[]{:S(2)}) collective-permute-start(bf16[256,128]{1,0:T(8,128)(2,1)S(1)} %get-tuple-element.37), channel_id=1, source_target_pairs={{0,128},{1,129},{64,192},{65,193},{128,256},{129,257},{192,320},{1... | collective-permute-start | bytes 196616 | tf_op jit(solution)/shard_map/cache_gather/ppermute | solution.py:188
  15.6 15.7 %collective-permute-start.2 = (bf16[256,128]{1,0:T(8,128)(2,1)S(1)}, bf16[256,128]{1,0:T(8,128)(2,1)S(1)}, u32[]{:S(2)}, u32[]{:S(2)}) collective-permute-start(bf16[256,128]{1,0:T(8,128)(2,1)S(1)} %get-tuple-element.40), channel_id=1, source_target_pairs={{0,264},{1,257},{64,328},{65,321},{128,392},{129,385},{192,456},{1... | collective-permute-start | bytes 196616 | tf_op jit(solution)/shard_map/cache_gather/ppermute | solution.py:188
  17.8 15.3 %collective-permute-start.4 = (bf16[256,128]{1,0:T(8,128)(2,1)S(1)}, bf16[256,128]{1,0:T(8,128)(2,1)S(1)}, u32[]{:S(2)}, u32[]{:S(2)}) collective-permute-start(bf16[256,128]{1,0:T(8,128)(2,1)S(1)} %get-tuple-element.36), channel_id=1, source_target_pairs={{0,328},{1,329},{64,256},{65,257},{128,456},{129,457},{192,384},{1... | collective-permute-start | bytes 196616 | tf_op jit(solution)/shard_map/cache_gather/ppermute | solution.py:188
  24.4 8.6 %collective-permute-start.3 = (bf16[768,128]{1,0:T(8,128)(2,1)S(1)}, bf16[768,128]{1,0:T(8,128)(2,1)S(1)}, u32[]{:S(2)}, u32[]{:S(2)}) collective-permute-start(bf16[768,128]{1,0:T(8,128)(2,1)S(1)} %pad_maximum_fusion.4), channel_id=1, source_target_pairs={{0,64},{64,0},{1,65},{65,1},{2,66},{66,2},{3,67},{67,3},{4,68},{68... | collective-permute-start | bytes 589832 | tf_op jit(solution)/shard_map/cache_gather/ppermute | solution.py:172
  28.3 4.0 %collective-permute-start.5 = (bf16[512,128]{1,0:T(8,128)(2,1)S(1)}, bf16[512,128]{1,0:T(8,128)(2,1)S(1)}, u32[]{:S(2)}, u32[]{:S(2)}) collective-permute-start(bf16[512,128]{1,0:T(8,128)(2,1)S(1)} %get-tuple-element.44), channel_id=1, source_target_pairs={{0,1},{1,0},{2,3},{3,2},{4,5},{5,4},{6,7},{7,6},{8,9},{9,8},{10,11... | collective-permute-start | bytes 393224 | tf_op jit(solution)/shard_map/weight_gather/ppermute | solution.py:172
  34.7 34.1 %all-to-all-start = ((bf16[4,2048,128]{2,1,0:T(8,128)(2,1)}), bf16[4,2048,128]{2,1,0:T(8,128)(2,1)}, u32[]{:S(2)}, u32[]{:S(2)}) async-start(bf16[4,2048,128]{2,1,0:T(8,128)(2,1)} %broadcast_in_dim.4), calls=%async_computation | async-start | bytes 4194304 | tf_op jit(solution)/shard_map/cache_gather/all_to_all | solution.py:168
  39.2 29.6 %collective-permute-start.6 = (bf16[1024,128]{1,0:T(8,128)(2,1)S(1)}, bf16[1024,128]{1,0:T(8,128)(2,1)S(1)}, u32[]{:S(2)}, u32[]{:S(2)}) collective-permute-start(bf16[1024,128]{1,0:T(8,128)(2,1)S(1)} %pad_maximum_fusion.3), channel_id=1, source_target_pairs={{0,256},{256,0},{1,257},{257,1},{2,258},{258,2},{3,259},{259,3},{4... | collective-permute-start | bytes 786440 | tf_op jit(solution)/shard_map/weight_gather/ppermute | solution.py:172
  68.8 9.8 %collective-permute-start.7 = (bf16[8192,128]{1,0:T(8,128)(2,1)}, bf16[8192,128]{1,0:T(8,128)(2,1)}, u32[]{:S(2)}, u32[]{:S(2)}) collective-permute-start(bf16[8192,128]{1,0:T(8,128)(2,1)} %bitcast.4.own_ref), channel_id=1, source_target_pairs={{0,1},{1,0},{2,3},{3,2},{4,5},{5,4},{6,7},{7,6},{8,9},{9,8},{10,11... | collective-permute-start | bytes 6291464 | tf_op jit(solution)/shard_map/cache_gather/ppermute | solution.py:172
  74.2 4.4 %copy-start.2 = (bf16[256,512]{1,0:T(8,128)(2,1)S(1)}, bf16[256,512]{1,0:T(8,128)(2,1)}, u32[]{:S(2)}) copy-start(bf16[256,512]{1,0:T(8,128)(2,1)} %q_ref.3) | copy-start | bytes 786436
  74.2 4.4 %copy-start.5 = (s32[32]{0:T(128)S(1)}, s32[32]{0:T(128)}, u32[]{:S(2)}) copy-start(s32[32]{0:T(128)} %counts.3) | copy-start | bytes 388
  74.2 4.4 %copy-start.6 = (s32[64]{0:T(128)S(1)}, s32[64]{0:T(128)}, u32[]{:S(2)}) copy-start(s32[64]{0:T(128)} %order.3) | copy-start | bytes 772
  74.2 31.3 %all-to-all-start.1 = ((bf16[4,2,1024,128]{3,2,1,0:T(8,128)(2,1)}), bf16[4,2,1024,128]{3,2,1,0:T(8,128)(2,1)S(1)}, u32[]{:S(2)}, u32[]{:S(2)}) async-start(bf16[4,2,1024,128]{3,2,1,0:T(8,128)(2,1)} %broadcast_in_dim.5), calls=%async_computation.1 | async-start | bytes 4194304 | tf_op jit(solution)/shard_map/weight_gather/all_to_all | solution.py:168
  86.1 16.1 %collective-permute-start.8 = (bf16[4,32,512]{2,1,0:T(8,128)(2,1)S(1)}, bf16[4,32,512]{2,1,0:T(8,128)(2,1)S(1)}, u32[]{:S(2)}, u32[]{:S(2)}) collective-permute-start(bf16[4,32,512]{2,1,0:T(8,128)(2,1)S(1)} %attention.2), channel_id=1, source_target_pairs={{0,192},{64,128},{128,64},{192,0},{1,193},{65,129},{129,65},{193,1... | collective-permute-start | bytes 393224 | tf_op jit(solution)/shard_map/rows_gather/ppermute | solution.py:176
  88.0 14.1 %collective-permute-start.9 = (bf16[4,32,512]{2,1,0:T(8,128)(2,1)S(1)}, bf16[4,32,512]{2,1,0:T(8,128)(2,1)S(1)}, u32[]{:S(2)}, u32[]{:S(2)}) collective-permute-start(bf16[4,32,512]{2,1,0:T(8,128)(2,1)S(1)} %attention.2), channel_id=1, source_target_pairs={{0,128},{64,192},{128,0},{192,64},{1,129},{65,193},{129,1},{193,65... | collective-permute-start | bytes 393224 | tf_op jit(solution)/shard_map/rows_gather/ppermute | solution.py:176
  89.9 12.2 %collective-permute-start.10 = (bf16[4,32,512]{2,1,0:T(8,128)(2,1)S(1)}, bf16[4,32,512]{2,1,0:T(8,128)(2,1)S(1)}, u32[]{:S(2)}, u32[]{:S(2)}) collective-permute-start(bf16[4,32,512]{2,1,0:T(8,128)(2,1)S(1)} %attention.2), channel_id=1, source_target_pairs={{0,64},{64,0},{128,192},{192,128},{1,65},{65,1},{129,193},{193,129... | collective-permute-start | bytes 393224 | tf_op jit(solution)/shard_map/rows_gather/ppermute | solution.py:176
  102.2 4.6 %collective-permute-start.11 = (bf16[4,4,32,512]{3,2,1,0:T(8,128)(2,1)S(1)}, bf16[4,4,32,512]{3,2,1,0:T(8,128)(2,1)S(1)}, u32[]{:S(2)}, u32[]{:S(2)}) collective-permute-start(bf16[4,4,32,512]{3,2,1,0:T(8,128)(2,1)S(1)} %pad_maximum_fusion.a_ref), channel_id=1, source_target_pairs={{0,1},{1,0},{2,3},{3,2},{4,5},{5,4},{6,7},{7,6},{8,9},{9,8},{10,11... | collective-permute-start | bytes 1572872 | tf_op jit(solution)/shard_map/rows_gather/ppermute | solution.py:172
  109.0 19.6 %all-to-all-start.2 = ((bf16[4,4,32,1024]{3,2,1,0:T(8,128)(2,1)}), bf16[4,4,32,1024]{3,2,1,0:T(8,128)(2,1)S(1)}, u32[]{:S(2)}, u32[]{:S(2)}) async-start(bf16[4,4,32,1024]{3,2,1,0:T(8,128)(2,1)} %projection.2), calls=%async_computation.2 | async-start | bytes 2097152 | tf_op jit(solution)/shard_map/sum_x/all_to_all | solution.py:254
  113.0 9.3 %collective-permute-start.12 = (bf16[4,32,512]{2,1,0:T(8,128)(2,1)S(1)}, bf16[4,32,512]{2,1,0:T(8,128)(2,1)S(1)}, u32[]{:S(2)}, u32[]{:S(2)}) collective-permute-start(bf16[4,32,512]{2,1,0:T(8,128)(2,1)S(1)} %attention.3), channel_id=1, source_target_pairs={{0,192},{64,128},{128,64},{192,0},{1,193},{65,129},{129,65},{193,1... | collective-permute-start | bytes 393224 | tf_op jit(solution)/shard_map/rows_gather/ppermute | solution.py:176
  115.3 12.5 %collective-permute-start.13 = (bf16[4,32,512]{2,1,0:T(8,128)(2,1)S(1)}, bf16[4,32,512]{2,1,0:T(8,128)(2,1)S(1)}, u32[]{:S(2)}, u32[]{:S(2)}) collective-permute-start(bf16[4,32,512]{2,1,0:T(8,128)(2,1)S(1)} %attention.3), channel_id=1, source_target_pairs={{0,128},{64,192},{128,0},{192,64},{1,129},{65,193},{129,1},{193,65... | collective-permute-start | bytes 393224 | tf_op jit(solution)/shard_map/rows_gather/ppermute | solution.py:176
  117.3 10.5 %collective-permute-start.14 = (bf16[4,32,512]{2,1,0:T(8,128)(2,1)S(1)}, bf16[4,32,512]{2,1,0:T(8,128)(2,1)S(1)}, u32[]{:S(2)}, u32[]{:S(2)}) collective-permute-start(bf16[4,32,512]{2,1,0:T(8,128)(2,1)S(1)} %attention.3), channel_id=1, source_target_pairs={{0,64},{64,0},{128,192},{192,128},{1,65},{65,1},{129,193},{193,129... | collective-permute-start | bytes 393224 | tf_op jit(solution)/shard_map/rows_gather/ppermute | solution.py:176
  129.0 0.8 copy-start
  129.8 35.8 %all-to-all-start.3 = ((bf16[2,4,32,1024]{3,2,1,0:T(8,128)(2,1)}), bf16[2,4,32,1024]{3,2,1,0:T(8,128)(2,1)}, u32[]{:S(2)}, u32[]{:S(2)}) async-start(bf16[2,4,32,1024]{3,2,1,0:T(8,128)(2,1)} %copy-done), calls=%async_computation.3 | async-start | bytes 1048576 | tf_op jit(solution)/shard_map/sum_zh/all_to_all | solution.py:258
  137.1 5.6 %collective-permute-start.15 = (bf16[4,4,32,512]{3,2,1,0:T(8,128)(2,1)}, bf16[4,4,32,512]{3,2,1,0:T(8,128)(2,1)S(1)}, u32[]{:S(2)}, u32[]{:S(2)}) collective-permute-start(bf16[4,4,32,512]{3,2,1,0:T(8,128)(2,1)} %pad_maximum_fusion.2.a_ref), channel_id=1, source_target_pairs={{0,1},{1,0},{2,3},{3,2},{4,5},{5,4},{6,7},{7,6},{8,9},{9,8},{10,11... | collective-permute-start | bytes 1572872 | tf_op jit(solution)/shard_map/sum_x/ppermute | solution.py:172
  142.7 0.8 copy-start.3
  143.5 1.0 copy-start.1
  144.5 1.0 copy-start.4
  147.2 10.8 %collective-permute-start.16 = (bf16[4,32,1024]{2,1,0:T(8,128)(2,1)S(1)}, bf16[4,32,1024]{2,1,0:T(8,128)(2,1)S(1)}, u32[]{:S(2)}, u32[]{:S(2)}) collective-permute-start(bf16[4,32,1024]{2,1,0:T(8,128)(2,1)S(1)} %get-tuple-element.33), channel_id=1, source_target_pairs={{6,0},{0,2},{2,4},{4,6},{7,1},{1,3},{3,5},{5,7},{14,8},{8,10},{10,... | collective-permute-start | bytes 786440 | tf_op jit(solution)/shard_map/sum_x/ppermute | solution.py:180
  150.5 14.0 %collective-permute-start.17 = (bf16[4,32,1024]{2,1,0:T(8,128)(2,1)S(1)}, bf16[4,32,1024]{2,1,0:T(8,128)(2,1)S(1)}, u32[]{:S(2)}, u32[]{:S(2)}) collective-permute-start(bf16[4,32,1024]{2,1,0:T(8,128)(2,1)S(1)} %get-tuple-element.35), channel_id=1, source_target_pairs={{4,0},{6,2},{0,4},{2,6},{5,1},{7,3},{1,5},{3,7},{12,8},{14,10},{8,... | collective-permute-start | bytes 786440 | tf_op jit(solution)/shard_map/sum_x/ppermute | solution.py:180
  154.8 10.7 %collective-permute-start.18 = (bf16[4,32,1024]{2,1,0:T(8,128)(2,1)S(1)}, bf16[4,32,1024]{2,1,0:T(8,128)(2,1)S(1)}, u32[]{:S(2)}, u32[]{:S(2)}) collective-permute-start(bf16[4,32,1024]{2,1,0:T(8,128)(2,1)S(1)} %get-tuple-element.34), channel_id=1, source_target_pairs={{2,0},{4,2},{6,4},{0,6},{3,1},{5,3},{7,5},{1,7},{10,8},{12,10},{14... | collective-permute-start | bytes 786440 | tf_op jit(solution)/shard_map/sum_x/ppermute | solution.py:180
